TPU v7x, 512 devices: a whole 4x8x8 slice. The times are simulated.
512 devices in a mesh: gz: 128 (over x, z, y_hi, core), tile: 4 (over y_lo).
Axes of the slice: x: 4, y: 8 (y_hi: 2, y_lo: 4; y = y_hi * 4 + y_lo), z: 8, core: 2. Of those that a mesh axis runs over, the one named last changes fastest.
Arguments:
- sections: bfloat16 [128, 32, 256, 256], P('gz', 'tile'), may hold values from -6 to 6
- offsets: int32 [2, 2, 128, 32], P(None, None, 'gz', 'tile'), may hold values from -3 to 3
- node_links: int32 [4, 128, 32], P(None, 'gz', 'tile'), may hold values from 0 to 31, as said below
Outputs:
- shifts_found: float32 [2, 2, 128, 32], P(None, None, 'gz', 'tile')
- positions: float32 [2, 128, 32], P(None, 'gz', 'tile')
Inputs may be any that keep to these rules, and one draw needn't show every extreme that they name: `node_links`: each entry names a node of the same section at most one row and one column away from node i in the grid of 8 rows of 4 nodes (node number = row * 4 + column), never node i itself; entry 0 lies in the same row and entry 1 in the same column.
All inputs are finite; a program needn't handle non-finite values.
Results may differ from a plain program's by a relative error of at most 0.0013.
Values may be sent and summed in bfloat16 or wider, within the bound.
No kernel may reach another device: no remote copies, remote signals or barrier semaphores. Data moves between devices by JAX's collectives and lax.ppermute only.
A program may use at most 64 MiB of HBM per device.

v0:
```python
import math

import jax
import jax.numpy as jnp
from jax import lax
from jax.sharding import PartitionSpec as P

NODE_COLS = 4
STEPS = 2


def shifted(value, axis, by):
    peers = lax.axis_size(axis)
    pairs = [(i, i + by) for i in range(peers) if 0 <= i + by < peers]
    return lax.ppermute(value, axis, pairs)


def extended(value, sides, width):
    for axis, dim in sides:
        peers, length = (lax.axis_size(axis), value.shape[dim])
        up = [(i, (i + 1) % peers) for i in range(peers - 1)]
        down = [(j, i) for i, j in up]
        last = lax.slice_in_dim(value, length - width, length, axis=dim)
        first = lax.slice_in_dim(value, 0, width, axis=dim)
        before = lax.ppermute(last, axis, up)
        after = lax.ppermute(first, axis, down)
        value = jnp.concatenate([before, value, after], axis=dim)
    return value


def dft_tables(length):
    indices = jnp.arange(length, dtype=jnp.int32)
    phases = indices[:, None] * indices[None, :] % length
    angles = phases.astype(jnp.float32) * (2.0 * math.pi / length)
    return (jnp.cos(angles).astype(jnp.bfloat16), jnp.sin(angles).astype(jnp.bfloat16))


def spectrum_one(patch, right_table, left_table):
    length = patch.shape[0]
    half_product = jnp.dot(patch, right_table, preferred_element_type=jnp.float32).astype(
        jnp.bfloat16
    )
    full_product = jnp.dot(left_table, half_product, preferred_element_type=jnp.float32)
    real_part = full_product[:length, :length] - full_product[length:, length:]
    imag_part = -(full_product[:length, length:] + full_product[length:, :length])
    return jnp.concatenate([real_part, imag_part], axis=1).astype(jnp.bfloat16)


def refine(spec_a, spec_b, offset_y, offset_x):
    length = spec_a.shape[0]
    highest = lax.Precision.HIGHEST
    spec_first = spec_a.astype(jnp.float32)
    spec_other = spec_b.astype(jnp.float32)
    a_real, a_imag = (spec_first[:, :length], spec_first[:, length:])
    b_real, b_imag = (spec_other[:, :length], spec_other[:, length:])
    cross_real = a_real * b_real + a_imag * b_imag
    cross_imag = a_imag * b_real - a_real * b_imag
    magnitude = jnp.sqrt(cross_real * cross_real + cross_imag * cross_imag)
    denominator = magnitude + jnp.mean(magnitude) + 1e-06
    power = jnp.concatenate([cross_real / denominator, cross_imag / denominator], axis=1)
    step_offsets = jnp.arange(-1, 2, dtype=jnp.int32)
    indices = jnp.arange(length, dtype=jnp.int32)
    row_phases = (offset_y + step_offsets)[:, None] * indices[None, :] % length
    col_phases = (offset_x + step_offsets)[:, None] * indices[None, :] % length
    row_angles = row_phases.astype(jnp.float32) * (2.0 * math.pi / length)
    col_angles = col_phases.astype(jnp.float32) * (2.0 * math.pi / length)
    left_rows = jnp.concatenate([jnp.cos(row_angles), jnp.sin(row_angles)], axis=0)
    folded = jnp.dot(left_rows, power, precision=highest, preferred_element_type=jnp.float32)
    col_cos = jnp.cos(col_angles).T
    col_sin = jnp.sin(col_angles).T
    cos_real, sin_real = (folded[:3, :length], folded[3:, :length])
    cos_imag, sin_imag = (folded[:3, length:], folded[3:, length:])
    correlation = (
        jnp.dot(cos_real, col_cos, precision=highest, preferred_element_type=jnp.float32)
        - jnp.dot(sin_real, col_sin, precision=highest, preferred_element_type=jnp.float32)
        - jnp.dot(sin_imag, col_cos, precision=highest, preferred_element_type=jnp.float32)
        - jnp.dot(cos_imag, col_sin, precision=highest, preferred_element_type=jnp.float32)
    ) / length
    weight = jnp.exp(3.0 * jnp.tanh(correlation))
    weight_sum = jnp.sum(weight)
    step_float = step_offsets.astype(jnp.float32)
    shift_y = offset_y.astype(jnp.float32) + jnp.sum(step_float[:, None] * weight) / weight_sum
    shift_x = offset_x.astype(jnp.float32) + jnp.sum(step_float[None, :] * weight) / weight_sum
    return jnp.stack([shift_y, shift_x])


def refine_group(inputs):
    spec_here, spec_next, spec_second, offset_pair = inputs
    first_pair = refine(spec_here, spec_next, offset_pair[0, 0], offset_pair[0, 1])
    second_pair = refine(spec_here, spec_second, offset_pair[1, 0], offset_pair[1, 1])
    return jnp.stack([first_pair, second_pair])


def shards(sections, offsets, node_links):
    local_patches = sections[0]
    patch_count = local_patches.shape[0]
    cos_table, sin_table = dft_tables(local_patches.shape[1])
    right_table = jnp.concatenate([cos_table, sin_table], axis=1)
    left_table = jnp.concatenate([cos_table, sin_table], axis=0)

    def transform(patch):
        return spectrum_one(patch, right_table, left_table)

    next_in = shifted(local_patches, "gz", -1)
    second_in = shifted(local_patches, "gz", -2)
    every_spectra = lax.map(transform, jnp.concatenate([local_patches, next_in, second_in], axis=0))
    local_spectra = every_spectra[:patch_count]
    next_spectra = every_spectra[patch_count : 2 * patch_count]
    second_spectra = every_spectra[2 * patch_count :]
    offset_rows = jnp.moveaxis(offsets[:, :, 0, :], 2, 0)
    pair_shifts = lax.map(refine_group, (local_spectra, next_spectra, second_spectra, offset_rows))
    shifts_found = jnp.transpose(pair_shifts, (1, 2, 0))[:, :, None, :]
    section_index = lax.axis_index("gz")
    section_total = lax.axis_size("gz")
    tile_index = lax.axis_index("tile")
    has_next = (section_index + 1 < section_total).astype(jnp.float32)
    local_links = node_links[:, 0, :] - (tile_index * patch_count - NODE_COLS)
    extent = patch_count + 2 * NODE_COLS
    counts = jnp.sum(
        (local_links[:, :, None] == jnp.arange(extent, dtype=jnp.int32)[None, None, :]).astype(
            jnp.float32
        ),
        axis=0,
    )
    found_next = shifts_found[0]
    positions = jnp.zeros((2, 1, patch_count), jnp.float32)
    for relax_step in range(STEPS):
        widened = extended(positions, (("tile", 2),), NODE_COLS)
        neighbours = jnp.einsum(
            "ie,cze->czi",
            counts,
            widened,
            precision=lax.Precision.HIGHEST,
            preferred_element_type=jnp.float32,
        )
        in_plane = 0.25 * (neighbours - 4.0 * positions)
        ahead_pos = shifted(positions, "gz", -1)
        spring_pull = has_next * (ahead_pos - positions - found_next)
        behind_pull = shifted(spring_pull, "gz", 1)
        spring_force = in_plane + 0.5 * (spring_pull - behind_pull)
        positions = positions + 0.5 * spring_force
    return (shifts_found, positions)


def solution(mesh):
    return jax.shard_map(
        shards,
        mesh=mesh,
        in_specs=(P("gz", "tile", None, None), P(None, None, "gz", "tile"), P(None, "gz", "tile")),
        out_specs=(P(None, None, "gz", "tile"), P(None, "gz", "tile")),
        check_vma=False,
    )
```

profile of v0, /device:TPU:6, one launch (start us, length us, event | category | flops | bytes accessed | tf_op | source)
XLA Modules:
  0.0 339.3 jit_solution(4070361073423787548)
XLA Ops:
  0.6 15.9 %collective-permute-start = (bf16[8,256,256]{2,1,0:T(8,128)(2,1)}, bf16[8,256,256]{2,1,0:T(8,128)(2,1)S(1)}, u32[]{:S(2)}, u32[]{:S(2)}) collective-permute-start(bf16[8,256,256]{2,1,0:T(8,128)(2,1)} %bitcast.119), channel_id=1, source_target_pairs={{4,0},{8,4},{12,8},{16,12},{20,16},{24,20},{28,24},{32,28},{36,32}... | collective-permute-start | bytes 3145736 | tf_op jit(solution)/shard_map/ppermute | solution.py:15
  16.6 2.5 collective-permute-start.1
  19.1 3.0 collective-permute-start.2
  23.4 2.0 collective-permute-start.4
  28.1 22.1 %collective-permute-done = bf16[8,256,256]{2,1,0:T(8,128)(2,1)S(1)} collective-permute-done((bf16[8,256,256]{2,1,0:T(8,128)(2,1)}, bf16[8,256,256]{2,1,0:T(8,128)(2,1)S(1)}, u32[]{:S(2)}, u32[]{:S(2)}) %collective-permute-start) | collective-permute-done | bytes 1048608 | tf_op jit(solution)/shard_map/ppermute | solution.py:15
  50.2 35.1 %collective-permute-done.1 = bf16[8,256,256]{2,1,0:T(8,128)(2,1)S(1)} collective-permute-done((bf16[8,256,256]{2,1,0:T(8,128)(2,1)}, bf16[8,256,256]{2,1,0:T(8,128)(2,1)S(1)}, u32[]{:S(2)}, u32[]{:S(2)}) %collective-permute-start.1) | collective-permute-done | bytes 1048608 | tf_op jit(solution)/shard_map/ppermute | solution.py:15
  85.3 2.9 pad_maximum_fusion.1
  88.2 58.8 %while.22 = (s32[]{:T(128)}, bf16[24,256,512]{2,1,0:T(8,128)(2,1)}, bf16[24,256,256]{2,1,0:T(8,128)(2,1)}, bf16[256,512]{1,0:T(8,128)(2,1)S(1)}, bf16[512,256]{1,0:T(8,128)(2,1)S(1)}, /*index=5*/s32[]{:T(128)}) while((s32[]{:T(128)}, bf16[24,256,512]{2,1,0:T(8,128)(2,1)}, bf16[24,256,256]{2,1,0:T(8,128)(2,1)}, bf16[256,512]{1,0:T(8,128)(2,1)S(1)}, ...), condition=%wide.region_1.2_spmd, body=%wide.region_0.1_spmd.sunk | while | flops 202309632 | bytes 4588613 | solution.py:106
  95.5 1.5 convolution_bitcast_fusion.3
  100.4 1.5 convolution_bitcast_fusion.3
  107.8 1.5 convolution_bitcast_fusion.3
  115.2 1.5 convolution_bitcast_fusion.3
  122.5 1.5 convolution_bitcast_fusion.3
  137.2 1.5 convolution_bitcast_fusion.3
  142.1 1.5 convolution_bitcast_fusion.3
  147.0 5.5 %fusion.143 = (bf16[8,256,512]{2,1,0:T(8,128)(2,1)S(1)}, bf16[8,256,512]{2,1,0:T(8,128)(2,1)}, bf16[8,256,512]{2,1,0:T(8,128)(2,1)}) fusion(bf16[24,256,512]{2,1,0:T(8,128)(2,1)} %get-tuple-element.107), kind=kLoop, calls=%fused_computation.195 | loop fusion | bytes 12582912 | tf_op jit(solution)/shard_map/slice | solution.py:109
  152.5 156.0 %while.23 = (s32[]{:T(128)}, f32[8,2,2]{2,1,0:T(2,128)S(1)}, s32[8,2,2]{2,1,0:T(2,128)S(1)}, bf16[8,256,512]{2,1,0:T(8,128)(2,1)}, bf16[8,256,512]{2,1,0:T(8,128...) while((s32[]{:T(128)}, f32[8,2,2]{2,1,0:T(2,128)S(1)}, s32[8,2,2]{2,1,0:T(2,128)S(1)}, ...), condition=%wide.region_11.12_spmd, body=%wide.region_2.11_spmd.sunk | while | flops 22089944 | bytes 8230629 | solution.py:111
  308.6 1.9 collective-permute-start.5
  311.2 9.2 %collective-permute-done.5 = f32[2,1,8]{2,0,1:T(2,128)S(1)} collective-permute-done((f32[2,1,8]{2,0,1:T(2,128)S(1)}, f32[2,1,8]{2,0,1:T(2,128)S(1)}, u32[]{:S(2)}, u32[]{:S(2)}) %collective-permute-start.5) | collective-permute-done | bytes 96 | tf_op jit(solution)/shard_map/ppermute | solution.py:15
  320.6 2.1 collective-permute-start.8
  322.8 2.6 collective-permute-start.6
  326.7 2.0 collective-permute-start.9
  328.7 2.1 collective-permute-done.7
  330.8 7.7 %collective-permute-done.9 = f32[2,1,8]{2,0,1:T(2,128)S(1)} collective-permute-done((f32[2,1,8]{2,0,1:T(2,128)S(1)}, f32[2,1,8]{2,0,1:T(2,128)S(1)}, u32[]{:S(2)}, u32[]{:S(2)}) %collective-permute-start.9) | collective-permute-done | bytes 96 | tf_op jit(solution)/shard_map/ppermute | solution.py:15
  (346 shorter events, 138.4 us)
Async XLA Ops:
  0.6 49.6 %collective-permute-start = (bf16[8,256,256]{2,1,0:T(8,128)(2,1)}, bf16[8,256,256]{2,1,0:T(8,128)(2,1)S(1)}, u32[]{:S(2)}, u32[]{:S(2)}) collective-permute-start(bf16[8,256,256]{2,1,0:T(8,128)(2,1)} %bitcast.119), channel_id=1, source_target_pairs={{4,0},{8,4},{12,8},{16,12},{20,16},{24,20},{28,24},{32,28},{36,32}... | collective-permute-start | bytes 3145736 | tf_op jit(solution)/shard_map/ppermute | solution.py:15
  16.6 68.8 %collective-permute-start.1 = (bf16[8,256,256]{2,1,0:T(8,128)(2,1)}, bf16[8,256,256]{2,1,0:T(8,128)(2,1)S(1)}, u32[]{:S(2)}, u32[]{:S(2)}) collective-permute-start(bf16[8,256,256]{2,1,0:T(8,128)(2,1)} %bitcast.120), channel_id=1, source_target_pairs={{8,0},{12,4},{16,8},{20,12},{24,16},{28,20},{32,24},{36,28},{40,32... | collective-permute-start | bytes 3145736 | tf_op jit(solution)/shard_map/ppermute | solution.py:15
  19.1 292.1 %collective-permute-start.2 = (f32[2,1,4]{2,0,1:T(2,128)S(1)}, f32[2,1,4]{2,0,1:T(2,128)S(1)}, u32[]{:S(2)}, u32[]{:S(2)}) collective-permute-start(f32[2,1,4]{2,0,1:T(2,128)S(1)} %broadcast.144), channel_id=1, source_target_pairs={{0,1},{1,2},{2,3},{4,5},{5,6},{6,7},{8,9},{9,10},{10,11},{12,13},{... | collective-permute-start | bytes 104 | tf_op jit(solution)/shard_map/ppermute | solution.py:25
  22.1 289.1 %collective-permute-start.3 = (f32[2,1,4]{2,0,1:T(2,128)S(1)}, f32[2,1,4]{2,0,1:T(2,128)S(1)}, u32[]{:S(2)}, u32[]{:S(2)}) collective-permute-start(f32[2,1,4]{2,0,1:T(2,128)S(1)} %broadcast.144), channel_id=1, source_target_pairs={{1,0},{2,1},{3,2},{5,4},{6,5},{7,6},{9,8},{10,9},{11,10},{13,12},{... | collective-permute-start | bytes 104 | tf_op jit(solution)/shard_map/ppermute | solution.py:26
  23.4 285.2 %collective-permute-start.4 = (f32[2,1,8]{2,0,1:T(2,128)S(1)}, f32[2,1,8]{2,0,1:T(2,128)S(1)}, u32[]{:S(2)}, u32[]{:S(2)}) collective-permute-start(f32[2,1,8]{2,0,1:T(2,128)S(1)} %broadcast.145), channel_id=1, source_target_pairs={{4,0},{8,4},{12,8},{16,12},{20,16},{24,20},{28,24},{32,28},{36,32}... | collective-permute-start | bytes 200 | tf_op jit(solution)/shard_map/ppermute | solution.py:15
  308.6 11.8 %collective-permute-start.5 = (f32[2,1,8]{2,0,1:T(2,128)S(1)}, f32[2,1,8]{2,0,1:T(2,128)S(1)}, u32[]{:S(2)}, u32[]{:S(2)}) collective-permute-start(f32[2,1,8]{2,0,1:T(2,128)S(1)} %fusion.138), channel_id=1, source_target_pairs={{0,4},{4,8},{8,12},{12,16},{16,20},{20,24},{24,28},{28,32},{32,36}... | collective-permute-start | bytes 200 | tf_op jit(solution)/shard_map/ppermute | solution.py:15
  320.6 6.1 %collective-permute-start.8 = (f32[2,1,8]{2,0,1:T(2,128)S(1)}, f32[2,1,8]{2,0,1:T(2,128)S(1)}, u32[]{:S(2)}, u32[]{:S(2)}) collective-permute-start(f32[2,1,8]{2,0,1:T(2,128)S(1)} %get-tuple-element.188), channel_id=1, source_target_pairs={{4,0},{8,4},{12,8},{16,12},{20,16},{24,20},{28,24},{32,28},{36,32}... | collective-permute-start | bytes 200 | tf_op jit(solution)/shard_map/ppermute | solution.py:15
  322.8 5.9 %collective-permute-start.6 = (f32[2,1,4]{2,0,1:T(2,128)S(1)}, f32[2,1,4]{2,0,1:T(2,128)S(1)}, u32[]{:S(2)}, u32[]{:S(2)}) collective-permute-start(f32[2,1,4]{2,0,1:T(2,128)S(1)} %get-tuple-element.186), channel_id=1, source_target_pairs={{0,1},{1,2},{2,3},{4,5},{5,6},{6,7},{8,9},{9,10},{10,11},{12,13},{... | collective-permute-start | bytes 104 | tf_op jit(solution)/shard_map/ppermute | solution.py:25
  325.4 5.5 %collective-permute-start.7 = (f32[2,1,4]{2,0,1:T(2,128)S(1)}, f32[2,1,4]{2,0,1:T(2,128)S(1)}, u32[]{:S(2)}, u32[]{:S(2)}) collective-permute-start(f32[2,1,4]{2,0,1:T(2,128)S(1)} %get-tuple-element.187), channel_id=1, source_target_pairs={{1,0},{2,1},{3,2},{5,4},{6,5},{7,6},{9,8},{10,9},{11,10},{13,12},{... | collective-permute-start | bytes 104 | tf_op jit(solution)/shard_map/ppermute | solution.py:26
  326.7 11.8 %collective-permute-start.9 = (f32[2,1,8]{2,0,1:T(2,128)S(1)}, f32[2,1,8]{2,0,1:T(2,128)S(1)}, u32[]{:S(2)}, u32[]{:S(2)}) collective-permute-start(f32[2,1,8]{2,0,1:T(2,128)S(1)} %fusion.139), channel_id=1, source_target_pairs={{0,4},{4,8},{8,12},{12,16},{16,20},{20,24},{24,28},{28,32},{32,36}... | collective-permute-start | bytes 200 | tf_op jit(solution)/shard_map/ppermute | solution.py:15
where the time goes:
time: 343 us; the launch traced here: 339 us
  waiting for transfers between devices  76.2 us (22%)
  loops' own time  73.3 us (21%)
  matrix products  63.8 us (19%)
  other arithmetic  57.2 us (17%)
  starting transfers between devices  34.6 us (10%)
  local copies, waits for them, and re-layouts  33.4 us (10%)
    ppermute x6, waiting for transfers between devices, shifted(): return lax.ppermute(value, axis, pairs)  74.1 us
    another operation x1, loops' own time, shards(): lax.map(refine_group, (local_spectra, next_spectra, second_spectra, offse...  72.6 us
    dot_general x24, matrix products, spectrum_one(): jnp.dot(left_table, half_product, preferred_element_type=jnp.float32)  35.1 us
    ppermute x6, starting transfers between devices, shifted(): return lax.ppermute(value, axis, pairs)  26.4 us
    dynamic_update_slice x48, local copies, waits for them, and re-layouts, shards(): lax.map(transform, jnp.concatenate([local_patches, next_in, second_in], a...  20.9 us
    add x16, other arithmetic, refine(): row_phases = (offset_y + step_offsets)[:, None] * indices[None, :] % length  10.2 us
    add x16, other arithmetic, refine(): col_phases = (offset_x + step_offsets)[:, None] * indices[None, :] % length  10.1 us
    dot_general x16, matrix products, refine(): jnp.dot(cos_imag, col_sin, precision=highest, preferred_element_type=jnp....  9.93 us
  transfers between devices with their start and end apart: 10, of which 5 were waited for; matrix products, arithmetic and copies ran while one was open for 45% of the time, Pallas kernels for 0%

commit v1 on v0

v1 whole, which is shorter than its diff:
```python
import functools
import math

import jax
import jax.numpy as jnp
import ml_dtypes
import numpy as np
from jax import lax
from jax.experimental import pallas as pl
from jax.experimental.pallas import tpu as pltpu
from jax.sharding import PartitionSpec as P

NODE_COLS = 4
STEPS = 2
SIDE = 256
HALF = SIDE // 2
ROWS = 144
REACH = 4
SPAN = 16
GROUP = 4
EXTRA = 16
BLOCK = GROUP * SIDE + EXTRA

SLOTS = ((0, 1, 4, 3, 2), (1, 0, 3, -1, None), (2, 3, 0, 4, None), (3, 2, -1, 0, 1))
STAGES = (
    ((), ((0, 1), (1, 3)), ((2, 3), (0, 2)), ()),
    (((3, 4),), ((-1, 0), (-1, 1)), ((3, 4), (2, 4)), ((-1, 0),)),
    (((1, 2), (2, 3), (0, 2), (2, 4)), (), (), ((0, 1), (1, 2), (-1, 1), (1, 3))),
)


def pair_places():
    places = {}
    for device in range(4):
        order = [pair for stage in STAGES for pair in stage[device]]
        for place, pair in enumerate(order):
            places[(device // 2, pair)] = (device, place)
    return places


def pair_table():
    table = np.zeros((3, 4, 17), np.int32)
    places = pair_places()
    for number, stage in enumerate(STAGES):
        for device in range(4):
            table[number, device, 0] = len(stage[device])
            for k, (a, b) in enumerate(stage[device]):
                slots = SLOTS[device]
                entry = (slots.index(a), slots.index(b), b - a - 1, places[(device // 2, (a, b))][1])
                table[number, device, 1 + 4 * k : 5 + 4 * k] = entry
    return table


def tables():
    index = np.arange(SIDE)

    def angle(phases):
        return (phases % SIDE).astype(np.float32) * np.float32(2.0 * math.pi / SIDE)

    phases = np.outer(index, index)
    cos_table = np.cos(angle(phases)).astype(ml_dtypes.bfloat16)
    sin_table = np.sin(angle(phases)).astype(ml_dtypes.bfloat16)
    right = np.concatenate([cos_table[: HALF + 1], sin_table[1:HALF]], axis=0)
    left = np.ascontiguousarray(right.T)
    row_freq = np.concatenate([np.arange(HALF + 1), -np.arange(1, HALF)])
    window = np.arange(-REACH, REACH + 1)
    fold_phase = 2.0 * math.pi * (np.outer(row_freq, window) % SIDE) / SIDE
    fold_cos, fold_sin = np.cos(fold_phase), np.sin(fold_phase)
    fold = np.zeros((GROUP, 2, SIDE, 2, 2, GROUP, SPAN), np.float32)
    for j in range(GROUP):
        for part, out, value in ((0, 0, fold_cos), (1, 0, -fold_sin), (0, 1, fold_sin), (1, 1, fold_cos)):
            high = value.astype(np.float32).astype(ml_dtypes.bfloat16).astype(np.float32)
            fold[j, part, :, out, 0, j, : window.size] = high
            fold[j, part, :, out, 1, j, : window.size] = value - high
    fold = fold.reshape(GROUP * 2 * SIDE, SIDE).astype(ml_dtypes.bfloat16)
    col_freq = np.arange(HALF + 1)
    twice = np.where((col_freq == 0) | (col_freq == HALF), 1.0, 2.0)[None, :] / SIDE
    col_phase = 2.0 * math.pi * (np.outer(window, col_freq) % SIDE) / SIDE
    close = np.zeros((2, SPAN, ROWS), np.float32)
    close[0, : window.size, : HALF + 1] = twice * np.cos(col_phase)
    close[1, : window.size, : HALF + 1] = twice * np.sin(col_phase)
    return right, left, fold, close.reshape(2 * SPAN, ROWS)


def transform(patch, right, left):
    half_product = lax.dot_general(
        right, patch, (((1,), (1,)), ((), ())), preferred_element_type=jnp.float32
    ).astype(jnp.bfloat16)
    full = jnp.dot(half_product, left, preferred_element_type=jnp.float32)
    lane = lax.broadcasted_iota(jnp.int32, (HALF, HALF), 1)
    row = lax.broadcasted_iota(jnp.int32, (HALF, HALF), 0)
    first_lane, first_row = lane == 0, row == 0
    cc, sc = full[:HALF, :HALF], full[:HALF, HALF:]
    last_c, last_s = full[HALF:, :HALF], full[HALF:, HALF:]
    cs, ss = jnp.where(first_row, 0.0, last_c), jnp.where(first_row, 0.0, last_s)

    def parts(cc, sc, cs, ss, edge):
        low_sc, low_ss = jnp.where(edge, 0.0, sc), jnp.where(edge, 0.0, ss)
        return jnp.concatenate(
            [
                cc - low_ss,
                jnp.where(edge, sc, cc + ss),
                -(cs + low_sc),
                jnp.where(edge, -ss, sc - cs),
            ],
            axis=1,
        ).astype(jnp.bfloat16)

    tail = ROWS - HALF
    keep = row[:tail] == 0
    end_c, end_s = jnp.where(keep, last_c[:tail], 0.0), jnp.where(keep, last_s[:tail], 0.0)
    none = jnp.zeros_like(end_c)
    return parts(cc, sc, cs, ss, first_lane), parts(end_c, end_s, none, none, first_lane[:tail])


def stage_kernel(number, new_count, old_count, *refs):
    table, right, left, fold, close, before = refs[:6]
    payloads = refs[6 : 6 + 2 * new_count]
    old_specs = refs[6 + 2 * new_count : 6 + 2 * new_count + old_count]
    old_offs = refs[6 + 2 * new_count + old_count : 6 + 2 * new_count + 2 * old_count]
    rest = refs[6 + 2 * new_count + 2 * old_count :]
    found, new_specs, new_offs = rest[0], rest[1 : 1 + new_count], rest[1 + new_count : 1 + 2 * new_count]
    specs, cross_r, cross_i, size, power, offs, old_sem, new_sem = rest[1 + 2 * new_count :]
    device = lax.rem(lax.axis_index("gz"), 4)
    chunk = 16

    old_copies = [
        pltpu.make_async_copy(old_specs[k], specs.at[pl.ds(GROUP * k, GROUP)], old_sem.at[k]) for k in range(old_count)
    ]
    for copy in old_copies:
        copy.start()
    for k in range(old_count):
        offs[k] = old_offs[k][...]
    right_table, left_table = right[...], left[...]
    for k in range(new_count):
        first, other = payloads[2 * k], payloads[2 * k + 1]
        slot = old_count + k
        both = first[GROUP * SIDE :, :] + other[GROUP * SIDE :, :]
        offs[slot] = both
        new_offs[k][...] = both

        @pl.loop(0, GROUP)
        def _(n, first=first, other=other, slot=slot):
            rows = pl.ds(pl.multiple_of(n * SIDE, SIDE), SIDE)
            main, end = transform(first[rows, :] + other[rows, :], right_table, left_table)
            specs[slot * GROUP + n, :HALF, :] = main
            specs[slot * GROUP + n, HALF:, :] = end

    new_copies = [
        pltpu.make_async_copy(specs.at[pl.ds(GROUP * (old_count + k), GROUP)], new_specs[k], new_sem.at[k])
        for k in range(new_count)
    ]
    for copy in old_copies:
        copy.wait()
    for copy in new_copies:
        copy.start()

    found[...] = before[...]
    lane = lax.broadcasted_iota(jnp.int32, (SPAN, 128), 1)
    step_u = (lax.rem(lane, SPAN) - REACH).astype(jnp.float32)
    step_v = (lax.broadcasted_iota(jnp.int32, (SPAN, 128), 0) - REACH).astype(jnp.float32)
    place_row = lax.broadcasted_iota(jnp.int32, (16, 128), 0)

    @pl.loop(0, table[number, device, 0])
    def _(k):
        base = 1 + 4 * k
        slot_a, slot_b = table[number, device, base], table[number, device, base + 1]
        partner, place = table[number, device, base + 2], table[number, device, base + 3]
        for j in range(GROUP):
            total = jnp.zeros((8, SIDE), jnp.float32)
            for start in range(0, ROWS, chunk):
                rows = slice(start, start + chunk)
                a = specs[slot_a * GROUP + j, rows, :].astype(jnp.float32)
                b = specs[slot_b * GROUP + j, rows, :].astype(jnp.float32)
                ar, ai, br, bi = a[:, :SIDE], a[:, SIDE:], b[:, :SIDE], b[:, SIDE:]
                real = ar * br + ai * bi
                imag = ai * br - ar * bi
                square = real * real + imag * imag
                magnitude = square * lax.rsqrt(jnp.maximum(square, 1e-30))
                cross_r[j, rows, :] = real
                cross_i[j, rows, :] = imag
                size[j, rows, :] = magnitude
                if start == 0:
                    edge = lax.broadcasted_iota(jnp.int32, (chunk, SIDE), 0) == 0
                    magnitude = jnp.where(edge, 0.5 * magnitude, magnitude)
                elif start == HALF:
                    magnitude = 0.5 * magnitude
                total = total + magnitude[:8] + magnitude[8:]
            mean = jnp.sum(total) * (2.0 / (SIDE * SIDE))
            floor = mean + 1e-6
            for start in range(0, ROWS, chunk):
                rows = slice(start, start + chunk)
                scale = pl.reciprocal(size[j, rows, :] + floor, approx=False)
                power[rows, 2 * SIDE * j : 2 * SIDE * j + SIDE] = (cross_r[j, rows, :] * scale).astype(jnp.bfloat16)
                power[rows, 2 * SIDE * j + SIDE : 2 * SIDE * (j + 1)] = (cross_i[j, rows, :] * scale).astype(jnp.bfloat16)
        folded = jnp.dot(power[...], fold[...], preferred_element_type=jnp.float32)
        closed = jnp.dot(
            close[...], folded, precision=lax.Precision.HIGHEST, preferred_element_type=jnp.float32
        )
        correlation = closed[:SPAN, :128] - closed[SPAN:, 128:]
        correlation = correlation + pltpu.roll(correlation, 64, axis=1)
        own = offs[slot_a].astype(jnp.float32)
        here = jnp.where(partner == 0, own[0:2, :128], own[2:4, :128])
        off_y, off_x = here[0:1], here[1:2]
        from_y, from_x = step_u - off_y, step_v - off_x
        inside = (jnp.abs(from_y) < 1.5) & (jnp.abs(from_x) < 1.5)
        weight = jnp.where(inside, jnp.exp(3.0 * jnp.tanh(correlation)), 0.0)
        sums = jnp.concatenate(
            [
                jnp.sum(weight, axis=0, keepdims=True),
                jnp.sum(weight * from_y, axis=0, keepdims=True),
                jnp.sum(weight * from_x, axis=0, keepdims=True),
                jnp.zeros((5, 128), jnp.float32),
            ],
            axis=0,
        )
        for shift in (8, 4, 2, 1):
            sums = sums + pltpu.roll(sums, 128 - shift, axis=1)
        shift_y = off_y + sums[1:2] / sums[0:1]
        shift_x = off_x + sums[2:3] / sums[0:1]
        found[...] = jnp.where(
            place_row == 2 * place, shift_y, jnp.where(place_row == 2 * place + 1, shift_x, found[...])
        )

    for copy in new_copies:
        copy.wait()


def run_stage(number, consts, before, payloads, old_specs, old_offs):
    new_count, old_count = len(payloads), len(old_specs)
    vmem, hbm = pl.BlockSpec(memory_space=pltpu.VMEM), pl.BlockSpec(memory_space=pl.ANY)
    slots = new_count + old_count
    spec_shape = jax.ShapeDtypeStruct((GROUP, ROWS, 2 * SIDE), jnp.bfloat16)
    off_shape = jax.ShapeDtypeStruct((EXTRA, SIDE), jnp.bfloat16)
    out = pl.pallas_call(
        functools.partial(stage_kernel, number, new_count, old_count),
        out_shape=(jax.ShapeDtypeStruct((16, 128), jnp.float32),)
        + (spec_shape,) * new_count
        + (off_shape,) * new_count,
        in_specs=[pl.BlockSpec(memory_space=pltpu.SMEM)]
        + [vmem] * (5 + 2 * new_count)
        + [hbm] * old_count
        + [vmem] * old_count,
        out_specs=(vmem,) + (hbm,) * new_count + (vmem,) * new_count,
        scratch_shapes=[
            pltpu.VMEM((slots * GROUP, ROWS, 2 * SIDE), jnp.bfloat16),
            pltpu.VMEM((GROUP, ROWS, SIDE), jnp.float32),
            pltpu.VMEM((GROUP, ROWS, SIDE), jnp.float32),
            pltpu.VMEM((GROUP, ROWS, SIDE), jnp.float32),
            pltpu.VMEM((ROWS, 2 * SIDE * GROUP), jnp.bfloat16),
            pltpu.VMEM((slots, EXTRA, SIDE), jnp.bfloat16),
            pltpu.SemaphoreType.DMA((max(old_count, 1),)),
            pltpu.SemaphoreType.DMA((max(new_count, 1),)),
        ],
        compiler_params=pltpu.CompilerParams(vmem_limit_bytes=40 * 1024 * 1024),
        name=f"stage{number}",
    )(*consts, before, *[p for pair in payloads for p in pair], *old_specs, *old_offs)
    return out[0], out[1 : 1 + new_count], out[1 + new_count :]


def shards(sections, offsets, node_links):
    patches = sections[0]
    sections_total, tiles = lax.axis_size("gz"), lax.axis_size("tile")
    position = lax.axis_index("gz")
    tile_index = lax.axis_index("tile")
    device = position % 4
    chip = device // 2

    def send(value, moves):
        pairs = [(i, i + moves[i % 4]) for i in range(sections_total) if i % 4 in moves]
        return lax.ppermute(value, "gz", [(i, j) for i, j in pairs if 0 <= j < sections_total])

    lanes = jnp.repeat(offsets[:, :, 0, :].reshape(4, 2, GROUP).astype(jnp.bfloat16), SPAN, axis=2)
    lanes = jnp.pad(jnp.moveaxis(lanes, 1, 0), ((0, 0), (0, EXTRA - 4), (0, SIDE - GROUP * SPAN)))
    flat = patches.reshape(2, GROUP * SIDE, SIDE)

    def block(row):
        return jnp.concatenate(
            [
                lax.dynamic_index_in_dim(flat, row, 0, keepdims=False),
                lax.dynamic_index_in_dim(lanes, row, 0, keepdims=False),
            ],
            axis=0,
        )

    away, own = block(1 - chip), block(chip)
    first = send(away, {0: 2, 3: -2})
    second = send(away, {2: -2, 1: 2})
    beside = send(own, {0: 1, 1: -1, 2: 1, 3: -1})
    border = send(own, {0: -4, 3: 4})
    border_late = send(first, {2: -4, 1: 4})
    first_on = send(first, {1: -1, 2: 1})

    right, left, fold, close = tables()
    consts = (jnp.asarray(pair_table()), *(jnp.asarray(t) for t in (right, left, fold, close)))
    nothing = jnp.zeros((16, 128), jnp.float32)
    zeros = jnp.zeros((BLOCK, SIDE), jnp.bfloat16)
    found, specs, offs = run_stage(
        0, consts, nothing, [(own, zeros), (beside, zeros), (first, border)], [], []
    )
    found, more_specs, more_offs = run_stage(1, consts, found, [(first_on, border_late)], specs, offs)
    found, _, _ = run_stage(2, consts, found, [(second, zeros)], specs + more_specs, offs + more_offs)

    quads = [list(range(4 * g, 4 * g + 4)) for g in range(sections_total // 4)]
    every = lax.all_gather(found, "gz", axis_index_groups=quads)
    values = every[:, :, : GROUP * SPAN : SPAN].reshape(4, 8, 2, GROUP)
    places = pair_places()

    def shift_of(pair):
        return jnp.concatenate([values[places[(row, pair)]] for row in range(2)], axis=1)

    next_all = jnp.stack([shift_of((s, s + 1)) for s in range(-1, 4)])
    second_all = jnp.stack([shift_of((s, s + 2)) for s in range(-1, 3)])
    halo_out = jnp.where(
        device == 0, jnp.stack([next_all[3], second_all[0]]), jnp.stack([next_all[1], second_all[0]])
    )
    halo = send(halo_out, {0: 4, 3: -4})
    found_behind = lax.dynamic_index_in_dim(next_all, device, 0, keepdims=False)
    found_next = lax.dynamic_index_in_dim(next_all, device + 1, 0, keepdims=False)
    found_behind2 = jnp.where(
        device == 0, halo[0], lax.dynamic_index_in_dim(next_all, jnp.maximum(device - 1, 0), 0, keepdims=False)
    )
    found_ahead = jnp.where(
        device == 3, halo[0], lax.dynamic_index_in_dim(next_all, jnp.minimum(device + 2, 4), 0, keepdims=False)
    )
    found_second = jnp.where(
        device == 3, halo[1], lax.dynamic_index_in_dim(second_all, jnp.minimum(device + 1, 3), 0, keepdims=False)
    )
    own_offsets = offsets[:, :, 0, :].astype(jnp.float32)
    found_second = jnp.where(position + 2 < sections_total, found_second, own_offsets[1])
    has_next = [
        ((position + d >= 0) & (position + d + 1 < sections_total)).astype(jnp.float32) for d in (-2, -1, 0, 1)
    ]
    pulls = [-h * f for h, f in zip(has_next, (found_behind2, found_behind, found_next, found_ahead))]
    behind_pos, positions, ahead_pos = (0.25 * (pulls[k + 1] - pulls[k]) for k in range(3))
    up = [(i, i + 1) for i in range(tiles - 1)]
    above = lax.ppermute(positions[:, GROUP:], "tile", up)
    below = lax.ppermute(positions[:, :GROUP], "tile", [(j, i) for i, j in up])
    widened = jnp.concatenate([above, positions, below], axis=1)
    count = positions.shape[1]
    links = node_links[:, 0, :] - (tile_index * count - NODE_COLS)
    extent = jnp.arange(count + 2 * NODE_COLS, dtype=jnp.int32)
    counts = jnp.sum((links[:, :, None] == extent[None, None, :]).astype(jnp.float32), axis=0)
    neighbours = jnp.sum(counts[None] * widened[:, None, :], axis=2)
    in_plane = 0.25 * (neighbours - 4.0 * positions)
    pull = has_next[2] * (ahead_pos - positions - found_next)
    pull_behind = has_next[1] * (positions - behind_pos - found_behind)
    positions = positions + 0.5 * (in_plane + 0.5 * (pull - pull_behind))
    shifts_found = jnp.stack([found_next, found_second])
    return (shifts_found[:, :, None, :], positions[:, None, :])


def solution(mesh):
    return jax.shard_map(
        shards,
        mesh=mesh,
        in_specs=(P("gz", "tile", None, None), P(None, None, "gz", "tile"), P(None, "gz", "tile")),
        out_specs=(P(None, None, "gz", "tile"), P(None, "gz", "tile")),
        check_vma=False,
    )
```

time: 343 us -> 89.3 us (0.26)
  loops' own time: 73.3 us -> 0 us
  waiting for transfers between devices: 76.2 us -> 11 us
  matrix products: 63.8 us -> 0 us
  other arithmetic: 57.2 us -> 3.64 us
  local copies, waits for them, and re-layouts: 33.4 us -> 1.79 us
  blocking collectives: 0 us -> 19.9 us
  Pallas kernels: 0 us -> 18.8 us
    another operation x2 -> x0, loops' own time: 73.3 us -> none  [the longest x1 72.6 us: shards(): lax.map(refine_group, (local_spectra, next_spectra, second_spectra, offse...]
    ppermute x10 -> x9, waiting for transfers between devices: 76.2 us -> 11 us  [the longest x7 8.97 us: send(): lax.ppermute(value, 'gz', [(i, j) for i, j in pairs if 0 <= j < sections_...]
    dot_general x106 -> x0, matrix products: 63.8 us -> none  [the longest x24 35.1 us: spectrum_one(): jnp.dot(left_table, half_product, preferred_element_type=jnp.float32)]
    dynamic_update_slice x48 -> x0, local copies, waits for them, and re-layouts: 20.9 us -> none  [shards(): lax.map(transform, jnp.concatenate([local_patches, next_in, second_in], a...]
    all_gather x0 -> x1, blocking collectives: none -> 19.9 us  [shards(): every = lax.all_gather(found, 'gz', axis_index_groups=quads)]
    add x32 -> x1, other arithmetic: 20.3 us -> 0.58 us  [shards(): positions = positions + 0.5 * (in_plane + 0.5 * (pull - pull_behind))]
    pallas_call x0 -> x3, Pallas kernels: none -> 18.8 us  [run_stage(): pl.pallas_call(functools.partial(stage_kernel, number, new_count, old_cou...]
    convert_element_type x17 -> x2, other arithmetic: 17.7 us -> 0.71 us  [the longest x1 0.7 us: shards(): offsets[:, :, 0, :].reshape(4, 2, GROUP).astype(jnp.bfloat16)]
  transfers between devices with their start and end apart: 10 -> 9, of which waited for: 5 -> 4; matrix products, arithmetic and copies ran while one was open for 45% -> 1% of each run, Pallas kernels for 0% -> 12%
where the time goes in v1:
time: 89.3 us; the launch traced here: 87.8 us
  starting transfers between devices  31.7 us (35%)
  blocking collectives  19.9 us (22%)
  Pallas kernels  18.8 us (21%)
  waiting for transfers between devices  11 us (12%)
  other arithmetic  3.64 us (4%)
  local copies, waits for them, and re-layouts  1.79 us (2%)
  between operations  1.01 us (1%)
    ppermute x7, starting transfers between devices, send(): lax.ppermute(value, 'gz', [(i, j) for i, j in pairs if 0 <= j < sections_...  26.2 us
    all_gather x1, blocking collectives, shards(): every = lax.all_gather(found, 'gz', axis_index_groups=quads)  19.9 us
    pallas_call x3, Pallas kernels, run_stage(): pl.pallas_call(functools.partial(stage_kernel, number, new_count, old_cou...  18.8 us
    ppermute x7, waiting for transfers between devices, send(): lax.ppermute(value, 'gz', [(i, j) for i, j in pairs if 0 <= j < sections_...  8.97 us
    ppermute x1, starting transfers between devices, shards(): above = lax.ppermute(positions[:, GROUP:], 'tile', up)  4.18 us
    ppermute x1, waiting for transfers between devices, shards(): below = lax.ppermute(positions[:, :GROUP], 'tile', [(j, i) for i, j in up])  2.01 us
  transfers between devices with their start and end apart: 9, of which 4 were waited for; matrix products, arithmetic and copies ran while one was open for 1% of the time, Pallas kernels for 12%

profile of v1, /device:TPU:6, one launch (start us, length us, event | category | flops | bytes accessed | tf_op | source)
XLA Modules:
  0.0 87.8 jit_solution(17769102835799657544)
XLA Ops:
  0.7 0.7 convert_reduce_fusion.1
  1.5 0.1 reshape.169
  1.6 1.3 %dynamic-slice_bitcast_fusion = (bf16[1024,256]{1,0:T(8,128)(2,1)S(1)}, bf16[1024,256]{1,0:T(8,128)(2,1)S(1)}) fusion(bf16[2,1024,256]{2,1,0:T(8,128)(2,1)} %bitcast.140, s32[]{:T(128)S(6)} %select_n.89, s32[]{:T(128)S(6)} %select_n.88), kind=kLoop, calls=%fused_computation.2 | loop fusion | bytes 2097160 | tf_op jit(solution)/shard_map/jit(dynamic_index_in_dim)/squeeze | solution.py:280
  3.0 0.8 pad_maximum_fusion.1
  3.8 7.9 %collective-permute-start.1 = (bf16[1040,256]{1,0:T(8,128)(2,1)}, bf16[1040,256]{1,0:T(8,128)(2,1)S(1)}, u32[]{:S(2)}, u32[]{:S(2)}) collective-permute-start(bf16[1040,256]{1,0:T(8,128)(2,1)} %pad_maximum_fusion.1), channel_id=1, source_target_pairs={{0,8},{12,4},{16,24},{28,20},{32,40},{44,36},{48,56},{60,52},{64,7... | collective-permute-start | bytes 1597448 | tf_op jit(solution)/shard_map/ppermute | solution.py:271
  11.8 1.9 %collective-permute-start = (bf16[1040,256]{1,0:T(8,128)(2,1)S(1)}, bf16[1040,256]{1,0:T(8,128)(2,1)S(1)}, u32[]{:S(2)}, u32[]{:S(2)}) collective-permute-start(bf16[1040,256]{1,0:T(8,128)(2,1)S(1)} %pad_maximum_fusion.refs_6_), channel_id=1, source_target_pairs={{0,4},{4,0},{8,12},{12,8},{16,20},{20,16},{24,28},{28,24},{32,36},... | collective-permute-start | bytes 1597448 | tf_op jit(solution)/shard_map/ppermute | solution.py:271
  13.7 11.2 %collective-permute-start.2 = (bf16[1040,256]{1,0:T(8,128)(2,1)S(1)}, bf16[1040,256]{1,0:T(8,128)(2,1)}, u32[]{:S(2)}, u32[]{:S(2)}) collective-permute-start(bf16[1040,256]{1,0:T(8,128)(2,1)S(1)} %pad_maximum_fusion.refs_6_), channel_id=1, source_target_pairs={{12,28},{16,0},{28,44},{32,16},{44,60},{48,32},{60,76},{64,48},{76... | collective-permute-start | bytes 1597448 | tf_op jit(solution)/shard_map/ppermute | solution.py:271
  24.9 1.3 %collective-permute-start.5 = (bf16[1040,256]{1,0:T(8,128)(2,1)}, bf16[1040,256]{1,0:T(8,128)(2,1)S(1)}, u32[]{:S(2)}, u32[]{:S(2)}) collective-permute-start(bf16[1040,256]{1,0:T(8,128)(2,1)} %pad_maximum_fusion.1), channel_id=1, source_target_pairs={{4,12},{8,0},{20,28},{24,16},{36,44},{40,32},{52,60},{56,48},{68,7... | collective-permute-start | bytes 1597448 | tf_op jit(solution)/shard_map/ppermute | solution.py:271
  26.3 1.3 %collective-permute-start.3 = (bf16[1040,256]{1,0:T(8,128)(2,1)S(1)}, bf16[1040,256]{1,0:T(8,128)(2,1)S(1)}, u32[]{:S(2)}, u32[]{:S(2)}) collective-permute-start(bf16[1040,256]{1,0:T(8,128)(2,1)S(1)} %collective-permute-done.1.refs_10_), channel_id=1, source_target_pairs={{4,0},{8,12},{20,16},{24,28},{36,32},{40,44},{52,48},{56,60},{68,6... | collective-permute-start | bytes 1597448 | tf_op jit(solution)/shard_map/ppermute | solution.py:271
  27.6 0.7 collective-permute-start.4
  28.4 3.3 %collective-permute-done.2.refs_11_ = bf16[1040,256]{1,0:T(8,128)(2,1)} collective-permute-done((bf16[1040,256]{1,0:T(8,128)(2,1)S(1)}, bf16[1040,256]{1,0:T(8,128)(2,1)}, u32[]{:S(2)}, u32[]{:S(2)}) %collective-permute-start.2) | collective-permute-done | bytes 532512 | tf_op jit(solution)/shard_map/ppermute | solution.py:271
  31.8 6.1 %stage0.1 = (f32[16,128]{1,0:T(8,128)S(1)}, bf16[4,144,512]{2,1,0:T(8,128)(2,1)S(1)}, bf16[4,144,512]{2,1,0:T(8,128)(2,1)S(1)}, bf16[4,144,512]{2,1,0:T(8,128)(2...) custom-call(s32[3,4,17]{2,1,0:T(4,128)S(1)} %copy-done.4, ...), custom_call_target="tpu_custom_call" | custom-call | tf_op jit(solution)/shard_map/stage0/pallas_call | solution.py:235
  37.9 4.1 %stage1.1 = (f32[16,128]{1,0:T(8,128)S(1)}, bf16[4,144,512]{2,1,0:T(8,128)(2,1)S(1)}, bf16[16,256]{1,0:T(8,128)(2,1)S(1)}) custom-call(s32[3,4,17]{2,1,0:T(4,128)S(1)} %copy-done.4, bf16[256,256]{1,0:T(8,128)(2,1)S(1)} %copy-done.1, bf16[256,256]{1,0:T(8,128)(2,1)S(1)} %copy-done.2, bf16[2048,256]{1,0:T(8,128)(2,1)S(1)} %copy-done, f32[32,144]{1,0:T(8,128)S(1)} %copy-done.3, ...), custom_call_target="tpu_custom_call" | custom-call | tf_op jit(solution)/shard_map/stage1/pallas_call | solution.py:235
  42.0 2.4 %collective-permute-done.5.refs_6_ = bf16[1040,256]{1,0:T(8,128)(2,1)S(1)} collective-permute-done((bf16[1040,256]{1,0:T(8,128)(2,1)}, bf16[1040,256]{1,0:T(8,128)(2,1)S(1)}, u32[]{:S(2)}, u32[]{:S(2)}) %collective-permute-start.5) | collective-permute-done | bytes 532512 | tf_op jit(solution)/shard_map/ppermute | solution.py:271
  44.3 8.7 %stage2.1 = (f32[16,128]{1,0:T(8,128)S(1)}, bf16[4,144,512]{2,1,0:T(8,128)(2,1)}, bf16[16,256]{1,0:T(8,128)(2,1)}) custom-call(s32[3,4,17]{2,1,0:T(4,128)S(1)} %copy-done.4, bf16[256,256]{1,0:T(8,128)(2,1)S(1)} %copy-done.1, bf16[256,256]{1,0:T(8,128)(2,1)S(1)} %copy-done.2, bf16[2048,256]{1,0:T(8,128)(2,1)S(1)} %copy-done, f32[32,144]{1,0:T(8,128)S(1)} %copy-done.3, ...), custom_call_target="tpu_custom_call" | custom-call | tf_op jit(solution)/shard_map/stage2/pallas_call | solution.py:235
  53.0 19.9 %all-gather = f32[64,128]{1,0:T(8,128)S(1)} all-gather(f32[16,128]{1,0:T(8,128)S(1)} %get-tuple-element.23), channel_id=2, replica_groups={{0,4,8,12},{16,20,24,28},{32,36,40,44},{48,52,56,60},{64,68,72,76},{80,..., dimensions={0}, use_global_device_ids=true | all-gather | bytes 40960 | tf_op jit(solution)/shard_map/all_gather | solution.py:305
  73.5 4.2 %collective-permute-start.7 = (f32[2,4]{1,0:T(2,128)S(1)}, f32[2,4]{1,0:T(2,128)S(1)}, u32[]{:S(2)}, u32[]{:S(2)}) collective-permute-start(f32[2,4]{1,0:T(2,128)S(1)} %get-tuple-element.56), channel_id=1, source_target_pairs={{0,1},{1,2},{2,3},{4,5},{5,6},{6,7},{8,9},{9,10},{10,11},{12,13},{... | collective-permute-start | bytes 104 | tf_op jit(solution)/shard_map/ppermute | solution.py:337
  77.7 1.3 %collective-permute-start.8 = (f32[2,4]{1,0:T(2,128)S(1)}, f32[2,4]{1,0:T(2,128)S(1)}, u32[]{:S(2)}, u32[]{:S(2)}) collective-permute-start(f32[2,4]{1,0:T(2,128)S(1)} %get-tuple-element.57), channel_id=1, source_target_pairs={{1,0},{2,1},{3,2},{5,4},{6,5},{7,6},{9,8},{10,9},{11,10},{13,12},{... | collective-permute-start | bytes 104 | tf_op jit(solution)/shard_map/ppermute | solution.py:338
  79.1 1.9 %collective-permute-start.6 = (f32[2,2,8]{2,1,0:T(2,128)S(1)}, f32[2,2,8]{2,1,0:T(2,128)S(1)}, u32[]{:S(2)}, u32[]{:S(2)}) collective-permute-start(f32[2,2,8]{2,1,0:T(2,128)S(1)} %fusion.2), channel_id=1, source_target_pairs={{0,16},{16,32},{28,12},{32,48},{44,28},{48,64},{60,44},{64,80},{76... | collective-permute-start | bytes 392 | tf_op jit(solution)/shard_map/ppermute | solution.py:271
  81.1 2.0 %collective-permute-done.8 = f32[2,4]{1,0:T(2,128)S(1)} collective-permute-done((f32[2,4]{1,0:T(2,128)S(1)}, f32[2,4]{1,0:T(2,128)S(1)}, u32[]{:S(2)}, u32[]{:S(2)}) %collective-permute-start.8) | collective-permute-done | bytes 64 | tf_op jit(solution)/shard_map/ppermute | solution.py:338
  83.2 0.1 multiply_reduce_fusion
  83.3 3.3 %collective-permute-done.6 = f32[2,2,8]{2,1,0:T(2,128)S(1)} collective-permute-done((f32[2,2,8]{2,1,0:T(2,128)S(1)}, f32[2,2,8]{2,1,0:T(2,128)S(1)}, u32[]{:S(2)}, u32[]{:S(2)}) %collective-permute-start.6) | collective-permute-done | bytes 160 | tf_op jit(solution)/shard_map/ppermute | solution.py:271
  86.6 0.6 pad_maximum_fusion.4
  87.2 0.6 fusion.24
  (44 shorter events, 1.3 us)
Async XLA Ops:
  2.9 25.4 %copy-start.6 = (s32[4,1,8]{2,1,0:T(1,128)S(1)}, s32[4,1,8]{2,1,0:T(1,128)}, u32[]{:S(2)}) copy-start(s32[4,1,8]{2,1,0:T(1,128)} %param.10) | copy-start | bytes 388
  2.9 25.5 %copy-start.5 = (s32[2,2,1,8]{3,2,1,0:T(1,128)S(1)}, s32[2,2,1,8]{3,2,1,0:T(1,128)}, u32[]{:S(2)}) copy-start(s32[2,2,1,8]{3,2,1,0:T(1,128)} %param.9) | copy-start | bytes 388
  3.8 27.9 %copy-start = (bf16[2048,256]{1,0:T(8,128)(2,1)S(1)}, bf16[2048,256]{1,0:T(8,128)(2,1)}, u32[]{:S(2)}) copy-start(bf16[2048,256]{1,0:T(8,128)(2,1)} %constant.108.clone.refs_3_) | copy-start | bytes 3145732
  3.8 27.9 %copy-start.1 = (bf16[256,256]{1,0:T(8,128)(2,1)S(1)}, bf16[256,256]{1,0:T(8,128)(2,1)}, u32[]{:S(2)}) copy-start(bf16[256,256]{1,0:T(8,128)(2,1)} %constant.106.clone.refs_1_) | copy-start | bytes 393220
  3.8 28.0 %copy-start.2 = (bf16[256,256]{1,0:T(8,128)(2,1)S(1)}, bf16[256,256]{1,0:T(8,128)(2,1)}, u32[]{:S(2)}) copy-start(bf16[256,256]{1,0:T(8,128)(2,1)} %constant.107.clone.refs_2_) | copy-start | bytes 393220
  3.8 28.0 %copy-start.3 = (f32[32,144]{1,0:T(8,128)S(1)}, f32[32,144]{1,0:T(8,128)}, u32[]{:S(2)}) copy-start(f32[32,144]{1,0:T(8,128)} %constant.109.clone.refs_4_) | copy-start | bytes 55300
  3.8 28.0 %copy-start.4 = (s32[3,4,17]{2,1,0:T(4,128)S(1)}, s32[3,4,17]{2,1,0:T(4,128)}, u32[]{:S(2)}) copy-start(s32[3,4,17]{2,1,0:T(4,128)} %constant.105.clone.refs_0_) | copy-start | bytes 2452
  3.8 22.5 %collective-permute-start.1 = (bf16[1040,256]{1,0:T(8,128)(2,1)}, bf16[1040,256]{1,0:T(8,128)(2,1)S(1)}, u32[]{:S(2)}, u32[]{:S(2)}) collective-permute-start(bf16[1040,256]{1,0:T(8,128)(2,1)} %pad_maximum_fusion.1), channel_id=1, source_target_pairs={{0,8},{12,4},{16,24},{28,20},{32,40},{44,36},{48,56},{60,52},{64,7... | collective-permute-start | bytes 1597448 | tf_op jit(solution)/shard_map/ppermute | solution.py:271
  11.8 16.6 %collective-permute-start = (bf16[1040,256]{1,0:T(8,128)(2,1)S(1)}, bf16[1040,256]{1,0:T(8,128)(2,1)S(1)}, u32[]{:S(2)}, u32[]{:S(2)}) collective-permute-start(bf16[1040,256]{1,0:T(8,128)(2,1)S(1)} %pad_maximum_fusion.refs_6_), channel_id=1, source_target_pairs={{0,4},{4,0},{8,12},{12,8},{16,20},{20,16},{24,28},{28,24},{32,36},... | collective-permute-start | bytes 1597448 | tf_op jit(solution)/shard_map/ppermute | solution.py:271
  13.7 18.0 %collective-permute-start.2 = (bf16[1040,256]{1,0:T(8,128)(2,1)S(1)}, bf16[1040,256]{1,0:T(8,128)(2,1)}, u32[]{:S(2)}, u32[]{:S(2)}) collective-permute-start(bf16[1040,256]{1,0:T(8,128)(2,1)S(1)} %pad_maximum_fusion.refs_6_), channel_id=1, source_target_pairs={{12,28},{16,0},{28,44},{32,16},{44,60},{48,32},{60,76},{64,48},{76... | collective-permute-start | bytes 1597448 | tf_op jit(solution)/shard_map/ppermute | solution.py:271
  24.9 19.4 %collective-permute-start.5 = (bf16[1040,256]{1,0:T(8,128)(2,1)}, bf16[1040,256]{1,0:T(8,128)(2,1)S(1)}, u32[]{:S(2)}, u32[]{:S(2)}) collective-permute-start(bf16[1040,256]{1,0:T(8,128)(2,1)} %pad_maximum_fusion.1), channel_id=1, source_target_pairs={{4,12},{8,0},{20,28},{24,16},{36,44},{40,32},{52,60},{56,48},{68,7... | collective-permute-start | bytes 1597448 | tf_op jit(solution)/shard_map/ppermute | solution.py:271
  26.3 11.6 %collective-permute-start.3 = (bf16[1040,256]{1,0:T(8,128)(2,1)S(1)}, bf16[1040,256]{1,0:T(8,128)(2,1)S(1)}, u32[]{:S(2)}, u32[]{:S(2)}) collective-permute-start(bf16[1040,256]{1,0:T(8,128)(2,1)S(1)} %collective-permute-done.1.refs_10_), channel_id=1, source_target_pairs={{4,0},{8,12},{20,16},{24,28},{36,32},{40,44},{52,48},{56,60},{68,6... | collective-permute-start | bytes 1597448 | tf_op jit(solution)/shard_map/ppermute | solution.py:271
  27.6 10.3 %collective-permute-start.4 = (bf16[1040,256]{1,0:T(8,128)(2,1)S(1)}, bf16[1040,256]{1,0:T(8,128)(2,1)S(1)}, u32[]{:S(2)}, u32[]{:S(2)}) collective-permute-start(bf16[1040,256]{1,0:T(8,128)(2,1)S(1)} %collective-permute-done.1.refs_10_), channel_id=1, source_target_pairs={{4,20},{20,36},{24,8},{36,52},{40,24},{52,68},{56,40},{68,84},{72,... | collective-permute-start | bytes 1597448 | tf_op jit(solution)/shard_map/ppermute | solution.py:271
  73.5 7.6 %collective-permute-start.7 = (f32[2,4]{1,0:T(2,128)S(1)}, f32[2,4]{1,0:T(2,128)S(1)}, u32[]{:S(2)}, u32[]{:S(2)}) collective-permute-start(f32[2,4]{1,0:T(2,128)S(1)} %get-tuple-element.56), channel_id=1, source_target_pairs={{0,1},{1,2},{2,3},{4,5},{5,6},{6,7},{8,9},{9,10},{10,11},{12,13},{... | collective-permute-start | bytes 104 | tf_op jit(solution)/shard_map/ppermute | solution.py:337
  77.7 5.5 %collective-permute-start.8 = (f32[2,4]{1,0:T(2,128)S(1)}, f32[2,4]{1,0:T(2,128)S(1)}, u32[]{:S(2)}, u32[]{:S(2)}) collective-permute-start(f32[2,4]{1,0:T(2,128)S(1)} %get-tuple-element.57), channel_id=1, source_target_pairs={{1,0},{2,1},{3,2},{5,4},{6,5},{7,6},{9,8},{10,9},{11,10},{13,12},{... | collective-permute-start | bytes 104 | tf_op jit(solution)/shard_map/ppermute | solution.py:338
  79.1 7.6 %collective-permute-start.6 = (f32[2,2,8]{2,1,0:T(2,128)S(1)}, f32[2,2,8]{2,1,0:T(2,128)S(1)}, u32[]{:S(2)}, u32[]{:S(2)}) collective-permute-start(f32[2,2,8]{2,1,0:T(2,128)S(1)} %fusion.2), channel_id=1, source_target_pairs={{0,16},{16,32},{28,12},{32,48},{44,28},{48,64},{60,44},{64,80},{76... | collective-permute-start | bytes 392 | tf_op jit(solution)/shard_map/ppermute | solution.py:271

commit v2 on v1

v2 whole, which is shorter than its diff:
```python
import functools
import math

import jax
import jax.numpy as jnp
import ml_dtypes
import numpy as np
from jax import lax
from jax.experimental import pallas as pl
from jax.experimental.pallas import tpu as pltpu
from jax.sharding import PartitionSpec as P

NODE_COLS = 4
SIDE = 256
HALF = SIDE // 2
ROWS = 144
REACH = 4
SPAN = 16
GROUP = 4
NODES = 2
EXTRA = 16
BLOCK = NODES * SIDE + EXTRA
WINDOW = 6

STAGES = (
    ((), ()),
    (
        (((0, 1), (4, 5)), ((1, 2), (0, 2)), ((2, 4), (0, 1))),
        (((0, 1), (4, 5)), ((3, 4), (1, 3)), ((3, 5), (0, 1))),
    ),
    ((((2, 3), (3, 4)), ((1, 3), (3, 5))), (((2, 3), (1, 2)), ((0, 2), (2, 4)))),
)
GROUPS = 5
FOUND = 2 * GROUP * GROUPS


def pair_places(side):
    places, group = {}, 0
    for stage in STAGES:
        for pairs in stage[side]:
            for number, pair in enumerate(pairs):
                places.setdefault(pair, (group, number))
            group += 1
    return places


def stage_codes(number, side):
    codes = []
    for groups in zip(*STAGES[number]):
        both = [
            sum((a | b << 3 | (b - a - 1) << 6) << 8 * k for k, (a, b) in enumerate(pairs)) for pairs in groups
        ]
        codes.append(jnp.where(side == 0, jnp.int32(both[0]), jnp.int32(both[1])))
    return codes


def tables():
    index = np.arange(SIDE)

    def angle(phases):
        return (phases % SIDE).astype(np.float32) * np.float32(2.0 * math.pi / SIDE)

    phases = np.outer(index, index)
    cos_table = np.cos(angle(phases)).astype(ml_dtypes.bfloat16)
    sin_table = np.sin(angle(phases)).astype(ml_dtypes.bfloat16)
    right = np.concatenate([cos_table[: HALF + 1], sin_table[1:HALF]], axis=0)
    left = np.ascontiguousarray(right.T)
    row_freq = np.concatenate([np.arange(HALF + 1), -np.arange(1, HALF)])
    window = np.arange(-REACH, REACH + 1)
    fold_phase = 2.0 * math.pi * (np.outer(row_freq, window) % SIDE) / SIDE
    fold_cos, fold_sin = np.cos(fold_phase), np.sin(fold_phase)
    fold = np.zeros((GROUP, 2, SIDE, 2, 2, GROUP, SPAN), np.float32)
    for j in range(GROUP):
        for part, out, value in ((0, 0, fold_cos), (1, 0, -fold_sin), (0, 1, fold_sin), (1, 1, fold_cos)):
            high = value.astype(np.float32).astype(ml_dtypes.bfloat16).astype(np.float32)
            fold[j, part, :, out, 0, j, : window.size] = high
            fold[j, part, :, out, 1, j, : window.size] = value - high
    fold = fold.reshape(GROUP * 2 * SIDE, SIDE).astype(ml_dtypes.bfloat16)
    col_freq = np.arange(HALF + 1)
    twice = np.where((col_freq == 0) | (col_freq == HALF), 1.0, 2.0)[None, :] / SIDE
    col_phase = 2.0 * math.pi * (np.outer(window, col_freq) % SIDE) / SIDE
    close = np.zeros((2, SPAN, ROWS), np.float32)
    close[0, : window.size, : HALF + 1] = twice * np.cos(col_phase)
    close[1, : window.size, : HALF + 1] = twice * np.sin(col_phase)
    close = close.reshape(2 * SPAN, ROWS)
    high = close.astype(ml_dtypes.bfloat16)
    low = (close - high.astype(np.float32)).astype(ml_dtypes.bfloat16)
    lane, wide = np.arange(128)[:, None], np.arange(128 * GROUP)[None, :]
    spread = (lane // SPAN == wide // 128).astype(ml_dtypes.bfloat16)
    return right, left, fold, np.concatenate([high, low], axis=0), spread


def transform(patch, right, left):
    half_product = lax.dot_general(
        right, patch, (((1,), (1,)), ((), ())), preferred_element_type=jnp.float32
    ).astype(jnp.bfloat16)
    full = jnp.dot(half_product, left, preferred_element_type=jnp.float32)
    lane = lax.broadcasted_iota(jnp.int32, (HALF, HALF), 1)
    row = lax.broadcasted_iota(jnp.int32, (HALF, HALF), 0)
    first_lane, first_row = lane == 0, row == 0
    cc, sc = full[:HALF, :HALF], full[:HALF, HALF:]
    last_c, last_s = full[HALF:, :HALF], full[HALF:, HALF:]
    cs, ss = jnp.where(first_row, 0.0, last_c), jnp.where(first_row, 0.0, last_s)

    def parts(cc, sc, cs, ss, edge):
        low_sc, low_ss = jnp.where(edge, 0.0, sc), jnp.where(edge, 0.0, ss)
        return jnp.concatenate(
            [
                cc - low_ss,
                jnp.where(edge, sc, cc + ss),
                -(cs + low_sc),
                jnp.where(edge, -ss, sc - cs),
            ],
            axis=1,
        ).astype(jnp.bfloat16)

    def with_size(spectrum):
        real, imag = spectrum[:, :SIDE].astype(jnp.float32), spectrum[:, SIDE:].astype(jnp.float32)
        square = real * real + imag * imag
        return spectrum, square * lax.rsqrt(jnp.maximum(square, 1e-30))

    tail = ROWS - HALF
    keep = row[:tail] == 0
    end_c, end_s = jnp.where(keep, last_c[:tail], 0.0), jnp.where(keep, last_s[:tail], 0.0)
    none = jnp.zeros_like(end_c)
    main = with_size(parts(cc, sc, cs, ss, first_lane))
    return main, with_size(parts(end_c, end_s, none, none, first_lane[:tail]))


def stage_kernel(number, consts, blocks, state, scratch):
    right, left, fold, close, spread = consts
    specs, sizes, offs, found = state
    power, folded = scratch
    device = lax.rem(lax.axis_index("gz"), 4)
    row, side = device // 2, lax.rem(device, 2)
    codes = stage_codes(number, side)
    first_group = sum(len(stage[0]) for stage in STAGES[:number])
    near, far = 4 * row, 4 * (1 - row)
    places = ((near + side, 2 + side), (near + 1 - side, far + side, far + 1 - side), (3 - side,))[number]
    chunk = 16

    right_table, left_table = right[...], left[...]
    for block, place in zip(blocks, places):
        offs[place] = block[NODES * SIDE :, :]
        for n in range(NODES):
            patch = block[n * SIDE : (n + 1) * SIDE, :]
            main, end = transform(patch, right_table, left_table)
            specs[place * NODES + n, :HALF, :], sizes[place * NODES + n, :HALF, :] = main
            specs[place * NODES + n, HALF:, :], sizes[place * NODES + n, HALF:, :] = end

    for k, code in enumerate(codes):
        for j in range(GROUP):
            bits = jnp.right_shift(code, 8 * (j // NODES))
            a_at = (bits & 7) * NODES + j % NODES
            b_at = (jnp.right_shift(bits, 3) & 7) * NODES + j % NODES
            total = jnp.zeros((8, SIDE), jnp.float32)
            for start in range(0, ROWS, chunk):
                rows = slice(start, start + chunk)
                size = sizes[a_at, rows, :] * sizes[b_at, rows, :]
                if start == 0:
                    edge = lax.broadcasted_iota(jnp.int32, (chunk, SIDE), 0) == 0
                    size = jnp.where(edge, 0.5 * size, size)
                elif start == HALF:
                    size = 0.5 * size
                total = total + size[:8] + size[8:]
            floor = jnp.sum(total) * (2.0 / (SIDE * SIDE)) + 1e-6
            for start in range(0, ROWS, chunk):
                rows = slice(start, start + chunk)
                scale = pl.reciprocal(sizes[a_at, rows, :] * sizes[b_at, rows, :] + floor, approx=True)
                a = specs[a_at, rows, :].astype(jnp.float32)
                b = specs[b_at, rows, :].astype(jnp.float32)
                ar, ai, br, bi = a[:, :SIDE], a[:, SIDE:], b[:, :SIDE], b[:, SIDE:]
                br, bi = br * scale, bi * scale
                at = 2 * SIDE * j
                power[k, rows, at : at + SIDE] = (ar * br + ai * bi).astype(jnp.bfloat16)
                power[k, rows, at + SIDE : at + 2 * SIDE] = (ai * br - ar * bi).astype(jnp.bfloat16)
        folded[k] = jnp.dot(power[k], fold[...], preferred_element_type=jnp.float32)

    lane = lax.broadcasted_iota(jnp.int32, (SPAN, 128), 1)
    step_u = ((lane & (SPAN - 1)) - REACH).astype(jnp.float32)
    step_v = (lax.broadcasted_iota(jnp.int32, (SPAN, 128), 0) - REACH).astype(jnp.float32)
    for k, code in enumerate(codes):
        sums = folded[k]
        high = sums.astype(jnp.bfloat16)
        low = (sums - high.astype(jnp.float32)).astype(jnp.bfloat16)
        closed = jnp.dot(close[...], high, preferred_element_type=jnp.float32)
        rest = jnp.dot(close[: 2 * SPAN], low, preferred_element_type=jnp.float32)
        closed = closed[: 2 * SPAN] + closed[2 * SPAN :] + rest
        correlation = closed[:SPAN, :128] - closed[SPAN:, 128:]
        correlation = correlation + pltpu.roll(correlation, 64, axis=1)
        off_rows = []
        for pair in range(2):
            bits = jnp.right_shift(code, 8 * pair)
            own = offs[bits & 7].astype(jnp.float32)[:8, :128]
            own = jnp.where((jnp.right_shift(bits, 6) & 1) == 0, own[:4], own[4:])
            off_rows += [(own[n : n + 1], own[NODES + n : NODES + n + 1]) for n in range(NODES)]
        off_y, off_x = off_rows[3]
        for j in range(3):
            below = lane[:1] < SPAN * (j + 1)
            first = lane[:1] >= SPAN * j
            off_y = jnp.where(below & first, off_rows[j][0], off_y)
            off_x = jnp.where(below & first, off_rows[j][1], off_x)
        from_y, from_x = step_u - off_y, step_v - off_x
        inside = (jnp.abs(from_y) < 1.5) & (jnp.abs(from_x) < 1.5)
        weight = jnp.where(inside, jnp.exp(3.0 * jnp.tanh(correlation)), 0.0)
        sums = jnp.concatenate(
            [
                jnp.sum(weight, axis=0, keepdims=True),
                jnp.sum(weight * from_y, axis=0, keepdims=True),
                jnp.sum(weight * from_x, axis=0, keepdims=True),
                jnp.zeros((5, 128), jnp.float32),
            ],
            axis=0,
        )
        pieces = []
        for _ in range(3):
            pieces.append(sums.astype(jnp.bfloat16))
            sums = sums - pieces[-1].astype(jnp.float32)
        whole = jnp.dot(jnp.concatenate(pieces, axis=0), spread[...], preferred_element_type=jnp.float32)
        whole = whole[:8] + whole[8:16] + whole[16:]
        ratio_y, ratio_x = whole[1:2] / whole[0:1], whole[2:3] / whole[0:1]
        lines = []
        for j in range(GROUP):
            at = slice(128 * j, 128 * (j + 1))
            lines += [off_rows[j][0] + ratio_y[:, at], off_rows[j][1] + ratio_x[:, at]]
        found[8 * (first_group + k) : 8 * (first_group + k + 1), :] = jnp.concatenate(lines, axis=0)


def run_stage(number, consts, state, blocks):
    vmem, hbm = pl.BlockSpec(memory_space=pltpu.VMEM), pl.BlockSpec(memory_space=pltpu.HBM)
    shapes = (
        ((WINDOW * NODES, ROWS, 2 * SIDE), jnp.bfloat16),
        ((WINDOW * NODES, ROWS, SIDE), jnp.float32),
        ((WINDOW, EXTRA, SIDE), jnp.bfloat16),
        ((FOUND, 128), jnp.float32),
    )
    first = number == 0
    if first:
        consts = [pltpu.with_memory_space_constraint(c, pltpu.HBM) for c in consts]
        shapes += tuple((c.shape, c.dtype) for c in consts)
    count = len(consts)
    args = [*consts, *blocks, *state]
    fixed = count + len(blocks)

    def kernel(*refs):
        outs, scratch = refs[len(args) : len(args) + len(shapes)], refs[len(args) + len(shapes) :]
        tables_in, blocks_in = refs[:count], refs[count:fixed]
        if first:
            held, sems = outs[4:], scratch[-1]
            copies = [pltpu.make_async_copy(tables_in[k], held[k], sems.at[k]) for k in range(count)]
            for copy in copies:
                copy.start()
            for copy in copies:
                copy.wait()
            tables_in = held
        stage_kernel(number, tables_in, blocks_in, outs[:4], scratch[:2])

    groups = max(len(STAGES[number][0]), 1)
    out = pl.pallas_call(
        kernel,
        out_shape=tuple(pltpu.VMEM(shape, dtype) for shape, dtype in shapes),
        in_specs=[hbm if first else vmem] * count + [vmem] * (len(args) - count),
        out_specs=(vmem,) * len(shapes),
        input_output_aliases={fixed + k: k for k in range(len(state))},
        scratch_shapes=[
            pltpu.VMEM((groups, ROWS, 2 * SIDE * GROUP), jnp.bfloat16),
            pltpu.VMEM((groups, ROWS, SIDE), jnp.float32),
        ]
        + ([pltpu.SemaphoreType.DMA((count,))] if first else []),
        compiler_params=pltpu.CompilerParams(vmem_limit_bytes=24 * 1024 * 1024),
        cost_estimate=pl.CostEstimate(flops=1, bytes_accessed=1, transcendentals=0),
        name=f"stage{number}",
    )(*args)
    return tuple(out[:4]), tuple(out[4:])


def prepare_kernel(patches, offsets, *refs):
    blocks, sems = refs[:4], refs[4]
    device = lax.rem(lax.axis_index("gz"), 4)
    row, side = device // 2, lax.rem(device, 2)
    numbers = [2 * r + s for r in (row, 1 - row) for s in (side, 1 - side)]
    copies = []
    for k in (2, 3, 1, 0):
        copies.append(
            pltpu.make_async_copy(patches.at[numbers[k]], blocks[k].at[pl.ds(0, NODES * SIDE)], sems.at[k])
        )
        copies[-1].start()
    line = lax.broadcasted_iota(jnp.int32, (EXTRA, SIDE), 0)
    for block, number in zip(blocks, numbers):
        rows = jnp.zeros((EXTRA, SIDE), jnp.float32)
        for partner in range(2):
            for part in range(2):
                for n in range(NODES):
                    value = offsets[partner, part, NODES * number + n].astype(jnp.float32)
                    rows = jnp.where(line == 4 * partner + 2 * part + n, value, rows)
        block[NODES * SIDE :, :] = rows.astype(jnp.bfloat16)
    for copy in copies:
        copy.wait()


def prepare(patches, offsets):
    return pl.pallas_call(
        prepare_kernel,
        out_shape=tuple(pltpu.VMEM((BLOCK, SIDE), jnp.bfloat16) for _ in range(4)),
        in_specs=[pl.BlockSpec(memory_space=pltpu.HBM), pl.BlockSpec(memory_space=pltpu.SMEM)],
        out_specs=(pl.BlockSpec(memory_space=pltpu.VMEM),) * 4,
        scratch_shapes=[pltpu.SemaphoreType.DMA((4,))],
        cost_estimate=pl.CostEstimate(flops=1, bytes_accessed=1, transcendentals=0),
        name="prepare",
    )(
        pltpu.with_memory_space_constraint(patches.reshape(4, NODES * SIDE, SIDE), pltpu.HBM),
        offsets[:, :, 0, :],
    )


def finish_kernel(total, every, links, offsets, shifts, moved):
    position = lax.axis_index("gz")
    device = lax.rem(position, 4)
    lane = lax.broadcasted_iota(jnp.int32, (2, 128), 1)
    places = [pair_places(side) for side in range(2)]

    def put(held, start, row, section, partner, source):
        first = section + 2 * row
        for side in range(2):
            group, number = places[side][(first, first + partner)]
            for n in range(NODES):
                at = FOUND * source + 8 * group + 4 * number + 2 * n
                held = jnp.where(lane == start + 2 * side + n, every[2 * row + side, at : at + 2, :], held)
        return held

    def put_next(held, start, row, section, source):
        if row == 0 and section < 0:
            return put(held, start, 0, section + 4, 1, source + 2)
        if row == 1 and section > 2:
            return put(held, start, 1, section - 4, 1, source + 2)
        return put(held, start, row, section, 1, source)

    blank = jnp.zeros((2, 128), jnp.float32)
    next_all, second_all = [], []
    for section in range(-2, 5):
        held = put_next(blank, NODE_COLS, 0, section, 0)
        held = put_next(held, 2 * NODE_COLS, 1, section, 0)
        if -1 <= section < 4:
            held = put_next(held, 0, 1, section, 1)
            held = put_next(held, 3 * NODE_COLS, 0, section, 1)
        next_all.append(held)
    for section in range(4):
        held = put(blank, NODE_COLS, 0, section, 2, 0)
        if section < 2:
            held = put(held, 2 * NODE_COLS, 1, section, 2, 0)
        else:
            held = put(held, 2 * NODE_COLS, 1, section - 4, 2, 2)
        second_all.append(held)

    def pick(values):
        chosen = values[3]
        for r in range(3):
            chosen = jnp.where(device == r, values[r], chosen)
        return chosen

    behind2, behind, here, ahead = (pick(next_all[k : k + 4]) for k in range(4))
    found_next = jnp.where(position + 1 < total, here, offsets[0:2, :])
    found_second = jnp.where(position + 2 < total, pick(second_all), offsets[2:4, :])
    has_next = [
        jnp.where((position + d >= 0) & (position + d + 1 < total), 1.0, 0.0).astype(jnp.float32)
        for d in (-2, -1, 0, 1)
    ]
    pulls = [-h * f for h, f in zip(has_next, (behind2, behind, here, ahead))]
    behind_pos, positions, ahead_pos = (0.25 * (pulls[k + 1] - pulls[k]) for k in range(3))
    neighbours = blank
    for e in range(4 * NODE_COLS):
        count = jnp.sum(jnp.where(links[...] == e, 1.0, 0.0), axis=0, keepdims=True)
        neighbours = neighbours + count * positions[:, e : e + 1]
    in_plane = 0.25 * (neighbours - 4.0 * positions)
    pull = has_next[2] * (ahead_pos - positions - here)
    pull_behind = has_next[1] * (positions - behind_pos - behind)
    positions = positions + 0.5 * (in_plane + 0.5 * (pull - pull_behind))
    own = slice(NODE_COLS, 3 * NODE_COLS)
    for part in range(2):
        shifts[0, part] = found_next[part : part + 1, own]
        shifts[1, part] = found_second[part : part + 1, own]
        moved[part] = positions[part : part + 1, own]


def finish(every, links, offsets, total):
    vmem = pl.BlockSpec(memory_space=pltpu.VMEM)
    count = 2 * NODE_COLS
    return pl.pallas_call(
        functools.partial(finish_kernel, total),
        out_shape=(
            jax.ShapeDtypeStruct((2, 2, 1, count), jnp.float32),
            jax.ShapeDtypeStruct((2, 1, count), jnp.float32),
        ),
        in_specs=[vmem] * 3,
        out_specs=(vmem, vmem),
        cost_estimate=pl.CostEstimate(flops=1, bytes_accessed=1, transcendentals=0),
        name="finish",
    )(every, links, offsets)


def shards(sections, offsets, node_links):
    patches = sections[0]
    total, tiles = lax.axis_size("gz"), lax.axis_size("tile")
    tile_index = lax.axis_index("tile")

    def send(value, steps, tile_steps=(0, 0, 0, 0)):
        pairs = []
        for i in range(total):
            for t in range(tiles):
                j, to = i + steps[i % 4], t + tile_steps[i % 4]
                if 0 <= j < total and 0 <= to < tiles:
                    pairs.append((i * tiles + t, j * tiles + to))
        return lax.ppermute(value, ("gz", "tile"), pairs)

    kept, beside, across, slanted = prepare(patches, offsets)
    across_in = send(across, (2, 2, -2, -2))
    beside_in = send(beside, (1, -1, 1, -1))
    border_in = send(kept, (-4, -4, 4, 4))
    border_beside_in = send(beside, (-3, -5, 5, 3))
    slanted_in = send(slanted, (3, 1, -1, -3))
    state, consts = run_stage(0, [jnp.asarray(t) for t in tables()], (), [kept, across_in])
    state, _ = run_stage(1, consts, state, [beside_in, border_in, border_beside_in])
    state, _ = run_stage(2, consts, state, [slanted_in])
    found = state[3]

    from_tile = send(found, (0, 0, 0, 0), (-1, -1, 1, 1))
    both = jnp.concatenate([found, from_tile], axis=0)
    from_group = send(both, (4, 4, -4, -4))
    quads = [list(range(4 * g, 4 * g + 4)) for g in range(total // 4)]
    every = lax.all_gather(jnp.concatenate([both, from_group], axis=0), "gz", axis_index_groups=quads)
    count = 2 * NODE_COLS
    links = node_links[:, 0, :] - (tile_index * count - NODE_COLS)
    side_lanes = ((0, 0), (NODE_COLS, 128 - NODE_COLS - count))
    links = jnp.pad(links, side_lanes, constant_values=-1)
    own_offsets = jnp.pad(offsets.reshape(4, count).astype(jnp.float32), side_lanes)
    return finish(every, links, own_offsets, total)


def solution(mesh):
    return jax.shard_map(
        shards,
        mesh=mesh,
        in_specs=(P("gz", "tile", None, None), P(None, None, "gz", "tile"), P(None, "gz", "tile")),
        out_specs=(P(None, None, "gz", "tile"), P(None, "gz", "tile")),
        check_vma=False,
    )
```

time: 89.3 us -> 73.7 us (0.83)
  blocking collectives: 19.9 us -> 10.4 us
  waiting for transfers between devices: 11 us -> 18.7 us
  Pallas kernels: 18.8 us -> 11.4 us
  other arithmetic: 3.64 us -> 0.02 us
  starting transfers between devices: 31.7 us -> 29.7 us
    all_gather x1, blocking collectives: 19.9 us -> 10.4 us  [shards(): lax.all_gather(jnp.concatenate([both, from_group], axis=0), 'gz', axis_in...]
    ppermute x9 -> x7, waiting for transfers between devices: 11 us -> 18.7 us  [send(): return lax.ppermute(value, ('gz', 'tile'), pairs)]
    pallas_call x3 -> x5, Pallas kernels: 18.8 us -> 11.4 us  [the longest x3 7.74 us: run_stage(): pl.pallas_call(kernel, out_shape=tuple((pltpu.VMEM(shape, dtype) for shap...]
    ppermute x9 -> x7, starting transfers between devices: 31.7 us -> 29.7 us  [send(): return lax.ppermute(value, ('gz', 'tile'), pairs)]
    pad x0 -> x2, local copies, waits for them, and re-layouts: none -> 1.31 us  [the longest x1 0.66 us: shards(): links = jnp.pad(links, side_lanes, constant_values=-1)]
    squeeze x3 -> x0, local copies, waits for them, and re-layouts: 1.3 us -> none  [the longest x1 1.27 us: block(): lax.dynamic_index_in_dim(flat, row, 0, keepdims=False)]
    concatenate x3 -> x2, other arithmetic: 0.95 us -> 0.01 us  [the longest x1 0.01 us: shards(): jnp.concatenate([both, from_group], axis=0)]
  transfers between devices with their start and end apart: 9 -> 7, of which waited for: 4 -> 5; matrix products, arithmetic and copies ran while one was open for 1% -> 2% of each run, Pallas kernels for 12% -> 8%
where the time goes in v2:
time: 73.7 us; the launch traced here: 72.4 us
  starting transfers between devices  29.7 us (40%)
  waiting for transfers between devices  18.7 us (25%)
  Pallas kernels  11.4 us (15%)
  blocking collectives  10.4 us (14%)
  local copies, waits for them, and re-layouts  1.32 us (2%)
  between operations  0.77 us (1%)
    ppermute x7, starting transfers between devices, send(): return lax.ppermute(value, ('gz', 'tile'), pairs)  29.7 us
    ppermute x7, waiting for transfers between devices, send(): return lax.ppermute(value, ('gz', 'tile'), pairs)  18.7 us
    all_gather x1, blocking collectives, shards(): lax.all_gather(jnp.concatenate([both, from_group], axis=0), 'gz', axis_in...  10.4 us
    pallas_call x3, Pallas kernels, run_stage(): pl.pallas_call(kernel, out_shape=tuple((pltpu.VMEM(shape, dtype) for shap...  7.74 us
    pallas_call x1, Pallas kernels, prepare(): pl.pallas_call(prepare_kernel, out_shape=tuple((pltpu.VMEM((BLOCK, SIDE),...  1.94 us
    pallas_call x1, Pallas kernels, finish(): pl.pallas_call(functools.partial(finish_kernel, total), out_shape=(jax.Sh...  1.73 us
  transfers between devices with their start and end apart: 7, of which 5 were waited for; matrix products, arithmetic and copies ran while one was open for 2% of the time, Pallas kernels for 8%

profile of v2, /device:TPU:6, one launch (start us, length us, event | category | flops | bytes accessed | tf_op | source)
XLA Modules:
  0.0 72.4 jit_solution(17508529733482342597)
XLA Ops:
  0.6 1.9 %prepare.1 = (bf16[528,256]{1,0:T(8,128)(2,1)S(1)}, bf16[528,256]{1,0:T(8,128)(2,1)S(1)}, bf16[528,256]{1,0:T(8,128)(2,1)S(1)}, bf16[528,256]{1,0:T(8,128)(2,1)S(1)}) custom-call(bf16[4,512,256]{2,1,0:T(8,128)(2,1)} %bitcast.6, s32[2,2,8]{2,1,0:T(2,128)} %bitcast.7), custom_call_target="tpu_custom_call" | custom-call | flops 1 | bytes 1 | tf_op jit(solution)/shard_map/prepare/pallas_call | solution.py:302
  2.6 7.7 %collective-permute-start = (bf16[528,256]{1,0:T(8,128)(2,1)S(1)}, bf16[528,256]{1,0:T(8,128)(2,1)S(1)}, u32[]{:S(2)}, u32[]{:S(2)}) collective-permute-start(bf16[528,256]{1,0:T(8,128)(2,1)S(1)} %get-tuple-element.21), channel_id=1, source_target_pairs={{0,8},{1,9},{2,10},{3,11},{4,12},{5,13},{6,14},{7,15},{8,0},{9,1},... | collective-permute-start | bytes 811016 | tf_op jit(solution)/shard_map/ppermute | solution.py:413
  10.3 1.9 %collective-permute-start.2 = (bf16[528,256]{1,0:T(8,128)(2,1)S(1)}, bf16[528,256]{1,0:T(8,128)(2,1)S(1)}, u32[]{:S(2)}, u32[]{:S(2)}) collective-permute-start(bf16[528,256]{1,0:T(8,128)(2,1)S(1)} %get-tuple-element.28), channel_id=1, source_target_pairs={{0,4},{1,5},{2,6},{3,7},{4,0},{5,1},{6,2},{7,3},{8,12},{9,13},{10,... | collective-permute-start | bytes 811016 | tf_op jit(solution)/shard_map/ppermute | solution.py:413
  12.2 11.2 %collective-permute-start.3 = (bf16[528,256]{1,0:T(8,128)(2,1)S(1)}, bf16[528,256]{1,0:T(8,128)(2,1)S(1)}, u32[]{:S(2)}, u32[]{:S(2)}) collective-permute-start(bf16[528,256]{1,0:T(8,128)(2,1)S(1)} %get-tuple-element.20.refs_5_), channel_id=1, source_target_pairs={{8,24},{9,25},{10,26},{11,27},{12,28},{13,29},{14,30},{15,31},{16,... | collective-permute-start | bytes 811016 | tf_op jit(solution)/shard_map/ppermute | solution.py:413
  23.5 2.3 %collective-permute-start.4 = (bf16[528,256]{1,0:T(8,128)(2,1)S(1)}, bf16[528,256]{1,0:T(8,128)(2,1)S(1)}, u32[]{:S(2)}, u32[]{:S(2)}) collective-permute-start(bf16[528,256]{1,0:T(8,128)(2,1)S(1)} %get-tuple-element.28), channel_id=1, source_target_pairs={{8,28},{9,29},{10,30},{11,31},{12,24},{13,25},{14,26},{15,27},{16,... | collective-permute-start | bytes 811016 | tf_op jit(solution)/shard_map/ppermute | solution.py:413
  25.8 1.9 %collective-permute-start.1 = (bf16[528,256]{1,0:T(8,128)(2,1)S(1)}, bf16[528,256]{1,0:T(8,128)(2,1)S(1)}, u32[]{:S(2)}, u32[]{:S(2)}) collective-permute-start(bf16[528,256]{1,0:T(8,128)(2,1)S(1)} %get-tuple-element.27), channel_id=1, source_target_pairs={{0,12},{1,13},{2,14},{3,15},{4,8},{5,9},{6,10},{7,11},{8,4},{9,5},... | collective-permute-start | bytes 811016 | tf_op jit(solution)/shard_map/ppermute | solution.py:413
  27.7 0.0 collective-permute-done.refs_6_
  27.7 2.2 %stage0.1 = (bf16[12,144,512]{2,1,0:T(8,128)(2,1)S(1)}, f32[12,144,256]{2,1,0:T(8,128)S(1)}, bf16[6,16,256]{2,1,0:T(8,128)(2,1)S(1)}, f32[40,128]{1,0:T(8,128)S(...) custom-call(bf16[256,256]{1,0:T(8,128)(2,1)} %constant.24.clone.refs, ...), custom_call_target="tpu_custom_call" | custom-call | flops 1 | bytes 1 | tf_op jit(solution)/shard_map/stage0/pallas_call | solution.py:259
  29.9 0.0 collective-permute-done.2.refs_5_
  29.9 0.3 collective-permute-done.3.refs_6_
  30.2 5.4 %collective-permute-done.4.refs_7_ = bf16[528,256]{1,0:T(8,128)(2,1)S(1)} collective-permute-done((bf16[528,256]{1,0:T(8,128)(2,1)S(1)}, bf16[528,256]{1,0:T(8,128)(2,1)S(1)}, u32[]{:S(2)}, u32[]{:S(2)}) %collective-permute-start.4) | collective-permute-done | bytes 270368 | tf_op jit(solution)/shard_map/ppermute | solution.py:413
  35.6 3.3 %stage1.1 = (bf16[12,144,512]{2,1,0:T(8,128)(2,1)S(1)}, f32[12,144,256]{2,1,0:T(8,128)S(1)}, bf16[6,16,256]{2,1,0:T(8,128)(2,1)S(1)}, f32[40,128]{1,0:T(8,128)S(1)}) custom-call(bf16[256,256]{1,0:T(8,128)(2,1)S(1)} %get-tuple-element.22.refs_0_, ...), custom_call_target="tpu_custom_call", output_to_operand_aliasing={{0}: (8, {}), {1}: (9, {}), {2}: (10, {}), {3}: (11, {})} | custom-call | flops 1 | bytes 1 | tf_op jit(solution)/shard_map/stage1/pallas_call | solution.py:259
  38.9 2.9 %collective-permute-done.1.refs_5_ = bf16[528,256]{1,0:T(8,128)(2,1)S(1)} collective-permute-done((bf16[528,256]{1,0:T(8,128)(2,1)S(1)}, bf16[528,256]{1,0:T(8,128)(2,1)S(1)}, u32[]{:S(2)}, u32[]{:S(2)}) %collective-permute-start.1) | collective-permute-done | bytes 270368 | tf_op jit(solution)/shard_map/ppermute | solution.py:413
  41.8 2.3 %stage2.1 = (bf16[12,144,512]{2,1,0:T(8,128)(2,1)S(1)}, f32[12,144,256]{2,1,0:T(8,128)S(1)}, bf16[6,16,256]{2,1,0:T(8,128)(2,1)S(1)}, f32[40,128]{1,0:T(8,128)S(1)}) custom-call(bf16[256,256]{1,0:T(8,128)(2,1)S(1)} %get-tuple-element.22.refs_0_, ...), custom_call_target="tpu_custom_call", output_to_operand_aliasing={{0}: (6, {}), {1}: (7, {}), {2}: (8, {}), {3}: (9, {})} | custom-call | flops 1 | bytes 1 | tf_op jit(solution)/shard_map/stage2/pallas_call | solution.py:259
  44.1 1.3 %collective-permute-start.5 = (f32[40,128]{1,0:T(8,128)S(1)}, f32[40,128]{1,0:T(8,128)S(1)}, u32[]{:S(2)}, u32[]{:S(2)}) collective-permute-start(f32[40,128]{1,0:T(8,128)S(1)} %get-tuple-element.37), channel_id=1, source_target_pairs={{1,0},{2,1},{3,2},{5,4},{6,5},{7,6},{8,9},{9,10},{10,11},{12,13},{... | collective-permute-start | bytes 61448 | tf_op jit(solution)/shard_map/ppermute | solution.py:413
  45.4 6.9 %collective-permute-done.5 = f32[40,128]{1,0:T(8,128)S(1)} collective-permute-done((f32[40,128]{1,0:T(8,128)S(1)}, f32[40,128]{1,0:T(8,128)S(1)}, u32[]{:S(2)}, u32[]{:S(2)}) %collective-permute-start.5) | collective-permute-done | bytes 20512 | tf_op jit(solution)/shard_map/ppermute | solution.py:413
  52.3 3.4 %collective-permute-start.6 = (f32[80,128]{1,0:T(8,128)S(1)}, f32[80,128]{1,0:T(8,128)S(1)}, u32[]{:S(2)}, u32[]{:S(2)}) collective-permute-start(f32[80,128]{1,0:T(8,128)S(1)} %pad_maximum_fusion.1), channel_id=1, source_target_pairs={{0,16},{1,17},{2,18},{3,19},{4,20},{5,21},{6,22},{7,23},{16,32},{1... | collective-permute-start | bytes 122888 | tf_op jit(solution)/shard_map/ppermute | solution.py:413
  55.6 0.0 copy-done.1
  55.7 0.0 copy-done
  55.7 0.7 pad.8.links
  56.3 0.7 pad.9.offsets
  57.0 3.3 %collective-permute-done.6 = f32[80,128]{1,0:T(8,128)S(1)} collective-permute-done((f32[80,128]{1,0:T(8,128)S(1)}, f32[80,128]{1,0:T(8,128)S(1)}, u32[]{:S(2)}, u32[]{:S(2)}) %collective-permute-start.6) | collective-permute-done | bytes 40992 | tf_op jit(solution)/shard_map/ppermute | solution.py:413
  60.3 10.4 %all-gather = f32[640,128]{1,0:T(8,128)} all-gather(f32[160,128]{1,0:T(8,128)S(1)} %pad_maximum_fusion), channel_id=2, replica_groups={{0,4,8,12},{16,20,24,28},{32,36,40,44},{48,52,56,60},{64,68,72,76},{80,..., dimensions={0}, use_global_device_ids=true | all-gather | bytes 409600 | tf_op jit(solution)/shard_map/all_gather | solution.py:430
  70.7 1.7 %finish.1 = (f32[2,2,1,8]{3,2,1,0:T(1,128)}, f32[2,1,8]{2,1,0:T(1,128)}) custom-call(f32[4,160,128]{2,1,0:T(8,128)} %bitcast.5, s32[4,128]{1,0:T(4,128)} %pad.8.links, f32[4,128]{1,0:T(4,128)} %pad.9.offsets), custom_call_target="tpu_custom_call" | custom-call | flops 1 | bytes 1 | tf_op jit(solution)/shard_map/finish/pallas_call | solution.py:388
  (6 shorter events, 0.0 us)
Async XLA Ops:
  2.6 25.1 %collective-permute-start = (bf16[528,256]{1,0:T(8,128)(2,1)S(1)}, bf16[528,256]{1,0:T(8,128)(2,1)S(1)}, u32[]{:S(2)}, u32[]{:S(2)}) collective-permute-start(bf16[528,256]{1,0:T(8,128)(2,1)S(1)} %get-tuple-element.21), channel_id=1, source_target_pairs={{0,8},{1,9},{2,10},{3,11},{4,12},{5,13},{6,14},{7,15},{8,0},{9,1},... | collective-permute-start | bytes 811016 | tf_op jit(solution)/shard_map/ppermute | solution.py:413
  10.3 19.6 %collective-permute-start.2 = (bf16[528,256]{1,0:T(8,128)(2,1)S(1)}, bf16[528,256]{1,0:T(8,128)(2,1)S(1)}, u32[]{:S(2)}, u32[]{:S(2)}) collective-permute-start(bf16[528,256]{1,0:T(8,128)(2,1)S(1)} %get-tuple-element.28), channel_id=1, source_target_pairs={{0,4},{1,5},{2,6},{3,7},{4,0},{5,1},{6,2},{7,3},{8,12},{9,13},{10,... | collective-permute-start | bytes 811016 | tf_op jit(solution)/shard_map/ppermute | solution.py:413
  12.2 18.0 %collective-permute-start.3 = (bf16[528,256]{1,0:T(8,128)(2,1)S(1)}, bf16[528,256]{1,0:T(8,128)(2,1)S(1)}, u32[]{:S(2)}, u32[]{:S(2)}) collective-permute-start(bf16[528,256]{1,0:T(8,128)(2,1)S(1)} %get-tuple-element.20.refs_5_), channel_id=1, source_target_pairs={{8,24},{9,25},{10,26},{11,27},{12,28},{13,29},{14,30},{15,31},{16,... | collective-permute-start | bytes 811016 | tf_op jit(solution)/shard_map/ppermute | solution.py:413
  23.5 12.2 %collective-permute-start.4 = (bf16[528,256]{1,0:T(8,128)(2,1)S(1)}, bf16[528,256]{1,0:T(8,128)(2,1)S(1)}, u32[]{:S(2)}, u32[]{:S(2)}) collective-permute-start(bf16[528,256]{1,0:T(8,128)(2,1)S(1)} %get-tuple-element.28), channel_id=1, source_target_pairs={{8,28},{9,29},{10,30},{11,31},{12,24},{13,25},{14,26},{15,27},{16,... | collective-permute-start | bytes 811016 | tf_op jit(solution)/shard_map/ppermute | solution.py:413
  25.8 16.0 %collective-permute-start.1 = (bf16[528,256]{1,0:T(8,128)(2,1)S(1)}, bf16[528,256]{1,0:T(8,128)(2,1)S(1)}, u32[]{:S(2)}, u32[]{:S(2)}) collective-permute-start(bf16[528,256]{1,0:T(8,128)(2,1)S(1)} %get-tuple-element.27), channel_id=1, source_target_pairs={{0,12},{1,13},{2,14},{3,15},{4,8},{5,9},{6,10},{7,11},{8,4},{9,5},... | collective-permute-start | bytes 811016 | tf_op jit(solution)/shard_map/ppermute | solution.py:413
  41.8 13.8 %copy-start.1 = (s32[4,1,8]{2,1,0:T(1,128)S(1)}, s32[4,1,8]{2,1,0:T(1,128)}, u32[]{:S(2)}) copy-start(s32[4,1,8]{2,1,0:T(1,128)} %param.10) | copy-start | bytes 388
  41.8 13.8 %copy-start = (s32[2,2,1,8]{3,2,1,0:T(1,128)S(1)}, s32[2,2,1,8]{3,2,1,0:T(1,128)}, u32[]{:S(2)}) copy-start(s32[2,2,1,8]{3,2,1,0:T(1,128)} %param.9) | copy-start | bytes 388
  44.1 8.2 %collective-permute-start.5 = (f32[40,128]{1,0:T(8,128)S(1)}, f32[40,128]{1,0:T(8,128)S(1)}, u32[]{:S(2)}, u32[]{:S(2)}) collective-permute-start(f32[40,128]{1,0:T(8,128)S(1)} %get-tuple-element.37), channel_id=1, source_target_pairs={{1,0},{2,1},{3,2},{5,4},{6,5},{7,6},{8,9},{9,10},{10,11},{12,13},{... | collective-permute-start | bytes 61448 | tf_op jit(solution)/shard_map/ppermute | solution.py:413
  52.3 8.0 %collective-permute-start.6 = (f32[80,128]{1,0:T(8,128)S(1)}, f32[80,128]{1,0:T(8,128)S(1)}, u32[]{:S(2)}, u32[]{:S(2)}) collective-permute-start(f32[80,128]{1,0:T(8,128)S(1)} %pad_maximum_fusion.1), channel_id=1, source_target_pairs={{0,16},{1,17},{2,18},{3,19},{4,20},{5,21},{6,22},{7,23},{16,32},{1... | collective-permute-start | bytes 122888 | tf_op jit(solution)/shard_map/ppermute | solution.py:413

commit v3 on v2

--- a/solution.py
+++ b/solution.py
@@ -20,6 +20,8 @@
 NODES = 2
 EXTRA = 16
 BLOCK = NODES * SIDE + EXTRA
+BORDER = BLOCK + 16
+LONG = BLOCK + 32
 WINDOW = 6
 
 STAGES = (
@@ -31,7 +33,7 @@
     ((((2, 3), (3, 4)), ((1, 3), (3, 5))), (((2, 3), (1, 2)), ((0, 2), (2, 4)))),
 )
 GROUPS = 5
-FOUND = 2 * GROUP * GROUPS
+FOUND = 2 * GROUP
 
 
 def pair_places(side):
@@ -131,7 +133,7 @@
     right, left, fold, close, spread = consts
     specs, sizes, offs, found = state
     power, folded = scratch
-    device = lax.rem(lax.axis_index("gz"), 4)
+    device = lax.axis_index("member")
     row, side = device // 2, lax.rem(device, 2)
     codes = stage_codes(number, side)
     first_group = sum(len(stage[0]) for stage in STAGES[:number])
@@ -139,9 +141,11 @@
     places = ((near + side, 2 + side), (near + 1 - side, far + side, far + 1 - side), (3 - side,))[number]
     chunk = 16
 
+    if number == 0:
+        found[...] = jnp.zeros_like(found)
     right_table, left_table = right[...], left[...]
     for block, place in zip(blocks, places):
-        offs[place] = block[NODES * SIDE :, :]
+        offs[place] = block[NODES * SIDE : BLOCK, :]
         for n in range(NODES):
             patch = block[n * SIDE : (n + 1) * SIDE, :]
             main, end = transform(patch, right_table, left_table)
@@ -223,7 +227,7 @@
         for j in range(GROUP):
             at = slice(128 * j, 128 * (j + 1))
             lines += [off_rows[j][0] + ratio_y[:, at], off_rows[j][1] + ratio_x[:, at]]
-        found[8 * (first_group + k) : 8 * (first_group + k + 1), :] = jnp.concatenate(lines, axis=0)
+        found[...] = jnp.where(lane[:FOUND] == first_group + k, jnp.concatenate(lines, axis=0), found[...])
 
 
 def run_stage(number, consts, state, blocks):
@@ -250,10 +254,13 @@
             copies = [pltpu.make_async_copy(tables_in[k], held[k], sems.at[k]) for k in range(count)]
             for copy in copies:
                 copy.start()
-            for copy in copies:
+            for copy in copies[:2]:
                 copy.wait()
             tables_in = held
         stage_kernel(number, tables_in, blocks_in, outs[:4], scratch[:2])
+        if first:
+            for copy in copies[2:]:
+                copy.wait()
 
     groups = max(len(STAGES[number][0]), 1)
     out = pl.pallas_call(
@@ -275,12 +282,13 @@
 
 
 def prepare_kernel(patches, offsets, *refs):
-    blocks, sems = refs[:4], refs[4]
-    device = lax.rem(lax.axis_index("gz"), 4)
+    blocks, sems = refs[:5], refs[5]
+    device = lax.axis_index("member")
     row, side = device // 2, lax.rem(device, 2)
     numbers = [2 * r + s for r in (row, 1 - row) for s in (side, 1 - side)]
+    numbers.append(numbers[1])
     copies = []
-    for k in (2, 3, 1, 0):
+    for k in (2, 3, 0, 1, 4):
         copies.append(
             pltpu.make_async_copy(patches.at[numbers[k]], blocks[k].at[pl.ds(0, NODES * SIDE)], sems.at[k])
         )
@@ -291,9 +299,11 @@
         for partner in range(2):
             for part in range(2):
                 for n in range(NODES):
-                    value = offsets[partner, part, NODES * number + n].astype(jnp.float32)
+                    value = offsets[partner, part, 0, NODES * number + n].astype(jnp.float32)
                     rows = jnp.where(line == 4 * partner + 2 * part + n, value, rows)
-        block[NODES * SIDE :, :] = rows.astype(jnp.bfloat16)
+        block[NODES * SIDE : BLOCK, :] = rows.astype(jnp.bfloat16)
+    for block in blocks[:4]:
+        block[BLOCK:, :] = jnp.zeros((block.shape[0] - BLOCK, SIDE), jnp.bfloat16)
     for copy in copies:
         copy.wait()
 
@@ -301,39 +311,55 @@
 def prepare(patches, offsets):
     return pl.pallas_call(
         prepare_kernel,
-        out_shape=tuple(pltpu.VMEM((BLOCK, SIDE), jnp.bfloat16) for _ in range(4)),
+        out_shape=tuple(pltpu.VMEM((rows, SIDE), jnp.bfloat16) for rows in (BORDER, BORDER, LONG, LONG, BLOCK)),
         in_specs=[pl.BlockSpec(memory_space=pltpu.HBM), pl.BlockSpec(memory_space=pltpu.SMEM)],
-        out_specs=(pl.BlockSpec(memory_space=pltpu.VMEM),) * 4,
-        scratch_shapes=[pltpu.SemaphoreType.DMA((4,))],
+        out_specs=(pl.BlockSpec(memory_space=pltpu.VMEM),) * 5,
+        scratch_shapes=[pltpu.SemaphoreType.DMA((5,))],
         cost_estimate=pl.CostEstimate(flops=1, bytes_accessed=1, transcendentals=0),
         name="prepare",
     )(
         pltpu.with_memory_space_constraint(patches.reshape(4, NODES * SIDE, SIDE), pltpu.HBM),
-        offsets[:, :, 0, :],
+        offsets,
     )
 
 
-def finish_kernel(total, every, links, offsets, shifts, moved):
-    position = lax.axis_index("gz")
-    device = lax.rem(position, 4)
+def finish_kernel(total, every, node_links, node_offsets, shifts, moved, links, offsets):
+    device, tile = lax.axis_index("member"), lax.axis_index("tile")
+    position = 4 * lax.axis_index("group") + device
     lane = lax.broadcasted_iota(jnp.int32, (2, 128), 1)
+    own = slice(NODE_COLS, 3 * NODE_COLS)
+    tiles = lax.axis_size("tile")
+    links[...] = jnp.full_like(links, -1)
+    offsets[...] = jnp.zeros_like(offsets)
+    for k in range(4):
+        links[k : k + 1, own] = node_links[k] - (tile * 2 * NODE_COLS - NODE_COLS)
+        offsets[k : k + 1, own] = node_offsets[k // 2, k % 2].astype(jnp.float32)
     places = [pair_places(side) for side in range(2)]
-
-    def put(held, start, row, section, partner, source):
+    spread = {}
+    near_tiles = {0: tile, -1: jnp.maximum(tile - 1, 0), 1: jnp.minimum(tile + 1, tiles - 1)}
+
+    def shifts_of(member, step, column):
+        if (member, step, column) not in spread:
+            values = every[member * tiles + near_tiles[step]][:, column : column + 1]
+            spread[member, step, column] = jnp.broadcast_to(values, (FOUND, 128))
+        return spread[member, step, column]
+
+    def put(held, start, row, section, partner, step, source=0):
         first = section + 2 * row
         for side in range(2):
             group, number = places[side][(first, first + partner)]
             for n in range(NODES):
-                at = FOUND * source + 8 * group + 4 * number + 2 * n
-                held = jnp.where(lane == start + 2 * side + n, every[2 * row + side, at : at + 2, :], held)
+                at = 4 * number + 2 * n
+                value = shifts_of(2 * row + side, step, GROUPS * source + group)[at : at + 2]
+                held = jnp.where(lane == start + 2 * side + n, value, held)
         return held
 
-    def put_next(held, start, row, section, source):
+    def put_next(held, start, row, section, step):
         if row == 0 and section < 0:
-            return put(held, start, 0, section + 4, 1, source + 2)
+            return put(held, start, 0, section + 4, 1, step, 1)
         if row == 1 and section > 2:
-            return put(held, start, 1, section - 4, 1, source + 2)
-        return put(held, start, row, section, 1, source)
+            return put(held, start, 1, section - 4, 1, step, 1)
+        return put(held, start, row, section, 1, step)
 
     blank = jnp.zeros((2, 128), jnp.float32)
     next_all, second_all = [], []
@@ -341,7 +367,7 @@
         held = put_next(blank, NODE_COLS, 0, section, 0)
         held = put_next(held, 2 * NODE_COLS, 1, section, 0)
         if -1 <= section < 4:
-            held = put_next(held, 0, 1, section, 1)
+            held = put_next(held, 0, 1, section, -1)
             held = put_next(held, 3 * NODE_COLS, 0, section, 1)
         next_all.append(held)
     for section in range(4):
@@ -349,7 +375,7 @@
         if section < 2:
             held = put(held, 2 * NODE_COLS, 1, section, 2, 0)
         else:
-            held = put(held, 2 * NODE_COLS, 1, section - 4, 2, 2)
+            held = put(held, 2 * NODE_COLS, 1, section - 4, 2, 0, 1)
         second_all.append(held)
 
     def pick(values):
@@ -369,13 +395,12 @@
     behind_pos, positions, ahead_pos = (0.25 * (pulls[k + 1] - pulls[k]) for k in range(3))
     neighbours = blank
     for e in range(4 * NODE_COLS):
-        count = jnp.sum(jnp.where(links[...] == e, 1.0, 0.0), axis=0, keepdims=True)
+        count = jnp.sum(jnp.where(links[0:4, :] == e, 1.0, 0.0), axis=0, keepdims=True)
         neighbours = neighbours + count * positions[:, e : e + 1]
     in_plane = 0.25 * (neighbours - 4.0 * positions)
     pull = has_next[2] * (ahead_pos - positions - here)
     pull_behind = has_next[1] * (positions - behind_pos - behind)
     positions = positions + 0.5 * (in_plane + 0.5 * (pull - pull_behind))
-    own = slice(NODE_COLS, 3 * NODE_COLS)
     for part in range(2):
         shifts[0, part] = found_next[part : part + 1, own]
         shifts[1, part] = found_second[part : part + 1, own]
@@ -393,6 +418,7 @@
         ),
         in_specs=[vmem] * 3,
         out_specs=(vmem, vmem),
+        scratch_shapes=[pltpu.VMEM((8, 128), jnp.int32), pltpu.VMEM((8, 128), jnp.float32)],
         cost_estimate=pl.CostEstimate(flops=1, bytes_accessed=1, transcendentals=0),
         name="finish",
     )(every, links, offsets)
@@ -400,21 +426,16 @@
 
 def shards(sections, offsets, node_links):
     patches = sections[0]
-    total, tiles = lax.axis_size("gz"), lax.axis_size("tile")
-    tile_index = lax.axis_index("tile")
-
-    def send(value, steps, tile_steps=(0, 0, 0, 0)):
-        pairs = []
-        for i in range(total):
-            for t in range(tiles):
-                j, to = i + steps[i % 4], t + tile_steps[i % 4]
-                if 0 <= j < total and 0 <= to < tiles:
-                    pairs.append((i * tiles + t, j * tiles + to))
-        return lax.ppermute(value, ("gz", "tile"), pairs)
-
-    kept, beside, across, slanted = prepare(patches, offsets)
+    groups, tiles = lax.axis_size("group"), lax.axis_size("tile")
+
+    def send(value, steps):
+        total = 4 * groups
+        pairs = [(i, i + steps[i % 4]) for i in range(total) if 0 <= i + steps[i % 4] < total]
+        return lax.ppermute(value, ("group", "member"), pairs)
+
+    kept, beside, across, slanted, beside_core = prepare(patches, offsets)
     across_in = send(across, (2, 2, -2, -2))
-    beside_in = send(beside, (1, -1, 1, -1))
+    beside_in = send(beside_core, (1, -1, 1, -1))
     border_in = send(kept, (-4, -4, 4, 4))
     border_beside_in = send(beside, (-3, -5, 5, 3))
     slanted_in = send(slanted, (3, 1, -1, -3))
@@ -423,24 +444,21 @@
     state, _ = run_stage(2, consts, state, [slanted_in])
     found = state[3]
 
-    from_tile = send(found, (0, 0, 0, 0), (-1, -1, 1, 1))
-    both = jnp.concatenate([found, from_tile], axis=0)
-    from_group = send(both, (4, 4, -4, -4))
-    quads = [list(range(4 * g, 4 * g + 4)) for g in range(total // 4)]
-    every = lax.all_gather(jnp.concatenate([both, from_group], axis=0), "gz", axis_index_groups=quads)
-    count = 2 * NODE_COLS
-    links = node_links[:, 0, :] - (tile_index * count - NODE_COLS)
-    side_lanes = ((0, 0), (NODE_COLS, 128 - NODE_COLS - count))
-    links = jnp.pad(links, side_lanes, constant_values=-1)
-    own_offsets = jnp.pad(offsets.reshape(4, count).astype(jnp.float32), side_lanes)
-    return finish(every, links, own_offsets, total)
+    rest = jnp.zeros((FOUND, 128 - 2 * GROUPS), jnp.float32)
+    near = send(found, (4, 4, -4, -4))
+    found = jnp.concatenate([found[:, :GROUPS], near[:, :GROUPS], rest], axis=1)
+    every = lax.all_to_all(jnp.broadcast_to(found[None], (4 * tiles, FOUND, 128)), ("member", "tile"), 0, 0)
+    return finish(every, node_links, offsets, 4 * groups)
 
 
 def solution(mesh):
+    sections, tiles = mesh.devices.shape
+    mesh = jax.sharding.Mesh(mesh.devices.reshape(sections // 4, 4, tiles), ("group", "member", "tile"))
+    gz = ("group", "member")
     return jax.shard_map(
         shards,
         mesh=mesh,
-        in_specs=(P("gz", "tile", None, None), P(None, None, "gz", "tile"), P(None, "gz", "tile")),
-        out_specs=(P(None, None, "gz", "tile"), P(None, "gz", "tile")),
+        in_specs=(P(gz, "tile", None, None), P(None, None, gz, "tile"), P(None, gz, "tile")),
+        out_specs=(P(None, None, gz, "tile"), P(None, gz, "tile")),
         check_vma=False,
     )

time: 73.7 us -> 66.5 us (0.902)
  waiting for transfers between devices: 18.7 us -> 12.6 us
  blocking collectives: 10.4 us -> 13.9 us
  starting transfers between devices: 29.7 us -> 27.3 us
  local copies, waits for them, and re-layouts: 1.32 us -> 0.09 us
    all_to_all x0 -> x1, blocking collectives: none -> 13.9 us  [shards(): lax.all_to_all(jnp.broadcast_to(found[None], (4 * tiles, FOUND, 128)), ('...]
    all_gather x1 -> x0, blocking collectives: 10.4 us -> none  [shards(): lax.all_gather(jnp.concatenate([both, from_group], axis=0), 'gz', axis_in...]
    ppermute x7 -> x6, waiting for transfers between devices: 18.7 us -> 12.6 us  [send(): return lax.ppermute(value, ('group', 'member'), pairs)]
    ppermute x7 -> x6, starting transfers between devices: 29.7 us -> 27.3 us  [send(): return lax.ppermute(value, ('group', 'member'), pairs)]
    pad x2 -> x0, local copies, waits for them, and re-layouts: 1.31 us -> none  [the longest x1 0.66 us: shards(): links = jnp.pad(links, side_lanes, constant_values=-1)]
  transfers between devices with their start and end apart: 7 -> 6, of which waited for: 5 -> 3; matrix products, arithmetic and copies ran while one was open for 2% -> 0% of each run, Pallas kernels for 8% -> 8%
where the time goes in v3:
time: 66.5 us; the launch traced here: 65.8 us
  starting transfers between devices  27.3 us (41%)
  blocking collectives  13.9 us (21%)
  waiting for transfers between devices  12.6 us (19%)
  Pallas kernels  11.2 us (17%)
  between operations  0.74 us (1%)
    ppermute x6, starting transfers between devices, send(): return lax.ppermute(value, ('group', 'member'), pairs)  27.3 us
    all_to_all x1, blocking collectives, shards(): lax.all_to_all(jnp.broadcast_to(found[None], (4 * tiles, FOUND, 128)), ('...  13.9 us
    ppermute x6, waiting for transfers between devices, send(): return lax.ppermute(value, ('group', 'member'), pairs)  12.6 us
    pallas_call x3, Pallas kernels, run_stage(): pl.pallas_call(kernel, out_shape=tuple((pltpu.VMEM(shape, dtype) for shap...  7.45 us
    pallas_call x1, Pallas kernels, prepare(): pl.pallas_call(prepare_kernel, out_shape=tuple((pltpu.VMEM((rows, SIDE),...  2.03 us
    pallas_call x1, Pallas kernels, finish(): pl.pallas_call(functools.partial(finish_kernel, total), out_shape=(jax.Sh...  1.75 us
  transfers between devices with their start and end apart: 6, of which 3 were waited for; matrix products, arithmetic and copies ran while one was open for 0% of the time, Pallas kernels for 8%

profile of v3, /device:TPU:6, one launch (start us, length us, event | category | flops | bytes accessed | tf_op | source)
XLA Modules:
  0.0 65.8 jit_solution(46236843163927657)
XLA Ops:
  0.6 2.0 %prepare.1 = (bf16[544,256]{1,0:T(8,128)(2,1)S(1)}, bf16[544,256]{1,0:T(8,128)(2,1)S(1)}, bf16[560,256]{1,0:T(8,128)(2,1)S(1)}, bf16[560,256]{1,0:T(8,128)(2,1)S(1)}, bf16[528,256]{1,0:T(8,128)(2,1)S(1)}) custom-call(bf16[4,512,256]{2,1,0:T(8,128)(2,1)} %bitcast.4, s32[2,2,1,8]{3,2,1,0:T(1,128)} %node_offsets.1), custom_call_target="tpu_custom_call" | custom-call | flops 1 | bytes 1 | tf_op jit(solution)/shard_map/prepare/pallas_call | solution.py:312
  2.7 7.7 %collective-permute-start = (bf16[560,256]{1,0:T(8,128)(2,1)S(1)}, bf16[560,256]{1,0:T(8,128)(2,1)S(1)}, u32[]{:S(2)}, u32[]{:S(2)}) collective-permute-start(bf16[560,256]{1,0:T(8,128)(2,1)S(1)} %get-tuple-element.22), channel_id=1, source_target_pairs={{0,8},{4,12},{8,0},{12,4},{16,24},{20,28},{24,16},{28,20},{32,40},... | collective-permute-start | bytes 860168 | tf_op jit(solution)/shard_map/ppermute | solution.py:434
  10.4 1.9 %collective-permute-start.1 = (bf16[560,256]{1,0:T(8,128)(2,1)S(1)}, bf16[560,256]{1,0:T(8,128)(2,1)S(1)}, u32[]{:S(2)}, u32[]{:S(2)}) collective-permute-start(bf16[560,256]{1,0:T(8,128)(2,1)S(1)} %get-tuple-element.28), channel_id=1, source_target_pairs={{0,12},{4,8},{8,4},{12,0},{16,28},{20,24},{24,20},{28,16},{32,44},... | collective-permute-start | bytes 860168 | tf_op jit(solution)/shard_map/ppermute | solution.py:434
  12.3 11.2 %collective-permute-start.3 = (bf16[544,256]{1,0:T(8,128)(2,1)S(1)}, bf16[544,256]{1,0:T(8,128)(2,1)S(1)}, u32[]{:S(2)}, u32[]{:S(2)}) collective-permute-start(bf16[544,256]{1,0:T(8,128)(2,1)S(1)} %get-tuple-element.21.refs_5_), channel_id=1, source_target_pairs={{8,24},{12,28},{16,0},{20,4},{24,40},{28,44},{32,16},{36,20},{40,5... | collective-permute-start | bytes 835592 | tf_op jit(solution)/shard_map/ppermute | solution.py:434
  23.6 2.0 %collective-permute-start.4 = (bf16[544,256]{1,0:T(8,128)(2,1)S(1)}, bf16[544,256]{1,0:T(8,128)(2,1)S(1)}, u32[]{:S(2)}, u32[]{:S(2)}) collective-permute-start(bf16[544,256]{1,0:T(8,128)(2,1)S(1)} %get-tuple-element.30), channel_id=1, source_target_pairs={{8,28},{12,24},{16,4},{20,0},{24,44},{28,40},{32,20},{36,16},{40,6... | collective-permute-start | bytes 835592 | tf_op jit(solution)/shard_map/ppermute | solution.py:434
  25.6 2.5 %collective-permute-start.2 = (bf16[528,256]{1,0:T(8,128)(2,1)S(1)}, bf16[528,256]{1,0:T(8,128)(2,1)S(1)}, u32[]{:S(2)}, u32[]{:S(2)}) collective-permute-start(bf16[528,256]{1,0:T(8,128)(2,1)S(1)} %get-tuple-element.29), channel_id=1, source_target_pairs={{0,4},{4,0},{8,12},{12,8},{16,20},{20,16},{24,28},{28,24},{32,36},... | collective-permute-start | bytes 811016 | tf_op jit(solution)/shard_map/ppermute | solution.py:434
  28.1 0.0 collective-permute-done.refs_6_
  28.1 1.8 %stage0.1 = (bf16[12,144,512]{2,1,0:T(8,128)(2,1)S(1)}, f32[12,144,256]{2,1,0:T(8,128)S(1)}, bf16[6,16,256]{2,1,0:T(8,128)(2,1)S(1)}, f32[8,128]{1,0:T(8,128)S(1...) custom-call(bf16[256,256]{1,0:T(8,128)(2,1)} %constant.12.clone.refs, ...), custom_call_target="tpu_custom_call" | custom-call | flops 1 | bytes 1 | tf_op jit(solution)/shard_map/stage0/pallas_call | solution.py:266
  29.9 0.0 collective-permute-done.2.refs_5_
  29.9 0.6 collective-permute-done.3.refs_6_
  30.5 5.2 %collective-permute-done.4.refs_7_ = bf16[544,256]{1,0:T(8,128)(2,1)S(1)} collective-permute-done((bf16[544,256]{1,0:T(8,128)(2,1)S(1)}, bf16[544,256]{1,0:T(8,128)(2,1)S(1)}, u32[]{:S(2)}, u32[]{:S(2)}) %collective-permute-start.4) | collective-permute-done | bytes 278560 | tf_op jit(solution)/shard_map/ppermute | solution.py:434
  35.8 3.3 %stage1.1 = (bf16[12,144,512]{2,1,0:T(8,128)(2,1)S(1)}, f32[12,144,256]{2,1,0:T(8,128)S(1)}, bf16[6,16,256]{2,1,0:T(8,128)(2,1)S(1)}, f32[8,128]{1,0:T(8,128)S(1)}) custom-call(bf16[256,256]{1,0:T(8,128)(2,1)S(1)} %get-tuple-element.23.refs_0_, ...), custom_call_target="tpu_custom_call", output_to_operand_aliasing={{0}: (8, {}), {1}: (9, {}), {2}: (10, {}), {3}: (11, {})} | custom-call | flops 1 | bytes 1 | tf_op jit(solution)/shard_map/stage1/pallas_call | solution.py:266
  39.1 0.0 collective-permute-done.1.refs_5_
  39.1 2.3 %stage2.1 = (bf16[12,144,512]{2,1,0:T(8,128)(2,1)S(1)}, f32[12,144,256]{2,1,0:T(8,128)S(1)}, bf16[6,16,256]{2,1,0:T(8,128)(2,1)S(1)}, f32[8,128]{1,0:T(8,128)S(1)}) custom-call(bf16[256,256]{1,0:T(8,128)(2,1)S(1)} %get-tuple-element.23.refs_0_, ...), custom_call_target="tpu_custom_call", output_to_operand_aliasing={{0}: (6, {}), {1}: (7, {}), {2}: (8, {}), {3}: (9, {})} | custom-call | flops 1 | bytes 1 | tf_op jit(solution)/shard_map/stage2/pallas_call | solution.py:266
  41.5 1.9 %collective-permute-start.5 = (f32[8,128]{1,0:T(8,128)S(1)}, f32[8,128]{1,0:T(8,128)S(1)}, u32[]{:S(2)}, u32[]{:S(2)}) collective-permute-start(f32[8,128]{1,0:T(8,128)S(1)} %get-tuple-element.39), channel_id=1, source_target_pairs={{0,16},{4,20},{16,32},{20,36},{24,8},{28,12},{32,48},{36,52},{40,2... | collective-permute-start | bytes 12296 | tf_op jit(solution)/shard_map/ppermute | solution.py:434
  43.4 0.1 pad.2.clone
  43.5 6.7 %collective-permute-done.5 = f32[8,128]{1,0:T(8,128)S(1)} collective-permute-done((f32[8,128]{1,0:T(8,128)S(1)}, f32[8,128]{1,0:T(8,128)S(1)}, u32[]{:S(2)}, u32[]{:S(2)}) %collective-permute-start.5) | collective-permute-done | bytes 4128 | tf_op jit(solution)/shard_map/ppermute | solution.py:434
  50.1 0.1 maximum_maximum_fusion
  50.2 13.9 %all_to_all.5.every = f32[16,8,128]{2,1,0:T(8,128)} all-to-all(f32[16,8,128]{2,1,0:T(8,128)S(1)} %broadcast_in_dim.10), channel_id=1, replica_groups=mesh['group'=32,'member'=4,'tile'=4] {'member','tile'}, dimensions={0} | all-to-all | bytes 131072 | tf_op jit(solution)/shard_map/all_to_all | solution.py:450
  64.1 1.7 %finish.1 = (f32[2,2,1,8]{3,2,1,0:T(1,128)}, f32[2,1,8]{2,1,0:T(1,128)}) custom-call(f32[16,8,128]{2,1,0:T(8,128)} %all_to_all.5.every, s32[4,1,8]{2,1,0:T(1,128)} %node_links.1, s32[2,2,1,8]{3,2,1,0:T(1,128)} %node_offsets.1), custom_call_target="tpu_custom_call" | custom-call | flops 1 | bytes 1 | tf_op jit(solution)/shard_map/finish/pallas_call | solution.py:413
  (2 shorter events, 0.0 us)
Async XLA Ops:
  2.7 25.4 %collective-permute-start = (bf16[560,256]{1,0:T(8,128)(2,1)S(1)}, bf16[560,256]{1,0:T(8,128)(2,1)S(1)}, u32[]{:S(2)}, u32[]{:S(2)}) collective-permute-start(bf16[560,256]{1,0:T(8,128)(2,1)S(1)} %get-tuple-element.22), channel_id=1, source_target_pairs={{0,8},{4,12},{8,0},{12,4},{16,24},{20,28},{24,16},{28,20},{32,40},... | collective-permute-start | bytes 860168 | tf_op jit(solution)/shard_map/ppermute | solution.py:434
  10.4 28.7 %collective-permute-start.1 = (bf16[560,256]{1,0:T(8,128)(2,1)S(1)}, bf16[560,256]{1,0:T(8,128)(2,1)S(1)}, u32[]{:S(2)}, u32[]{:S(2)}) collective-permute-start(bf16[560,256]{1,0:T(8,128)(2,1)S(1)} %get-tuple-element.28), channel_id=1, source_target_pairs={{0,12},{4,8},{8,4},{12,0},{16,28},{20,24},{24,20},{28,16},{32,44},... | collective-permute-start | bytes 860168 | tf_op jit(solution)/shard_map/ppermute | solution.py:434
  12.3 18.2 %collective-permute-start.3 = (bf16[544,256]{1,0:T(8,128)(2,1)S(1)}, bf16[544,256]{1,0:T(8,128)(2,1)S(1)}, u32[]{:S(2)}, u32[]{:S(2)}) collective-permute-start(bf16[544,256]{1,0:T(8,128)(2,1)S(1)} %get-tuple-element.21.refs_5_), channel_id=1, source_target_pairs={{8,24},{12,28},{16,0},{20,4},{24,40},{28,44},{32,16},{36,20},{40,5... | collective-permute-start | bytes 835592 | tf_op jit(solution)/shard_map/ppermute | solution.py:434
  23.6 12.2 %collective-permute-start.4 = (bf16[544,256]{1,0:T(8,128)(2,1)S(1)}, bf16[544,256]{1,0:T(8,128)(2,1)S(1)}, u32[]{:S(2)}, u32[]{:S(2)}) collective-permute-start(bf16[544,256]{1,0:T(8,128)(2,1)S(1)} %get-tuple-element.30), channel_id=1, source_target_pairs={{8,28},{12,24},{16,4},{20,0},{24,44},{28,40},{32,20},{36,16},{40,6... | collective-permute-start | bytes 835592 | tf_op jit(solution)/shard_map/ppermute | solution.py:434
  25.6 4.3 %collective-permute-start.2 = (bf16[528,256]{1,0:T(8,128)(2,1)S(1)}, bf16[528,256]{1,0:T(8,128)(2,1)S(1)}, u32[]{:S(2)}, u32[]{:S(2)}) collective-permute-start(bf16[528,256]{1,0:T(8,128)(2,1)S(1)} %get-tuple-element.29), channel_id=1, source_target_pairs={{0,4},{4,0},{8,12},{12,8},{16,20},{20,16},{24,28},{28,24},{32,36},... | collective-permute-start | bytes 811016 | tf_op jit(solution)/shard_map/ppermute | solution.py:434
  41.5 8.7 %collective-permute-start.5 = (f32[8,128]{1,0:T(8,128)S(1)}, f32[8,128]{1,0:T(8,128)S(1)}, u32[]{:S(2)}, u32[]{:S(2)}) collective-permute-start(f32[8,128]{1,0:T(8,128)S(1)} %get-tuple-element.39), channel_id=1, source_target_pairs={{0,16},{4,20},{16,32},{20,36},{24,8},{28,12},{32,48},{36,52},{40,2... | collective-permute-start | bytes 12296 | tf_op jit(solution)/shard_map/ppermute | solution.py:434

commit v4 on v3

--- a/solution.py
+++ b/solution.py
@@ -20,20 +20,17 @@
 NODES = 2
 EXTRA = 16
 BLOCK = NODES * SIDE + EXTRA
-BORDER = BLOCK + 16
-LONG = BLOCK + 32
+LONG = BLOCK + 16
 WINDOW = 6
 
 STAGES = (
     ((), ()),
-    (
-        (((0, 1), (4, 5)), ((1, 2), (0, 2)), ((2, 4), (0, 1))),
-        (((0, 1), (4, 5)), ((3, 4), (1, 3)), ((3, 5), (0, 1))),
-    ),
+    ((((0, 2), (2, 4)),), (((1, 3), (3, 5)),)),
+    ((((0, 1), (4, 5)), ((1, 2),)), (((0, 1), (4, 5)), ((3, 4),))),
     ((((2, 3), (3, 4)), ((1, 3), (3, 5))), (((2, 3), (1, 2)), ((0, 2), (2, 4)))),
 )
 GROUPS = 5
-FOUND = 2 * GROUP
+FOUND = GROUP * GROUPS
 
 
 def pair_places(side):
@@ -138,7 +135,7 @@
     codes = stage_codes(number, side)
     first_group = sum(len(stage[0]) for stage in STAGES[:number])
     near, far = 4 * row, 4 * (1 - row)
-    places = ((near + side, 2 + side), (near + 1 - side, far + side, far + 1 - side), (3 - side,))[number]
+    places = ((near + side, far + side), (2 + side,), (far + 1 - side, near + 1 - side), (3 - side,))[number]
     chunk = 16
 
     if number == 0:
@@ -153,7 +150,10 @@
             specs[place * NODES + n, HALF:, :], sizes[place * NODES + n, HALF:, :] = end
 
     for k, code in enumerate(codes):
-        for j in range(GROUP):
+        held = NODES * len(STAGES[number][0][k])
+        if held < GROUP:
+            power[k, :, 2 * SIDE * held :] = jnp.zeros((ROWS, 2 * SIDE * (GROUP - held)), jnp.bfloat16)
+        for j in range(held):
             bits = jnp.right_shift(code, 8 * (j // NODES))
             a_at = (bits & 7) * NODES + j % NODES
             b_at = (jnp.right_shift(bits, 3) & 7) * NODES + j % NODES
@@ -223,35 +223,38 @@
         whole = jnp.dot(jnp.concatenate(pieces, axis=0), spread[...], preferred_element_type=jnp.float32)
         whole = whole[:8] + whole[8:16] + whole[16:]
         ratio_y, ratio_x = whole[1:2] / whole[0:1], whole[2:3] / whole[0:1]
-        lines = []
         for j in range(GROUP):
             at = slice(128 * j, 128 * (j + 1))
-            lines += [off_rows[j][0] + ratio_y[:, at], off_rows[j][1] + ratio_x[:, at]]
-        found[...] = jnp.where(lane[:FOUND] == first_group + k, jnp.concatenate(lines, axis=0), found[...])
-
-
-def run_stage(number, consts, state, blocks):
+            both = jnp.concatenate([off_rows[j][0] + ratio_y[:, at], off_rows[j][1] + ratio_x[:, at]], axis=0)
+            found[...] = jnp.where(lane[:2] == GROUP * (first_group + k) + j, both, found[...])
+
+
+def run_stage(number, consts, state, blocks, mesh_inputs=()):
     vmem, hbm = pl.BlockSpec(memory_space=pltpu.VMEM), pl.BlockSpec(memory_space=pltpu.HBM)
     shapes = (
         ((WINDOW * NODES, ROWS, 2 * SIDE), jnp.bfloat16),
         ((WINDOW * NODES, ROWS, SIDE), jnp.float32),
         ((WINDOW, EXTRA, SIDE), jnp.bfloat16),
-        ((FOUND, 128), jnp.float32),
+        ((2, 128), jnp.float32),
     )
     first = number == 0
     if first:
         consts = [pltpu.with_memory_space_constraint(c, pltpu.HBM) for c in consts]
         shapes += tuple((c.shape, c.dtype) for c in consts)
+        shapes += (((4 * NODE_COLS, 128), jnp.float32), ((8, 128), jnp.float32))
+        mesh_inputs = [pltpu.with_memory_space_constraint(x, pltpu.HBM) for x in mesh_inputs]
     count = len(consts)
-    args = [*consts, *blocks, *state]
+    args = [*consts, *blocks, *state, *mesh_inputs]
     fixed = count + len(blocks)
 
     def kernel(*refs):
         outs, scratch = refs[len(args) : len(args) + len(shapes)], refs[len(args) + len(shapes) :]
         tables_in, blocks_in = refs[:count], refs[count:fixed]
         if first:
-            held, sems = outs[4:], scratch[-1]
-            copies = [pltpu.make_async_copy(tables_in[k], held[k], sems.at[k]) for k in range(count)]
+            held, sems = outs[4 : 4 + count], scratch[-1]
+            sources = [*tables_in, *refs[fixed : len(args)]]
+            targets = [*held, *scratch[2:4]]
+            copies = [pltpu.make_async_copy(a, b, sems.at[k]) for k, (a, b) in enumerate(zip(sources, targets))]
             for copy in copies:
                 copy.start()
             for copy in copies[:2]:
@@ -261,19 +264,23 @@
         if first:
             for copy in copies[2:]:
                 copy.wait()
+            mesh_rows(*scratch[2:4], *outs[4 + count :], scratch[4])
 
     groups = max(len(STAGES[number][0]), 1)
     out = pl.pallas_call(
         kernel,
         out_shape=tuple(pltpu.VMEM(shape, dtype) for shape, dtype in shapes),
-        in_specs=[hbm if first else vmem] * count + [vmem] * (len(args) - count),
+        in_specs=[hbm if first else vmem] * count
+        + [vmem] * (len(args) - count - len(mesh_inputs))
+        + [hbm] * len(mesh_inputs),
         out_specs=(vmem,) * len(shapes),
         input_output_aliases={fixed + k: k for k in range(len(state))},
         scratch_shapes=[
             pltpu.VMEM((groups, ROWS, 2 * SIDE * GROUP), jnp.bfloat16),
             pltpu.VMEM((groups, ROWS, SIDE), jnp.float32),
         ]
-        + ([pltpu.SemaphoreType.DMA((count,))] if first else []),
+        + [pltpu.VMEM(x.shape, x.dtype) for x in mesh_inputs]
+        + ([pltpu.VMEM((8, 128), jnp.int32), pltpu.SemaphoreType.DMA((count + 2,))] if first else []),
         compiler_params=pltpu.CompilerParams(vmem_limit_bytes=24 * 1024 * 1024),
         cost_estimate=pl.CostEstimate(flops=1, bytes_accessed=1, transcendentals=0),
         name=f"stage{number}",
@@ -281,18 +288,32 @@
     return tuple(out[:4]), tuple(out[4:])
 
 
-def prepare_kernel(patches, offsets, *refs):
-    blocks, sems = refs[:5], refs[5]
+def mesh_rows(node_links, node_offsets, counts, offsets, links):
+    own = slice(NODE_COLS, 3 * NODE_COLS)
+    links[...] = jnp.full_like(links, -1)
+    offsets[...] = jnp.zeros_like(offsets)
+    first = (lax.axis_index("tile") * 2 - 1) * NODE_COLS
+    for k in range(4):
+        links[k : k + 1, own] = node_links[k] - first
+        offsets[k : k + 1, own] = node_offsets[k // 2, k % 2].astype(jnp.float32)
+    for e in range(4 * NODE_COLS):
+        counts[e : e + 1, :] = jnp.sum(jnp.where(links[0:4, :] == e, 1.0, 0.0), axis=0, keepdims=True)
+
+
+def prepare_kernel(patches, all_offsets, *refs):
+    blocks, offsets, sems = refs[:4], refs[4], refs[5]
     device = lax.axis_index("member")
     row, side = device // 2, lax.rem(device, 2)
     numbers = [2 * r + s for r in (row, 1 - row) for s in (side, 1 - side)]
-    numbers.append(numbers[1])
     copies = []
-    for k in (2, 3, 0, 1, 4):
+    for k in (2, 3, 0, 1):
         copies.append(
             pltpu.make_async_copy(patches.at[numbers[k]], blocks[k].at[pl.ds(0, NODES * SIDE)], sems.at[k])
         )
         copies[-1].start()
+    offsets_copy = pltpu.make_async_copy(all_offsets, offsets, sems.at[4])
+    offsets_copy.start()
+    offsets_copy.wait()
     line = lax.broadcasted_iota(jnp.int32, (EXTRA, SIDE), 0)
     for block, number in zip(blocks, numbers):
         rows = jnp.zeros((EXTRA, SIDE), jnp.float32)
@@ -302,7 +323,7 @@
                     value = offsets[partner, part, 0, NODES * number + n].astype(jnp.float32)
                     rows = jnp.where(line == 4 * partner + 2 * part + n, value, rows)
         block[NODES * SIDE : BLOCK, :] = rows.astype(jnp.bfloat16)
-    for block in blocks[:4]:
+    for block in blocks[2:]:
         block[BLOCK:, :] = jnp.zeros((block.shape[0] - BLOCK, SIDE), jnp.bfloat16)
     for copy in copies:
         copy.wait()
@@ -311,29 +332,24 @@
 def prepare(patches, offsets):
     return pl.pallas_call(
         prepare_kernel,
-        out_shape=tuple(pltpu.VMEM((rows, SIDE), jnp.bfloat16) for rows in (BORDER, BORDER, LONG, LONG, BLOCK)),
-        in_specs=[pl.BlockSpec(memory_space=pltpu.HBM), pl.BlockSpec(memory_space=pltpu.SMEM)],
-        out_specs=(pl.BlockSpec(memory_space=pltpu.VMEM),) * 5,
-        scratch_shapes=[pltpu.SemaphoreType.DMA((5,))],
+        out_shape=tuple(pltpu.VMEM((rows, SIDE), jnp.bfloat16) for rows in (BLOCK, BLOCK, LONG, LONG)),
+        in_specs=[pl.BlockSpec(memory_space=pltpu.HBM)] * 2,
+        out_specs=(pl.BlockSpec(memory_space=pltpu.VMEM),) * 4,
+        scratch_shapes=[pltpu.SMEM((2, 2, 1, 2 * GROUP), jnp.int32), pltpu.SemaphoreType.DMA((5,))],
         cost_estimate=pl.CostEstimate(flops=1, bytes_accessed=1, transcendentals=0),
         name="prepare",
     )(
         pltpu.with_memory_space_constraint(patches.reshape(4, NODES * SIDE, SIDE), pltpu.HBM),
-        offsets,
+        pltpu.with_memory_space_constraint(offsets, pltpu.HBM),
     )
 
 
-def finish_kernel(total, every, node_links, node_offsets, shifts, moved, links, offsets):
+def finish_kernel(total, every, counts, offsets, shifts, moved):
     device, tile = lax.axis_index("member"), lax.axis_index("tile")
     position = 4 * lax.axis_index("group") + device
     lane = lax.broadcasted_iota(jnp.int32, (2, 128), 1)
     own = slice(NODE_COLS, 3 * NODE_COLS)
     tiles = lax.axis_size("tile")
-    links[...] = jnp.full_like(links, -1)
-    offsets[...] = jnp.zeros_like(offsets)
-    for k in range(4):
-        links[k : k + 1, own] = node_links[k] - (tile * 2 * NODE_COLS - NODE_COLS)
-        offsets[k : k + 1, own] = node_offsets[k // 2, k % 2].astype(jnp.float32)
     places = [pair_places(side) for side in range(2)]
     spread = {}
     near_tiles = {0: tile, -1: jnp.maximum(tile - 1, 0), 1: jnp.minimum(tile + 1, tiles - 1)}
@@ -341,7 +357,7 @@
     def shifts_of(member, step, column):
         if (member, step, column) not in spread:
             values = every[member * tiles + near_tiles[step]][:, column : column + 1]
-            spread[member, step, column] = jnp.broadcast_to(values, (FOUND, 128))
+            spread[member, step, column] = jnp.broadcast_to(values, (2, 128))
         return spread[member, step, column]
 
     def put(held, start, row, section, partner, step, source=0):
@@ -349,8 +365,7 @@
         for side in range(2):
             group, number = places[side][(first, first + partner)]
             for n in range(NODES):
-                at = 4 * number + 2 * n
-                value = shifts_of(2 * row + side, step, GROUPS * source + group)[at : at + 2]
+                value = shifts_of(2 * row + side, step, FOUND * source + GROUP * group + NODES * number + n)
                 held = jnp.where(lane == start + 2 * side + n, value, held)
         return held
 
@@ -395,8 +410,7 @@
     behind_pos, positions, ahead_pos = (0.25 * (pulls[k + 1] - pulls[k]) for k in range(3))
     neighbours = blank
     for e in range(4 * NODE_COLS):
-        count = jnp.sum(jnp.where(links[0:4, :] == e, 1.0, 0.0), axis=0, keepdims=True)
-        neighbours = neighbours + count * positions[:, e : e + 1]
+        neighbours = neighbours + counts[e : e + 1, :] * positions[:, e : e + 1]
     in_plane = 0.25 * (neighbours - 4.0 * positions)
     pull = has_next[2] * (ahead_pos - positions - here)
     pull_behind = has_next[1] * (positions - behind_pos - behind)
@@ -407,21 +421,20 @@
         moved[part] = positions[part : part + 1, own]
 
 
-def finish(every, links, offsets, total):
+def finish(every, counts, offsets, total):
     vmem = pl.BlockSpec(memory_space=pltpu.VMEM)
-    count = 2 * NODE_COLS
+    nodes = 2 * NODE_COLS
     return pl.pallas_call(
         functools.partial(finish_kernel, total),
         out_shape=(
-            jax.ShapeDtypeStruct((2, 2, 1, count), jnp.float32),
-            jax.ShapeDtypeStruct((2, 1, count), jnp.float32),
+            jax.ShapeDtypeStruct((2, 2, 1, nodes), jnp.float32),
+            jax.ShapeDtypeStruct((2, 1, nodes), jnp.float32),
         ),
         in_specs=[vmem] * 3,
         out_specs=(vmem, vmem),
-        scratch_shapes=[pltpu.VMEM((8, 128), jnp.int32), pltpu.VMEM((8, 128), jnp.float32)],
         cost_estimate=pl.CostEstimate(flops=1, bytes_accessed=1, transcendentals=0),
         name="finish",
-    )(every, links, offsets)
+    )(every, counts, offsets)
 
 
 def shards(sections, offsets, node_links):
@@ -433,22 +446,24 @@
         pairs = [(i, i + steps[i % 4]) for i in range(total) if 0 <= i + steps[i % 4] < total]
         return lax.ppermute(value, ("group", "member"), pairs)
 
-    kept, beside, across, slanted, beside_core = prepare(patches, offsets)
+    kept, beside, across, slanted = prepare(patches, offsets)
     across_in = send(across, (2, 2, -2, -2))
-    beside_in = send(beside_core, (1, -1, 1, -1))
     border_in = send(kept, (-4, -4, 4, 4))
     border_beside_in = send(beside, (-3, -5, 5, 3))
+    beside_in = send(beside, (1, -1, 1, -1))
     slanted_in = send(slanted, (3, 1, -1, -3))
-    state, consts = run_stage(0, [jnp.asarray(t) for t in tables()], (), [kept, across_in])
-    state, _ = run_stage(1, consts, state, [beside_in, border_in, border_beside_in])
-    state, _ = run_stage(2, consts, state, [slanted_in])
+    state, held = run_stage(0, [jnp.asarray(t) for t in tables()], (), [kept, border_in], (node_links, offsets))
+    *consts, counts, own_offsets = held
+    state, _ = run_stage(1, consts, state, [across_in])
+    state, _ = run_stage(2, consts, state, [border_beside_in, beside_in])
+    state, _ = run_stage(3, consts, state, [slanted_in])
     found = state[3]
 
-    rest = jnp.zeros((FOUND, 128 - 2 * GROUPS), jnp.float32)
     near = send(found, (4, 4, -4, -4))
-    found = jnp.concatenate([found[:, :GROUPS], near[:, :GROUPS], rest], axis=1)
-    every = lax.all_to_all(jnp.broadcast_to(found[None], (4 * tiles, FOUND, 128)), ("member", "tile"), 0, 0)
-    return finish(every, node_links, offsets, 4 * groups)
+    rest = jnp.zeros((2, 128 - 2 * FOUND), jnp.float32)
+    found = jnp.concatenate([found[:, :FOUND], near[:, :FOUND], rest], axis=1)
+    every = lax.all_to_all(jnp.broadcast_to(found[None], (4 * tiles, 2, 128)), ("member", "tile"), 0, 0)
+    return finish(every, counts, own_offsets, 4 * groups)
 
 
 def solution(mesh):

time: 66.5 us -> 64.6 us (0.971)
  waiting for transfers between devices: 12.6 us -> 9.42 us
  blocking collectives: 13.9 us -> 15.3 us
    ppermute x6, waiting for transfers between devices: 12.6 us -> 9.42 us  [send(): return lax.ppermute(value, ('group', 'member'), pairs)]
    all_to_all x1, blocking collectives: 13.9 us -> 15.3 us  [shards(): lax.all_to_all(jnp.broadcast_to(found[None], (4 * tiles, 2, 128)), ('memb...]
    pallas_call x1, Pallas kernels: 2.03 us -> 1.25 us  [prepare(): pl.pallas_call(prepare_kernel, out_shape=tuple((pltpu.VMEM((rows, SIDE),...]
    pallas_call x3 -> x4, Pallas kernels: 7.45 us -> 7.96 us  [run_stage(): pl.pallas_call(kernel, out_shape=tuple((pltpu.VMEM(shape, dtype) for shap...]
  transfers between devices with their start and end apart: 6 -> 6, of which waited for: 3 -> 3; matrix products, arithmetic and copies ran while one was open for 0% -> 0% of each run, Pallas kernels for 8% -> 9%
where the time goes in v4:
time: 64.6 us; the launch traced here: 63.9 us
  starting transfers between devices  27.3 us (42%)
  blocking collectives  15.3 us (24%)
  Pallas kernels  11 us (17%)
  waiting for transfers between devices  9.42 us (15%)
  between operations  0.76 us (1%)
    ppermute x6, starting transfers between devices, send(): return lax.ppermute(value, ('group', 'member'), pairs)  27.3 us
    all_to_all x1, blocking collectives, shards(): lax.all_to_all(jnp.broadcast_to(found[None], (4 * tiles, 2, 128)), ('memb...  15.3 us
    ppermute x6, waiting for transfers between devices, send(): return lax.ppermute(value, ('group', 'member'), pairs)  9.42 us
    pallas_call x4, Pallas kernels, run_stage(): pl.pallas_call(kernel, out_shape=tuple((pltpu.VMEM(shape, dtype) for shap...  7.96 us
    pallas_call x1, Pallas kernels, finish(): pl.pallas_call(functools.partial(finish_kernel, total), out_shape=(jax.Sh...  1.74 us
  transfers between devices with their start and end apart: 6, of which 3 were waited for; matrix products, arithmetic and copies ran while one was open for 0% of the time, Pallas kernels for 9%

profile of v4, /device:TPU:6, one launch (start us, length us, event | category | flops | bytes accessed | tf_op | source)
XLA Modules:
  0.0 63.9 jit_solution(17923779114367365940)
XLA Ops:
  0.6 1.2 %prepare.1 = (bf16[528,256]{1,0:T(8,128)(2,1)S(1)}, bf16[528,256]{1,0:T(8,128)(2,1)S(1)}, bf16[544,256]{1,0:T(8,128)(2,1)S(1)}, bf16[544,256]{1,0:T(8,128)(2,1)S(1)}) custom-call(bf16[4,512,256]{2,1,0:T(8,128)(2,1)} %bitcast.4, s32[2,2,1,8]{3,2,1,0:T(1,128)} %refs_8_.1), custom_call_target="tpu_custom_call" | custom-call | flops 1 | bytes 1 | tf_op jit(solution)/shard_map/prepare/pallas_call | solution.py:333
  1.9 7.7 %collective-permute-start.4 = (bf16[544,256]{1,0:T(8,128)(2,1)S(1)}, bf16[544,256]{1,0:T(8,128)(2,1)S(1)}, u32[]{:S(2)}, u32[]{:S(2)}) collective-permute-start(bf16[544,256]{1,0:T(8,128)(2,1)S(1)} %get-tuple-element.34), channel_id=1, source_target_pairs={{0,8},{4,12},{8,0},{12,4},{16,24},{20,28},{24,16},{28,20},{32,40},... | collective-permute-start | bytes 835592 | tf_op jit(solution)/shard_map/ppermute | solution.py:447
  9.6 1.9 %collective-permute-start.1 = (bf16[544,256]{1,0:T(8,128)(2,1)S(1)}, bf16[544,256]{1,0:T(8,128)(2,1)S(1)}, u32[]{:S(2)}, u32[]{:S(2)}) collective-permute-start(bf16[544,256]{1,0:T(8,128)(2,1)S(1)} %get-tuple-element.32), channel_id=1, source_target_pairs={{0,12},{4,8},{8,4},{12,0},{16,28},{20,24},{24,20},{28,16},{32,44},... | collective-permute-start | bytes 835592 | tf_op jit(solution)/shard_map/ppermute | solution.py:447
  11.6 11.2 %collective-permute-start = (bf16[528,256]{1,0:T(8,128)(2,1)S(1)}, bf16[528,256]{1,0:T(8,128)(2,1)S(1)}, u32[]{:S(2)}, u32[]{:S(2)}) collective-permute-start(bf16[528,256]{1,0:T(8,128)(2,1)S(1)} %get-tuple-element.26.refs_5_), channel_id=1, source_target_pairs={{8,24},{12,28},{16,0},{20,4},{24,40},{28,44},{32,16},{36,20},{40,5... | collective-permute-start | bytes 811016 | tf_op jit(solution)/shard_map/ppermute | solution.py:447
  22.8 2.0 %collective-permute-start.2 = (bf16[528,256]{1,0:T(8,128)(2,1)S(1)}, bf16[528,256]{1,0:T(8,128)(2,1)S(1)}, u32[]{:S(2)}, u32[]{:S(2)}) collective-permute-start(bf16[528,256]{1,0:T(8,128)(2,1)S(1)} %get-tuple-element.33), channel_id=1, source_target_pairs={{8,28},{12,24},{16,4},{20,0},{24,44},{28,40},{32,20},{36,16},{40,6... | collective-permute-start | bytes 811016 | tf_op jit(solution)/shard_map/ppermute | solution.py:447
  24.8 2.5 %collective-permute-start.3 = (bf16[528,256]{1,0:T(8,128)(2,1)S(1)}, bf16[528,256]{1,0:T(8,128)(2,1)S(1)}, u32[]{:S(2)}, u32[]{:S(2)}) collective-permute-start(bf16[528,256]{1,0:T(8,128)(2,1)S(1)} %get-tuple-element.33), channel_id=1, source_target_pairs={{0,4},{4,0},{8,12},{12,8},{16,20},{20,16},{24,28},{28,24},{32,36},... | collective-permute-start | bytes 811016 | tf_op jit(solution)/shard_map/ppermute | solution.py:447
  27.3 2.3 %collective-permute-done.refs_6_ = bf16[528,256]{1,0:T(8,128)(2,1)S(1)} collective-permute-done((bf16[528,256]{1,0:T(8,128)(2,1)S(1)}, bf16[528,256]{1,0:T(8,128)(2,1)S(1)}, u32[]{:S(2)}, u32[]{:S(2)}) %collective-permute-start) | collective-permute-done | bytes 270368 | tf_op jit(solution)/shard_map/ppermute | solution.py:447
  29.6 1.9 %stage0.1 = (bf16[12,144,512]{2,1,0:T(8,128)(2,1)S(1)}, f32[12,144,256]{2,1,0:T(8,128)S(1)}, bf16[6,16,256]{2,1,0:T(8,128)(2,1)S(1)}, f32[2,128]{1,0:T(2,128)S(1...) custom-call(bf16[256,256]{1,0:T(8,128)(2,1)} %constant.12.clone.refs, ...), custom_call_target="tpu_custom_call" | custom-call | flops 1 | bytes 1 | tf_op jit(solution)/shard_map/stage0/pallas_call | solution.py:270
  31.5 0.0 copy-start
  31.5 0.0 copy-start.1
  31.6 0.0 collective-permute-done.4.refs_5_
  31.6 1.5 %stage1.1 = (bf16[12,144,512]{2,1,0:T(8,128)(2,1)S(1)}, f32[12,144,256]{2,1,0:T(8,128)S(1)}, bf16[6,16,256]{2,1,0:T(8,128)(2,1)S(1)}, f32[2,128]{1,0:T(2,128)S(1)}) custom-call(bf16[256,256]{1,0:T(8,128)(2,1)S(1)} %get-tuple-element.27.refs_0_, ...), custom_call_target="tpu_custom_call", output_to_operand_aliasing={{0}: (6, {}), {1}: (7, {}), {2}: (8, {}), {3}: (9, {})} | custom-call | flops 1 | bytes 1 | tf_op jit(solution)/shard_map/stage1/pallas_call | solution.py:270
  33.1 0.0 copy-done
  33.1 1.5 %collective-permute-done.2.refs_5_ = bf16[528,256]{1,0:T(8,128)(2,1)S(1)} collective-permute-done((bf16[528,256]{1,0:T(8,128)(2,1)S(1)}, bf16[528,256]{1,0:T(8,128)(2,1)S(1)}, u32[]{:S(2)}, u32[]{:S(2)}) %collective-permute-start.2) | collective-permute-done | bytes 270368 | tf_op jit(solution)/shard_map/ppermute | solution.py:447
  34.7 0.0 collective-permute-done.3.refs_6_
  34.7 2.3 %stage2.1 = (bf16[12,144,512]{2,1,0:T(8,128)(2,1)S(1)}, f32[12,144,256]{2,1,0:T(8,128)S(1)}, bf16[6,16,256]{2,1,0:T(8,128)(2,1)S(1)}, f32[2,128]{1,0:T(2,128)S(1)}) custom-call(bf16[256,256]{1,0:T(8,128)(2,1)S(1)} %get-tuple-element.27.refs_0_, ...), custom_call_target="tpu_custom_call", output_to_operand_aliasing={{0}: (7, {}), {1}: (8, {}), {2}: (9, {}), {3}: (10, {})} | custom-call | flops 1 | bytes 1 | tf_op jit(solution)/shard_map/stage2/pallas_call | solution.py:270
  37.0 0.0 collective-permute-done.1.refs_5_
  37.0 2.2 %stage3.1 = (bf16[12,144,512]{2,1,0:T(8,128)(2,1)S(1)}, f32[12,144,256]{2,1,0:T(8,128)S(1)}, bf16[6,16,256]{2,1,0:T(8,128)(2,1)S(1)}, f32[2,128]{1,0:T(2,128)S(1)}) custom-call(bf16[256,256]{1,0:T(8,128)(2,1)S(1)} %get-tuple-element.27.refs_0_, ...), custom_call_target="tpu_custom_call", output_to_operand_aliasing={{0}: (6, {}), {1}: (7, {}), {2}: (8, {}), {3}: (9, {})} | custom-call | flops 1 | bytes 1 | tf_op jit(solution)/shard_map/stage3/pallas_call | solution.py:270
  39.2 1.9 %collective-permute-start.5 = (f32[2,128]{1,0:T(2,128)S(1)}, f32[2,128]{1,0:T(2,128)S(1)}, u32[]{:S(2)}, u32[]{:S(2)}) collective-permute-start(f32[2,128]{1,0:T(2,128)S(1)} %get-tuple-element.47), channel_id=1, source_target_pairs={{0,16},{4,20},{16,32},{20,36},{24,8},{28,12},{32,48},{36,52},{40,2... | collective-permute-start | bytes 3080 | tf_op jit(solution)/shard_map/ppermute | solution.py:447
  41.1 0.1 pad.2.clone
  41.2 5.6 %collective-permute-done.5 = f32[2,128]{1,0:T(2,128)S(1)} collective-permute-done((f32[2,128]{1,0:T(2,128)S(1)}, f32[2,128]{1,0:T(2,128)S(1)}, u32[]{:S(2)}, u32[]{:S(2)}) %collective-permute-start.5) | collective-permute-done | bytes 1056 | tf_op jit(solution)/shard_map/ppermute | solution.py:447
  46.8 0.1 maximum_maximum_fusion
  46.8 15.3 %all_to_all.5.every = f32[16,2,128]{2,1,0:T(2,128)} all-to-all(f32[16,2,128]{2,1,0:T(2,128)S(1)} %broadcast_in_dim.10), channel_id=1, replica_groups=mesh['group'=32,'member'=4,'tile'=4] {'member','tile'}, dimensions={0} | all-to-all | bytes 32768 | tf_op jit(solution)/shard_map/all_to_all | solution.py:465
  62.1 1.7 %finish.1 = (f32[2,2,1,8]{3,2,1,0:T(1,128)}, f32[2,1,8]{2,1,0:T(1,128)}) custom-call(f32[16,2,128]{2,1,0:T(2,128)} %all_to_all.5.every, f32[16,128]{1,0:T(8,128)} %copy-done, f32[8,128]{1,0:T(8,128)} %copy-done.1), custom_call_target="tpu_custom_call" | custom-call | flops 1 | bytes 1 | tf_op jit(solution)/shard_map/finish/pallas_call | solution.py:427
  (3 shorter events, 0.0 us)
Async XLA Ops:
  1.9 29.7 %collective-permute-start.4 = (bf16[544,256]{1,0:T(8,128)(2,1)S(1)}, bf16[544,256]{1,0:T(8,128)(2,1)S(1)}, u32[]{:S(2)}, u32[]{:S(2)}) collective-permute-start(bf16[544,256]{1,0:T(8,128)(2,1)S(1)} %get-tuple-element.34), channel_id=1, source_target_pairs={{0,8},{4,12},{8,0},{12,4},{16,24},{20,28},{24,16},{28,20},{32,40},... | collective-permute-start | bytes 835592 | tf_op jit(solution)/shard_map/ppermute | solution.py:447
  9.6 27.3 %collective-permute-start.1 = (bf16[544,256]{1,0:T(8,128)(2,1)S(1)}, bf16[544,256]{1,0:T(8,128)(2,1)S(1)}, u32[]{:S(2)}, u32[]{:S(2)}) collective-permute-start(bf16[544,256]{1,0:T(8,128)(2,1)S(1)} %get-tuple-element.32), channel_id=1, source_target_pairs={{0,12},{4,8},{8,4},{12,0},{16,28},{20,24},{24,20},{28,16},{32,44},... | collective-permute-start | bytes 835592 | tf_op jit(solution)/shard_map/ppermute | solution.py:447
  11.6 18.0 %collective-permute-start = (bf16[528,256]{1,0:T(8,128)(2,1)S(1)}, bf16[528,256]{1,0:T(8,128)(2,1)S(1)}, u32[]{:S(2)}, u32[]{:S(2)}) collective-permute-start(bf16[528,256]{1,0:T(8,128)(2,1)S(1)} %get-tuple-element.26.refs_5_), channel_id=1, source_target_pairs={{8,24},{12,28},{16,0},{20,4},{24,40},{28,44},{32,16},{36,20},{40,5... | collective-permute-start | bytes 811016 | tf_op jit(solution)/shard_map/ppermute | solution.py:447
  22.8 11.9 %collective-permute-start.2 = (bf16[528,256]{1,0:T(8,128)(2,1)S(1)}, bf16[528,256]{1,0:T(8,128)(2,1)S(1)}, u32[]{:S(2)}, u32[]{:S(2)}) collective-permute-start(bf16[528,256]{1,0:T(8,128)(2,1)S(1)} %get-tuple-element.33), channel_id=1, source_target_pairs={{8,28},{12,24},{16,4},{20,0},{24,44},{28,40},{32,20},{36,16},{40,6... | collective-permute-start | bytes 811016 | tf_op jit(solution)/shard_map/ppermute | solution.py:447
  24.8 9.9 %collective-permute-start.3 = (bf16[528,256]{1,0:T(8,128)(2,1)S(1)}, bf16[528,256]{1,0:T(8,128)(2,1)S(1)}, u32[]{:S(2)}, u32[]{:S(2)}) collective-permute-start(bf16[528,256]{1,0:T(8,128)(2,1)S(1)} %get-tuple-element.33), channel_id=1, source_target_pairs={{0,4},{4,0},{8,12},{12,8},{16,20},{20,16},{24,28},{28,24},{32,36},... | collective-permute-start | bytes 811016 | tf_op jit(solution)/shard_map/ppermute | solution.py:447
  31.5 1.6 %copy-start = (f32[16,128]{1,0:T(8,128)}, f32[16,128]{1,0:T(8,128)S(1)}, u32[]{:S(2)}) copy-start(f32[16,128]{1,0:T(8,128)S(1)} %get-tuple-element.48.counts) | copy-start | bytes 24580
  31.5 1.6 %copy-start.1 = (f32[8,128]{1,0:T(8,128)}, f32[8,128]{1,0:T(8,128)S(1)}, u32[]{:S(2)}) copy-start(f32[8,128]{1,0:T(8,128)S(1)} %get-tuple-element.49.offsets) | copy-start | bytes 12292
  39.2 7.6 %collective-permute-start.5 = (f32[2,128]{1,0:T(2,128)S(1)}, f32[2,128]{1,0:T(2,128)S(1)}, u32[]{:S(2)}, u32[]{:S(2)}) collective-permute-start(f32[2,128]{1,0:T(2,128)S(1)} %get-tuple-element.47), channel_id=1, source_target_pairs={{0,16},{4,20},{16,32},{20,36},{24,8},{28,12},{32,48},{36,52},{40,2... | collective-permute-start | bytes 3080 | tf_op jit(solution)/shard_map/ppermute | solution.py:447

commit v5 on v4

--- a/solution.py
+++ b/solution.py
@@ -20,7 +20,7 @@
 NODES = 2
 EXTRA = 16
 BLOCK = NODES * SIDE + EXTRA
-LONG = BLOCK + 16
+HALVES = 2 * NODES * SIDE + EXTRA
 WINDOW = 6
 
 STAGES = (
@@ -68,13 +68,13 @@
     window = np.arange(-REACH, REACH + 1)
     fold_phase = 2.0 * math.pi * (np.outer(row_freq, window) % SIDE) / SIDE
     fold_cos, fold_sin = np.cos(fold_phase), np.sin(fold_phase)
-    fold = np.zeros((GROUP, 2, SIDE, 2, 2, GROUP, SPAN), np.float32)
-    for j in range(GROUP):
+    fold = np.zeros((2, 2, SIDE, 2, 2, 2, SPAN), np.float32)
+    for odd in range(2):
         for part, out, value in ((0, 0, fold_cos), (1, 0, -fold_sin), (0, 1, fold_sin), (1, 1, fold_cos)):
             high = value.astype(np.float32).astype(ml_dtypes.bfloat16).astype(np.float32)
-            fold[j, part, :, out, 0, j, : window.size] = high
-            fold[j, part, :, out, 1, j, : window.size] = value - high
-    fold = fold.reshape(GROUP * 2 * SIDE, SIDE).astype(ml_dtypes.bfloat16)
+            fold[odd, part, :, odd, out, 0, : window.size] = high
+            fold[odd, part, :, odd, out, 1, : window.size] = value - high
+    fold = fold.reshape(2, 2 * SIDE, 128).astype(ml_dtypes.bfloat16)
     col_freq = np.arange(HALF + 1)
     twice = np.where((col_freq == 0) | (col_freq == HALF), 1.0, 2.0)[None, :] / SIDE
     col_phase = 2.0 * math.pi * (np.outer(window, col_freq) % SIDE) / SIDE
@@ -84,8 +84,8 @@
     close = close.reshape(2 * SPAN, ROWS)
     high = close.astype(ml_dtypes.bfloat16)
     low = (close - high.astype(np.float32)).astype(ml_dtypes.bfloat16)
-    lane, wide = np.arange(128)[:, None], np.arange(128 * GROUP)[None, :]
-    spread = (lane // SPAN == wide // 128).astype(ml_dtypes.bfloat16)
+    lane, wide = np.arange(128)[:, None], np.arange(256)[None, :]
+    spread = ((lane // 64 == wide // 128) & (lane % 64 < SPAN)).astype(ml_dtypes.bfloat16)
     return right, left, fold, np.concatenate([high, low], axis=0), spread
 
 
@@ -142,17 +142,17 @@
         found[...] = jnp.zeros_like(found)
     right_table, left_table = right[...], left[...]
     for block, place in zip(blocks, places):
-        offs[place] = block[NODES * SIDE : BLOCK, :]
+        offs[place] = block[block.shape[0] - EXTRA :, :128]
         for n in range(NODES):
             patch = block[n * SIDE : (n + 1) * SIDE, :]
+            if block.shape[1] < SIDE:
+                patch = jnp.concatenate([patch, block[(NODES + n) * SIDE : (NODES + n + 1) * SIDE, :]], axis=1)
             main, end = transform(patch, right_table, left_table)
             specs[place * NODES + n, :HALF, :], sizes[place * NODES + n, :HALF, :] = main
             specs[place * NODES + n, HALF:, :], sizes[place * NODES + n, HALF:, :] = end
 
     for k, code in enumerate(codes):
         held = NODES * len(STAGES[number][0][k])
-        if held < GROUP:
-            power[k, :, 2 * SIDE * held :] = jnp.zeros((ROWS, 2 * SIDE * (GROUP - held)), jnp.bfloat16)
         for j in range(held):
             bits = jnp.right_shift(code, 8 * (j // NODES))
             a_at = (bits & 7) * NODES + j % NODES
@@ -175,58 +175,69 @@
                 b = specs[b_at, rows, :].astype(jnp.float32)
                 ar, ai, br, bi = a[:, :SIDE], a[:, SIDE:], b[:, :SIDE], b[:, SIDE:]
                 br, bi = br * scale, bi * scale
-                at = 2 * SIDE * j
-                power[k, rows, at : at + SIDE] = (ar * br + ai * bi).astype(jnp.bfloat16)
-                power[k, rows, at + SIDE : at + 2 * SIDE] = (ai * br - ar * bi).astype(jnp.bfloat16)
-        folded[k] = jnp.dot(power[k], fold[...], preferred_element_type=jnp.float32)
-
+                to = slice(ROWS * (j // 2) + start, ROWS * (j // 2) + start + chunk)
+                power[k, j % 2, to, :SIDE] = (ar * br + ai * bi).astype(jnp.bfloat16)
+                power[k, j % 2, to, SIDE:] = (ai * br - ar * bi).astype(jnp.bfloat16)
+        used = ROWS * held // 2
+        both = sum(
+            jnp.dot(power[k, odd, :used, :], fold[odd], preferred_element_type=jnp.float32) for odd in range(2)
+        )
+        folded[:, 256 * k : 256 * k + 128] = both[:ROWS]
+        folded[:, 256 * k + 128 : 256 * (k + 1)] = both[ROWS:] if held > 2 else jnp.zeros_like(both)
+    if not codes:
+        return
+
+    sums = folded[...]
+    high = sums.astype(jnp.bfloat16)
+    low = (sums - high.astype(jnp.float32)).astype(jnp.bfloat16)
+    closed = jnp.dot(close[...], high, preferred_element_type=jnp.float32)
+    rest = jnp.dot(close[: 2 * SPAN], low, preferred_element_type=jnp.float32)
+    closed = closed[: 2 * SPAN] + closed[2 * SPAN :] + rest
     lane = lax.broadcasted_iota(jnp.int32, (SPAN, 128), 1)
     step_u = ((lane & (SPAN - 1)) - REACH).astype(jnp.float32)
     step_v = (lax.broadcasted_iota(jnp.int32, (SPAN, 128), 0) - REACH).astype(jnp.float32)
+    all_offs, pieces = [], []
     for k, code in enumerate(codes):
-        sums = folded[k]
-        high = sums.astype(jnp.bfloat16)
-        low = (sums - high.astype(jnp.float32)).astype(jnp.bfloat16)
-        closed = jnp.dot(close[...], high, preferred_element_type=jnp.float32)
-        rest = jnp.dot(close[: 2 * SPAN], low, preferred_element_type=jnp.float32)
-        closed = closed[: 2 * SPAN] + closed[2 * SPAN :] + rest
-        correlation = closed[:SPAN, :128] - closed[SPAN:, 128:]
-        correlation = correlation + pltpu.roll(correlation, 64, axis=1)
-        off_rows = []
         for pair in range(2):
             bits = jnp.right_shift(code, 8 * pair)
-            own = offs[bits & 7].astype(jnp.float32)[:8, :128]
+            own = offs[bits & 7].astype(jnp.float32)[:8]
             own = jnp.where((jnp.right_shift(bits, 6) & 1) == 0, own[:4], own[4:])
-            off_rows += [(own[n : n + 1], own[NODES + n : NODES + n + 1]) for n in range(NODES)]
-        off_y, off_x = off_rows[3]
-        for j in range(3):
-            below = lane[:1] < SPAN * (j + 1)
-            first = lane[:1] >= SPAN * j
-            off_y = jnp.where(below & first, off_rows[j][0], off_y)
-            off_x = jnp.where(below & first, off_rows[j][1], off_x)
-        from_y, from_x = step_u - off_y, step_v - off_x
-        inside = (jnp.abs(from_y) < 1.5) & (jnp.abs(from_x) < 1.5)
-        weight = jnp.where(inside, jnp.exp(3.0 * jnp.tanh(correlation)), 0.0)
-        sums = jnp.concatenate(
-            [
-                jnp.sum(weight, axis=0, keepdims=True),
-                jnp.sum(weight * from_y, axis=0, keepdims=True),
-                jnp.sum(weight * from_x, axis=0, keepdims=True),
-                jnp.zeros((5, 128), jnp.float32),
-            ],
-            axis=0,
-        )
-        pieces = []
-        for _ in range(3):
-            pieces.append(sums.astype(jnp.bfloat16))
-            sums = sums - pieces[-1].astype(jnp.float32)
-        whole = jnp.dot(jnp.concatenate(pieces, axis=0), spread[...], preferred_element_type=jnp.float32)
-        whole = whole[:8] + whole[8:16] + whole[16:]
-        ratio_y, ratio_x = whole[1:2] / whole[0:1], whole[2:3] / whole[0:1]
-        for j in range(GROUP):
-            at = slice(128 * j, 128 * (j + 1))
-            both = jnp.concatenate([off_rows[j][0] + ratio_y[:, at], off_rows[j][1] + ratio_x[:, at]], axis=0)
-            found[...] = jnp.where(lane[:2] == GROUP * (first_group + k) + j, both, found[...])
+            off_y = jnp.where(lane[:1] < 64, own[0:1], own[1:2])
+            off_x = jnp.where(lane[:1] < 64, own[2:3], own[3:4])
+            all_offs.append(own)
+            at = slice(256 * k + 128 * pair, 256 * k + 128 * (pair + 1))
+            by_cos, by_sin = closed[:SPAN, at], closed[SPAN:, at]
+            by_cos = by_cos + pltpu.roll(by_cos, 128 - SPAN, axis=1)
+            by_sin = pltpu.roll(by_sin, 128 - 2 * SPAN, axis=1) + pltpu.roll(by_sin, 128 - 3 * SPAN, axis=1)
+            correlation = by_cos - by_sin
+            from_y, from_x = step_u - off_y, step_v - off_x
+            inside = (jnp.abs(from_y) < 1.5) & (jnp.abs(from_x) < 1.5)
+            weight = jnp.where(inside, jnp.exp(3.0 * jnp.tanh(correlation)), 0.0)
+            sums = jnp.concatenate(
+                [
+                    jnp.sum(weight, axis=0, keepdims=True),
+                    jnp.sum(weight * from_y, axis=0, keepdims=True),
+                    jnp.sum(weight * from_x, axis=0, keepdims=True),
+                    jnp.zeros((5, 128), jnp.float32),
+                ],
+                axis=0,
+            )
+            for _ in range(3):
+                pieces.append(sums.astype(jnp.bfloat16))
+                sums = sums - pieces[-1].astype(jnp.float32)
+    whole = jnp.dot(jnp.concatenate(pieces, axis=0), spread[...], preferred_element_type=jnp.float32)
+    result = found[...]
+    for pair, own in enumerate(all_offs):
+        parts = [whole[24 * pair + 8 * piece : 24 * pair + 8 * (piece + 1)] for piece in range(3)]
+        total = parts[0] + parts[1] + parts[2]
+        ratio_y, ratio_x = total[1:2] / total[0:1], total[2:3] / total[0:1]
+        for n in range(NODES):
+            at = slice(128 * n, 128 * (n + 1))
+            both = jnp.concatenate(
+                [own[n : n + 1] + ratio_y[:, at], own[NODES + n : NODES + n + 1] + ratio_x[:, at]], axis=0
+            )
+            result = jnp.where(lane[:2] == GROUP * first_group + NODES * pair + n, both, result)
+    found[...] = result
 
 
 def run_stage(number, consts, state, blocks, mesh_inputs=()):
@@ -234,7 +245,7 @@
     shapes = (
         ((WINDOW * NODES, ROWS, 2 * SIDE), jnp.bfloat16),
         ((WINDOW * NODES, ROWS, SIDE), jnp.float32),
-        ((WINDOW, EXTRA, SIDE), jnp.bfloat16),
+        ((WINDOW, EXTRA, 128), jnp.bfloat16),
         ((2, 128), jnp.float32),
     )
     first = number == 0
@@ -276,8 +287,8 @@
         out_specs=(vmem,) * len(shapes),
         input_output_aliases={fixed + k: k for k in range(len(state))},
         scratch_shapes=[
-            pltpu.VMEM((groups, ROWS, 2 * SIDE * GROUP), jnp.bfloat16),
-            pltpu.VMEM((groups, ROWS, SIDE), jnp.float32),
+            pltpu.VMEM((groups, 2, 2 * ROWS, 2 * SIDE), jnp.bfloat16),
+            pltpu.VMEM((ROWS, 256 * groups), jnp.float32),
         ]
         + [pltpu.VMEM(x.shape, x.dtype) for x in mesh_inputs]
         + ([pltpu.VMEM((8, 128), jnp.int32), pltpu.SemaphoreType.DMA((count + 2,))] if first else []),
@@ -307,24 +318,25 @@
     numbers = [2 * r + s for r in (row, 1 - row) for s in (side, 1 - side)]
     copies = []
     for k in (2, 3, 0, 1):
-        copies.append(
-            pltpu.make_async_copy(patches.at[numbers[k]], blocks[k].at[pl.ds(0, NODES * SIDE)], sems.at[k])
-        )
-        copies[-1].start()
-    offsets_copy = pltpu.make_async_copy(all_offsets, offsets, sems.at[4])
+        block, width = blocks[k], blocks[k].shape[1]
+        for half in range(SIDE // width):
+            source = patches.at[numbers[k], :, pl.ds(half * width, width)]
+            target = block.at[pl.ds(half * NODES * SIDE, NODES * SIDE)]
+            copies.append(pltpu.make_async_copy(source, target, sems.at[len(copies)]))
+            copies[-1].start()
+    offsets_copy = pltpu.make_async_copy(all_offsets, offsets, sems.at[6])
     offsets_copy.start()
     offsets_copy.wait()
-    line = lax.broadcasted_iota(jnp.int32, (EXTRA, SIDE), 0)
+    line = lax.broadcasted_iota(jnp.int32, (EXTRA, 128), 0)
     for block, number in zip(blocks, numbers):
-        rows = jnp.zeros((EXTRA, SIDE), jnp.float32)
+        rows = jnp.zeros((EXTRA, 128), jnp.float32)
         for partner in range(2):
             for part in range(2):
                 for n in range(NODES):
                     value = offsets[partner, part, 0, NODES * number + n].astype(jnp.float32)
                     rows = jnp.where(line == 4 * partner + 2 * part + n, value, rows)
-        block[NODES * SIDE : BLOCK, :] = rows.astype(jnp.bfloat16)
-    for block in blocks[2:]:
-        block[BLOCK:, :] = jnp.zeros((block.shape[0] - BLOCK, SIDE), jnp.bfloat16)
+        for start in range(0, block.shape[1], 128):
+            block[block.shape[0] - EXTRA :, start : start + 128] = rows.astype(jnp.bfloat16)
     for copy in copies:
         copy.wait()
 
@@ -332,10 +344,10 @@
 def prepare(patches, offsets):
     return pl.pallas_call(
         prepare_kernel,
-        out_shape=tuple(pltpu.VMEM((rows, SIDE), jnp.bfloat16) for rows in (BLOCK, BLOCK, LONG, LONG)),
+        out_shape=tuple(pltpu.VMEM(shape, jnp.bfloat16) for shape in ((HALVES, 128),) * 2 + ((BLOCK, SIDE),) * 2),
         in_specs=[pl.BlockSpec(memory_space=pltpu.HBM)] * 2,
         out_specs=(pl.BlockSpec(memory_space=pltpu.VMEM),) * 4,
-        scratch_shapes=[pltpu.SMEM((2, 2, 1, 2 * GROUP), jnp.int32), pltpu.SemaphoreType.DMA((5,))],
+        scratch_shapes=[pltpu.SMEM((2, 2, 1, 2 * GROUP), jnp.int32), pltpu.SemaphoreType.DMA((7,))],
         cost_estimate=pl.CostEstimate(flops=1, bytes_accessed=1, transcendentals=0),
         name="prepare",
     )(
@@ -344,7 +356,7 @@
     )
 
 
-def finish_kernel(total, every, counts, offsets, shifts, moved):
+def finish_kernel(total, every, counts, offsets, shifts_out, moved_out, shifts, moved, sems):
     device, tile = lax.axis_index("member"), lax.axis_index("tile")
     position = 4 * lax.axis_index("group") + device
     lane = lax.broadcasted_iota(jnp.int32, (2, 128), 1)
@@ -419,19 +431,26 @@
         shifts[0, part] = found_next[part : part + 1, own]
         shifts[1, part] = found_second[part : part + 1, own]
         moved[part] = positions[part : part + 1, own]
+    copies = [
+        pltpu.make_async_copy(shifts, shifts_out, sems.at[0]),
+        pltpu.make_async_copy(moved, moved_out, sems.at[1]),
+    ]
+    for copy in copies:
+        copy.start()
+    for copy in copies:
+        copy.wait()
 
 
 def finish(every, counts, offsets, total):
-    vmem = pl.BlockSpec(memory_space=pltpu.VMEM)
+    vmem, hbm = pl.BlockSpec(memory_space=pltpu.VMEM), pl.BlockSpec(memory_space=pltpu.HBM)
     nodes = 2 * NODE_COLS
+    shapes = ((2, 2, 1, nodes), (2, 1, nodes))
     return pl.pallas_call(
         functools.partial(finish_kernel, total),
-        out_shape=(
-            jax.ShapeDtypeStruct((2, 2, 1, nodes), jnp.float32),
-            jax.ShapeDtypeStruct((2, 1, nodes), jnp.float32),
-        ),
+        out_shape=tuple(jax.ShapeDtypeStruct(shape, jnp.float32) for shape in shapes),
         in_specs=[vmem] * 3,
-        out_specs=(vmem, vmem),
+        out_specs=(hbm, hbm),
+        scratch_shapes=[pltpu.VMEM(shape, jnp.float32) for shape in shapes] + [pltpu.SemaphoreType.DMA((2,))],
         cost_estimate=pl.CostEstimate(flops=1, bytes_accessed=1, transcendentals=0),
         name="finish",
     )(every, counts, offsets)

time: 64.6 us -> 63.7 us (0.986)
  no operation moved by 1% of the time
where the time goes in v5:
time: 63.7 us; the launch traced here: 63.1 us
  starting transfers between devices  27.3 us (43%)
  blocking collectives  14.9 us (23%)
  Pallas kernels  10.8 us (17%)
  waiting for transfers between devices  9.14 us (14%)
  between operations  0.77 us (1%)
    ppermute x6, starting transfers between devices, send(): return lax.ppermute(value, ('group', 'member'), pairs)  27.3 us
    all_to_all x1, blocking collectives, shards(): lax.all_to_all(jnp.broadcast_to(found[None], (4 * tiles, 2, 128)), ('memb...  14.9 us
    ppermute x6, waiting for transfers between devices, send(): return lax.ppermute(value, ('group', 'member'), pairs)  9.14 us
    pallas_call x4, Pallas kernels, run_stage(): pl.pallas_call(kernel, out_shape=tuple((pltpu.VMEM(shape, dtype) for shap...  7.8 us
    pallas_call x1, Pallas kernels, finish(): pl.pallas_call(functools.partial(finish_kernel, total), out_shape=tuple((...  1.76 us
  transfers between devices with their start and end apart: 6, of which 3 were waited for; matrix products, arithmetic and copies ran while one was open for 0% of the time, Pallas kernels for 9%

profile of v5, /device:TPU:6, one launch (start us, length us, event | category | flops | bytes accessed | tf_op | source)
XLA Modules:
  0.0 63.1 jit_solution(16103973794952515048)
XLA Ops:
  0.6 1.3 %prepare.1 = (bf16[1040,128]{1,0:T(8,128)(2,1)S(1)}, bf16[1040,128]{1,0:T(8,128)(2,1)S(1)}, bf16[528,256]{1,0:T(8,128)(2,1)S(1)}, bf16[528,256]{1,0:T(8,128)(2,1)S(1)}) custom-call(bf16[4,512,256]{2,1,0:T(8,128)(2,1)} %bitcast.4, s32[2,2,1,8]{3,2,1,0:T(1,128)} %refs_8_.1), custom_call_target="tpu_custom_call" | custom-call | flops 1 | bytes 1 | tf_op jit(solution)/shard_map/prepare/pallas_call | solution.py:345
  1.9 7.7 %collective-permute-start.4 = (bf16[528,256]{1,0:T(8,128)(2,1)S(1)}, bf16[528,256]{1,0:T(8,128)(2,1)S(1)}, u32[]{:S(2)}, u32[]{:S(2)}) collective-permute-start(bf16[528,256]{1,0:T(8,128)(2,1)S(1)} %get-tuple-element.34), channel_id=1, source_target_pairs={{0,8},{4,12},{8,0},{12,4},{16,24},{20,28},{24,16},{28,20},{32,40},... | collective-permute-start | bytes 811016 | tf_op jit(solution)/shard_map/ppermute | solution.py:466
  9.6 1.9 %collective-permute-start.1 = (bf16[528,256]{1,0:T(8,128)(2,1)S(1)}, bf16[528,256]{1,0:T(8,128)(2,1)S(1)}, u32[]{:S(2)}, u32[]{:S(2)}) collective-permute-start(bf16[528,256]{1,0:T(8,128)(2,1)S(1)} %get-tuple-element.32), channel_id=1, source_target_pairs={{0,12},{4,8},{8,4},{12,0},{16,28},{20,24},{24,20},{28,16},{32,44},... | collective-permute-start | bytes 811016 | tf_op jit(solution)/shard_map/ppermute | solution.py:466
  11.6 11.2 %collective-permute-start = (bf16[1040,128]{1,0:T(8,128)(2,1)S(1)}, bf16[1040,128]{1,0:T(8,128)(2,1)S(1)}, u32[]{:S(2)}, u32[]{:S(2)}) collective-permute-start(bf16[1040,128]{1,0:T(8,128)(2,1)S(1)} %get-tuple-element.26.refs_5_), channel_id=1, source_target_pairs={{8,24},{12,28},{16,0},{20,4},{24,40},{28,44},{32,16},{36,20},{40,5... | collective-permute-start | bytes 798728 | tf_op jit(solution)/shard_map/ppermute | solution.py:466
  22.8 2.0 %collective-permute-start.2 = (bf16[1040,128]{1,0:T(8,128)(2,1)S(1)}, bf16[1040,128]{1,0:T(8,128)(2,1)S(1)}, u32[]{:S(2)}, u32[]{:S(2)}) collective-permute-start(bf16[1040,128]{1,0:T(8,128)(2,1)S(1)} %get-tuple-element.33), channel_id=1, source_target_pairs={{8,28},{12,24},{16,4},{20,0},{24,44},{28,40},{32,20},{36,16},{40,6... | collective-permute-start | bytes 798728 | tf_op jit(solution)/shard_map/ppermute | solution.py:466
  24.8 2.5 %collective-permute-start.3 = (bf16[1040,128]{1,0:T(8,128)(2,1)S(1)}, bf16[1040,128]{1,0:T(8,128)(2,1)S(1)}, u32[]{:S(2)}, u32[]{:S(2)}) collective-permute-start(bf16[1040,128]{1,0:T(8,128)(2,1)S(1)} %get-tuple-element.33), channel_id=1, source_target_pairs={{0,4},{4,0},{8,12},{12,8},{16,20},{20,16},{24,28},{28,24},{32,36},... | collective-permute-start | bytes 798728 | tf_op jit(solution)/shard_map/ppermute | solution.py:466
  27.3 2.2 %collective-permute-done.refs_6_ = bf16[1040,128]{1,0:T(8,128)(2,1)S(1)} collective-permute-done((bf16[1040,128]{1,0:T(8,128)(2,1)S(1)}, bf16[1040,128]{1,0:T(8,128)(2,1)S(1)}, u32[]{:S(2)}, u32[]{:S(2)}) %collective-permute-start) | collective-permute-done | bytes 266272 | tf_op jit(solution)/shard_map/ppermute | solution.py:466
  29.5 1.9 %stage0.1 = (bf16[12,144,512]{2,1,0:T(8,128)(2,1)S(1)}, f32[12,144,256]{2,1,0:T(8,128)S(1)}, bf16[6,16,128]{2,1,0:T(8,128)(2,1)S(1)}, f32[2,128]{1,0:T(2,128)S(1...) custom-call(bf16[256,256]{1,0:T(8,128)(2,1)} %constant.12.clone.refs, ...), custom_call_target="tpu_custom_call" | custom-call | flops 1 | bytes 1 | tf_op jit(solution)/shard_map/stage0/pallas_call | solution.py:281
  31.5 0.0 copy-start
  31.5 0.0 copy-start.1
  31.5 0.0 collective-permute-done.4.refs_5_
  31.5 1.6 %stage1.1 = (bf16[12,144,512]{2,1,0:T(8,128)(2,1)S(1)}, f32[12,144,256]{2,1,0:T(8,128)S(1)}, bf16[6,16,128]{2,1,0:T(8,128)(2,1)S(1)}, f32[2,128]{1,0:T(2,128)S(1)}) custom-call(bf16[256,256]{1,0:T(8,128)(2,1)S(1)} %get-tuple-element.27.refs_0_, ...), custom_call_target="tpu_custom_call", output_to_operand_aliasing={{0}: (6, {}), {1}: (7, {}), {2}: (8, {}), {3}: (9, {})} | custom-call | flops 1 | bytes 1 | tf_op jit(solution)/shard_map/stage1/pallas_call | solution.py:281
  33.1 0.0 copy-done
  33.2 1.3 %collective-permute-done.2.refs_5_ = bf16[1040,128]{1,0:T(8,128)(2,1)S(1)} collective-permute-done((bf16[1040,128]{1,0:T(8,128)(2,1)S(1)}, bf16[1040,128]{1,0:T(8,128)(2,1)S(1)}, u32[]{:S(2)}, u32[]{:S(2)}) %collective-permute-start.2) | collective-permute-done | bytes 266272 | tf_op jit(solution)/shard_map/ppermute | solution.py:466
  34.5 0.0 collective-permute-done.3.refs_6_
  34.5 2.1 %stage2.1 = (bf16[12,144,512]{2,1,0:T(8,128)(2,1)S(1)}, f32[12,144,256]{2,1,0:T(8,128)S(1)}, bf16[6,16,128]{2,1,0:T(8,128)(2,1)S(1)}, f32[2,128]{1,0:T(2,128)S(1)}) custom-call(bf16[256,256]{1,0:T(8,128)(2,1)S(1)} %get-tuple-element.27.refs_0_, ...), custom_call_target="tpu_custom_call", output_to_operand_aliasing={{0}: (7, {}), {1}: (8, {}), {2}: (9, {}), {3}: (10, {})} | custom-call | flops 1 | bytes 1 | tf_op jit(solution)/shard_map/stage2/pallas_call | solution.py:281
  36.6 0.0 collective-permute-done.1.refs_5_
  36.6 2.1 %stage3.1 = (bf16[12,144,512]{2,1,0:T(8,128)(2,1)S(1)}, f32[12,144,256]{2,1,0:T(8,128)S(1)}, bf16[6,16,128]{2,1,0:T(8,128)(2,1)S(1)}, f32[2,128]{1,0:T(2,128)S(1)}) custom-call(bf16[256,256]{1,0:T(8,128)(2,1)S(1)} %get-tuple-element.27.refs_0_, ...), custom_call_target="tpu_custom_call", output_to_operand_aliasing={{0}: (6, {}), {1}: (7, {}), {2}: (8, {}), {3}: (9, {})} | custom-call | flops 1 | bytes 1 | tf_op jit(solution)/shard_map/stage3/pallas_call | solution.py:281
  38.8 1.9 %collective-permute-start.5 = (f32[2,128]{1,0:T(2,128)S(1)}, f32[2,128]{1,0:T(2,128)S(1)}, u32[]{:S(2)}, u32[]{:S(2)}) collective-permute-start(f32[2,128]{1,0:T(2,128)S(1)} %get-tuple-element.47), channel_id=1, source_target_pairs={{0,16},{4,20},{16,32},{20,36},{24,8},{28,12},{32,48},{36,52},{40,2... | collective-permute-start | bytes 3080 | tf_op jit(solution)/shard_map/ppermute | solution.py:466
  40.7 0.1 pad.2.clone
  40.8 5.6 %collective-permute-done.5 = f32[2,128]{1,0:T(2,128)S(1)} collective-permute-done((f32[2,128]{1,0:T(2,128)S(1)}, f32[2,128]{1,0:T(2,128)S(1)}, u32[]{:S(2)}, u32[]{:S(2)}) %collective-permute-start.5) | collective-permute-done | bytes 1056 | tf_op jit(solution)/shard_map/ppermute | solution.py:466
  46.3 0.1 maximum_maximum_fusion
  46.4 14.9 %all_to_all.5.every = f32[16,2,128]{2,1,0:T(2,128)} all-to-all(f32[16,2,128]{2,1,0:T(2,128)S(1)} %broadcast_in_dim.10), channel_id=1, replica_groups=mesh['group'=32,'member'=4,'tile'=4] {'member','tile'}, dimensions={0} | all-to-all | bytes 32768 | tf_op jit(solution)/shard_map/all_to_all | solution.py:484
  61.3 1.8 %finish.1 = (f32[2,2,1,8]{3,2,1,0:T(1,128)}, f32[2,1,8]{2,1,0:T(1,128)}) custom-call(f32[16,2,128]{2,1,0:T(2,128)} %all_to_all.5.every, f32[16,128]{1,0:T(8,128)} %copy-done, f32[8,128]{1,0:T(8,128)} %copy-done.1), custom_call_target="tpu_custom_call" | custom-call | flops 1 | bytes 1 | tf_op jit(solution)/shard_map/finish/pallas_call | solution.py:448
  (3 shorter events, 0.0 us)
Async XLA Ops:
  1.9 29.6 %collective-permute-start.4 = (bf16[528,256]{1,0:T(8,128)(2,1)S(1)}, bf16[528,256]{1,0:T(8,128)(2,1)S(1)}, u32[]{:S(2)}, u32[]{:S(2)}) collective-permute-start(bf16[528,256]{1,0:T(8,128)(2,1)S(1)} %get-tuple-element.34), channel_id=1, source_target_pairs={{0,8},{4,12},{8,0},{12,4},{16,24},{20,28},{24,16},{28,20},{32,40},... | collective-permute-start | bytes 811016 | tf_op jit(solution)/shard_map/ppermute | solution.py:466
  9.6 27.0 %collective-permute-start.1 = (bf16[528,256]{1,0:T(8,128)(2,1)S(1)}, bf16[528,256]{1,0:T(8,128)(2,1)S(1)}, u32[]{:S(2)}, u32[]{:S(2)}) collective-permute-start(bf16[528,256]{1,0:T(8,128)(2,1)S(1)} %get-tuple-element.32), channel_id=1, source_target_pairs={{0,12},{4,8},{8,4},{12,0},{16,28},{20,24},{24,20},{28,16},{32,44},... | collective-permute-start | bytes 811016 | tf_op jit(solution)/shard_map/ppermute | solution.py:466
  11.6 17.9 %collective-permute-start = (bf16[1040,128]{1,0:T(8,128)(2,1)S(1)}, bf16[1040,128]{1,0:T(8,128)(2,1)S(1)}, u32[]{:S(2)}, u32[]{:S(2)}) collective-permute-start(bf16[1040,128]{1,0:T(8,128)(2,1)S(1)} %get-tuple-element.26.refs_5_), channel_id=1, source_target_pairs={{8,24},{12,28},{16,0},{20,4},{24,40},{28,44},{32,16},{36,20},{40,5... | collective-permute-start | bytes 798728 | tf_op jit(solution)/shard_map/ppermute | solution.py:466
  22.8 11.7 %collective-permute-start.2 = (bf16[1040,128]{1,0:T(8,128)(2,1)S(1)}, bf16[1040,128]{1,0:T(8,128)(2,1)S(1)}, u32[]{:S(2)}, u32[]{:S(2)}) collective-permute-start(bf16[1040,128]{1,0:T(8,128)(2,1)S(1)} %get-tuple-element.33), channel_id=1, source_target_pairs={{8,28},{12,24},{16,4},{20,0},{24,44},{28,40},{32,20},{36,16},{40,6... | collective-permute-start | bytes 798728 | tf_op jit(solution)/shard_map/ppermute | solution.py:466
  24.8 9.7 %collective-permute-start.3 = (bf16[1040,128]{1,0:T(8,128)(2,1)S(1)}, bf16[1040,128]{1,0:T(8,128)(2,1)S(1)}, u32[]{:S(2)}, u32[]{:S(2)}) collective-permute-start(bf16[1040,128]{1,0:T(8,128)(2,1)S(1)} %get-tuple-element.33), channel_id=1, source_target_pairs={{0,4},{4,0},{8,12},{12,8},{16,20},{20,16},{24,28},{28,24},{32,36},... | collective-permute-start | bytes 798728 | tf_op jit(solution)/shard_map/ppermute | solution.py:466
  31.5 1.7 %copy-start = (f32[16,128]{1,0:T(8,128)}, f32[16,128]{1,0:T(8,128)S(1)}, u32[]{:S(2)}) copy-start(f32[16,128]{1,0:T(8,128)S(1)} %get-tuple-element.48.counts) | copy-start | bytes 24580
  31.5 1.7 %copy-start.1 = (f32[8,128]{1,0:T(8,128)}, f32[8,128]{1,0:T(8,128)S(1)}, u32[]{:S(2)}) copy-start(f32[8,128]{1,0:T(8,128)S(1)} %get-tuple-element.49.offsets) | copy-start | bytes 12292
  38.8 7.6 %collective-permute-start.5 = (f32[2,128]{1,0:T(2,128)S(1)}, f32[2,128]{1,0:T(2,128)S(1)}, u32[]{:S(2)}, u32[]{:S(2)}) collective-permute-start(f32[2,128]{1,0:T(2,128)S(1)} %get-tuple-element.47), channel_id=1, source_target_pairs={{0,16},{4,20},{16,32},{20,36},{24,8},{28,12},{32,48},{36,52},{40,2... | collective-permute-start | bytes 3080 | tf_op jit(solution)/shard_map/ppermute | solution.py:466

commit v6 on v5

--- a/solution.py
+++ b/solution.py
@@ -482,7 +482,8 @@
     rest = jnp.zeros((2, 128 - 2 * FOUND), jnp.float32)
     found = jnp.concatenate([found[:, :FOUND], near[:, :FOUND], rest], axis=1)
     every = lax.all_to_all(jnp.broadcast_to(found[None], (4 * tiles, 2, 128)), ("member", "tile"), 0, 0)
-    return finish(every, counts, own_offsets, 4 * groups)
+    near_by = [pltpu.with_memory_space_constraint(x, pltpu.VMEM) for x in (every, counts, own_offsets)]
+    return finish(*near_by, 4 * groups)
 
 
 def solution(mesh):

time: 63.7 us -> 62.8 us (0.986)
  Pallas kernels: 10.8 us -> 10.1 us
    pallas_call x1, Pallas kernels: 1.76 us -> 1.03 us  [finish(): pl.pallas_call(functools.partial(finish_kernel, total), out_shape=tuple((...]
where the time goes in v6:
time: 62.8 us; the launch traced here: 62.2 us
  starting transfers between devices  27.3 us (43%)
  blocking collectives  14.8 us (24%)
  Pallas kernels  10.1 us (16%)
  waiting for transfers between devices  9.18 us (15%)
  between operations  0.74 us (1%)
    ppermute x6, starting transfers between devices, send(): return lax.ppermute(value, ('group', 'member'), pairs)  27.3 us
    all_to_all x1, blocking collectives, shards(): lax.all_to_all(jnp.broadcast_to(found[None], (4 * tiles, 2, 128)), ('memb...  14.8 us
    ppermute x6, waiting for transfers between devices, send(): return lax.ppermute(value, ('group', 'member'), pairs)  9.18 us
    pallas_call x4, Pallas kernels, run_stage(): pl.pallas_call(kernel, out_shape=tuple((pltpu.VMEM(shape, dtype) for shap...  7.8 us
    pallas_call x1, Pallas kernels, prepare(): pl.pallas_call(prepare_kernel, out_shape=tuple((pltpu.VMEM(shape, jnp.bfl...  1.26 us
  transfers between devices with their start and end apart: 6, of which 3 were waited for; matrix products, arithmetic and copies ran while one was open for 0% of the time, Pallas kernels for 9%

profile of v6, /device:TPU:6, one launch (start us, length us, event | category | flops | bytes accessed | tf_op | source)
XLA Modules:
  0.0 62.2 jit_solution(5387032821173871427)
XLA Ops:
  0.6 1.3 %prepare.1 = (bf16[1040,128]{1,0:T(8,128)(2,1)S(1)}, bf16[1040,128]{1,0:T(8,128)(2,1)S(1)}, bf16[528,256]{1,0:T(8,128)(2,1)S(1)}, bf16[528,256]{1,0:T(8,128)(2,1)S(1)}) custom-call(bf16[4,512,256]{2,1,0:T(8,128)(2,1)} %bitcast.4, s32[2,2,1,8]{3,2,1,0:T(1,128)} %refs_8_.1), custom_call_target="tpu_custom_call" | custom-call | flops 1 | bytes 1 | tf_op jit(solution)/shard_map/prepare/pallas_call | solution.py:345
  1.9 7.7 %collective-permute-start.4 = (bf16[528,256]{1,0:T(8,128)(2,1)S(1)}, bf16[528,256]{1,0:T(8,128)(2,1)S(1)}, u32[]{:S(2)}, u32[]{:S(2)}) collective-permute-start(bf16[528,256]{1,0:T(8,128)(2,1)S(1)} %get-tuple-element.34), channel_id=1, source_target_pairs={{0,8},{4,12},{8,0},{12,4},{16,24},{20,28},{24,16},{28,20},{32,40},... | collective-permute-start | bytes 811016 | tf_op jit(solution)/shard_map/ppermute | solution.py:466
  9.6 1.9 %collective-permute-start.1 = (bf16[528,256]{1,0:T(8,128)(2,1)S(1)}, bf16[528,256]{1,0:T(8,128)(2,1)S(1)}, u32[]{:S(2)}, u32[]{:S(2)}) collective-permute-start(bf16[528,256]{1,0:T(8,128)(2,1)S(1)} %get-tuple-element.32), channel_id=1, source_target_pairs={{0,12},{4,8},{8,4},{12,0},{16,28},{20,24},{24,20},{28,16},{32,44},... | collective-permute-start | bytes 811016 | tf_op jit(solution)/shard_map/ppermute | solution.py:466
  11.6 11.2 %collective-permute-start = (bf16[1040,128]{1,0:T(8,128)(2,1)S(1)}, bf16[1040,128]{1,0:T(8,128)(2,1)S(1)}, u32[]{:S(2)}, u32[]{:S(2)}) collective-permute-start(bf16[1040,128]{1,0:T(8,128)(2,1)S(1)} %get-tuple-element.26.refs_5_), channel_id=1, source_target_pairs={{8,24},{12,28},{16,0},{20,4},{24,40},{28,44},{32,16},{36,20},{40,5... | collective-permute-start | bytes 798728 | tf_op jit(solution)/shard_map/ppermute | solution.py:466
  22.8 2.0 %collective-permute-start.2 = (bf16[1040,128]{1,0:T(8,128)(2,1)S(1)}, bf16[1040,128]{1,0:T(8,128)(2,1)S(1)}, u32[]{:S(2)}, u32[]{:S(2)}) collective-permute-start(bf16[1040,128]{1,0:T(8,128)(2,1)S(1)} %get-tuple-element.33), channel_id=1, source_target_pairs={{8,28},{12,24},{16,4},{20,0},{24,44},{28,40},{32,20},{36,16},{40,6... | collective-permute-start | bytes 798728 | tf_op jit(solution)/shard_map/ppermute | solution.py:466
  24.8 2.5 %collective-permute-start.3 = (bf16[1040,128]{1,0:T(8,128)(2,1)S(1)}, bf16[1040,128]{1,0:T(8,128)(2,1)S(1)}, u32[]{:S(2)}, u32[]{:S(2)}) collective-permute-start(bf16[1040,128]{1,0:T(8,128)(2,1)S(1)} %get-tuple-element.33), channel_id=1, source_target_pairs={{0,4},{4,0},{8,12},{12,8},{16,20},{20,16},{24,28},{28,24},{32,36},... | collective-permute-start | bytes 798728 | tf_op jit(solution)/shard_map/ppermute | solution.py:466
  27.3 2.2 %collective-permute-done.refs_6_ = bf16[1040,128]{1,0:T(8,128)(2,1)S(1)} collective-permute-done((bf16[1040,128]{1,0:T(8,128)(2,1)S(1)}, bf16[1040,128]{1,0:T(8,128)(2,1)S(1)}, u32[]{:S(2)}, u32[]{:S(2)}) %collective-permute-start) | collective-permute-done | bytes 266272 | tf_op jit(solution)/shard_map/ppermute | solution.py:466
  29.5 1.9 %stage0.1 = (bf16[12,144,512]{2,1,0:T(8,128)(2,1)S(1)}, f32[12,144,256]{2,1,0:T(8,128)S(1)}, bf16[6,16,128]{2,1,0:T(8,128)(2,1)S(1)}, f32[2,128]{1,0:T(2,128)S(1...) custom-call(bf16[256,256]{1,0:T(8,128)(2,1)} %constant.12.clone.refs, ...), custom_call_target="tpu_custom_call" | custom-call | flops 1 | bytes 1 | tf_op jit(solution)/shard_map/stage0/pallas_call | solution.py:281
  31.5 0.0 collective-permute-done.4.refs_5_
  31.5 1.6 %stage1.1 = (bf16[12,144,512]{2,1,0:T(8,128)(2,1)S(1)}, f32[12,144,256]{2,1,0:T(8,128)S(1)}, bf16[6,16,128]{2,1,0:T(8,128)(2,1)S(1)}, f32[2,128]{1,0:T(2,128)S(1)}) custom-call(bf16[256,256]{1,0:T(8,128)(2,1)S(1)} %get-tuple-element.27.refs_0_, ...), custom_call_target="tpu_custom_call", output_to_operand_aliasing={{0}: (6, {}), {1}: (7, {}), {2}: (8, {}), {3}: (9, {})} | custom-call | flops 1 | bytes 1 | tf_op jit(solution)/shard_map/stage1/pallas_call | solution.py:281
  33.1 1.4 %collective-permute-done.2.refs_5_ = bf16[1040,128]{1,0:T(8,128)(2,1)S(1)} collective-permute-done((bf16[1040,128]{1,0:T(8,128)(2,1)S(1)}, bf16[1040,128]{1,0:T(8,128)(2,1)S(1)}, u32[]{:S(2)}, u32[]{:S(2)}) %collective-permute-start.2) | collective-permute-done | bytes 266272 | tf_op jit(solution)/shard_map/ppermute | solution.py:466
  34.5 0.0 collective-permute-done.3.refs_6_
  34.5 2.1 %stage2.1 = (bf16[12,144,512]{2,1,0:T(8,128)(2,1)S(1)}, f32[12,144,256]{2,1,0:T(8,128)S(1)}, bf16[6,16,128]{2,1,0:T(8,128)(2,1)S(1)}, f32[2,128]{1,0:T(2,128)S(1)}) custom-call(bf16[256,256]{1,0:T(8,128)(2,1)S(1)} %get-tuple-element.27.refs_0_, ...), custom_call_target="tpu_custom_call", output_to_operand_aliasing={{0}: (7, {}), {1}: (8, {}), {2}: (9, {}), {3}: (10, {})} | custom-call | flops 1 | bytes 1 | tf_op jit(solution)/shard_map/stage2/pallas_call | solution.py:281
  36.6 0.0 collective-permute-done.1.refs_5_
  36.6 2.1 %stage3.1 = (bf16[12,144,512]{2,1,0:T(8,128)(2,1)S(1)}, f32[12,144,256]{2,1,0:T(8,128)S(1)}, bf16[6,16,128]{2,1,0:T(8,128)(2,1)S(1)}, f32[2,128]{1,0:T(2,128)S(1)}) custom-call(bf16[256,256]{1,0:T(8,128)(2,1)S(1)} %get-tuple-element.27.refs_0_, ...), custom_call_target="tpu_custom_call", output_to_operand_aliasing={{0}: (6, {}), {1}: (7, {}), {2}: (8, {}), {3}: (9, {})} | custom-call | flops 1 | bytes 1 | tf_op jit(solution)/shard_map/stage3/pallas_call | solution.py:281
  38.8 1.9 %collective-permute-start.5 = (f32[2,128]{1,0:T(2,128)S(1)}, f32[2,128]{1,0:T(2,128)S(1)}, u32[]{:S(2)}, u32[]{:S(2)}) collective-permute-start(f32[2,128]{1,0:T(2,128)S(1)} %get-tuple-element.47), channel_id=1, source_target_pairs={{0,16},{4,20},{16,32},{20,36},{24,8},{28,12},{32,48},{36,52},{40,2... | collective-permute-start | bytes 3080 | tf_op jit(solution)/shard_map/ppermute | solution.py:466
  40.7 0.1 pad.2.clone
  40.8 5.6 %collective-permute-done.5 = f32[2,128]{1,0:T(2,128)S(1)} collective-permute-done((f32[2,128]{1,0:T(2,128)S(1)}, f32[2,128]{1,0:T(2,128)S(1)}, u32[]{:S(2)}, u32[]{:S(2)}) %collective-permute-start.5) | collective-permute-done | bytes 1056 | tf_op jit(solution)/shard_map/ppermute | solution.py:466
  46.3 0.1 maximum_maximum_fusion
  46.4 14.8 %all_to_all.5.every = f32[16,2,128]{2,1,0:T(2,128)S(1)} all-to-all(f32[16,2,128]{2,1,0:T(2,128)S(1)} %broadcast_in_dim.10), channel_id=1, replica_groups=mesh['group'=32,'member'=4,'tile'=4] {'member','tile'}, dimensions={0} | all-to-all | bytes 32768 | tf_op jit(solution)/shard_map/all_to_all | solution.py:484
  61.2 1.0 %finish.1 = (f32[2,2,1,8]{3,2,1,0:T(1,128)}, f32[2,1,8]{2,1,0:T(1,128)}) custom-call(f32[16,2,128]{2,1,0:T(2,128)S(1)} %all_to_all.5.every, f32[16,128]{1,0:T(8,128)S(1)} %get-tuple-element.48.counts, f32[8,128]{1,0:T(8,128)S(1)} %get-tuple-element.49.offsets), custom_call_target="tpu_custom_call" | custom-call | flops 1 | bytes 1 | tf_op jit(solution)/shard_map/finish/pallas_call | solution.py:448
  (2 shorter events, 0.0 us)
Async XLA Ops:
  1.9 29.6 %collective-permute-start.4 = (bf16[528,256]{1,0:T(8,128)(2,1)S(1)}, bf16[528,256]{1,0:T(8,128)(2,1)S(1)}, u32[]{:S(2)}, u32[]{:S(2)}) collective-permute-start(bf16[528,256]{1,0:T(8,128)(2,1)S(1)} %get-tuple-element.34), channel_id=1, source_target_pairs={{0,8},{4,12},{8,0},{12,4},{16,24},{20,28},{24,16},{28,20},{32,40},... | collective-permute-start | bytes 811016 | tf_op jit(solution)/shard_map/ppermute | solution.py:466
  9.6 27.0 %collective-permute-start.1 = (bf16[528,256]{1,0:T(8,128)(2,1)S(1)}, bf16[528,256]{1,0:T(8,128)(2,1)S(1)}, u32[]{:S(2)}, u32[]{:S(2)}) collective-permute-start(bf16[528,256]{1,0:T(8,128)(2,1)S(1)} %get-tuple-element.32), channel_id=1, source_target_pairs={{0,12},{4,8},{8,4},{12,0},{16,28},{20,24},{24,20},{28,16},{32,44},... | collective-permute-start | bytes 811016 | tf_op jit(solution)/shard_map/ppermute | solution.py:466
  11.6 17.9 %collective-permute-start = (bf16[1040,128]{1,0:T(8,128)(2,1)S(1)}, bf16[1040,128]{1,0:T(8,128)(2,1)S(1)}, u32[]{:S(2)}, u32[]{:S(2)}) collective-permute-start(bf16[1040,128]{1,0:T(8,128)(2,1)S(1)} %get-tuple-element.26.refs_5_), channel_id=1, source_target_pairs={{8,24},{12,28},{16,0},{20,4},{24,40},{28,44},{32,16},{36,20},{40,5... | collective-permute-start | bytes 798728 | tf_op jit(solution)/shard_map/ppermute | solution.py:466
  22.8 11.7 %collective-permute-start.2 = (bf16[1040,128]{1,0:T(8,128)(2,1)S(1)}, bf16[1040,128]{1,0:T(8,128)(2,1)S(1)}, u32[]{:S(2)}, u32[]{:S(2)}) collective-permute-start(bf16[1040,128]{1,0:T(8,128)(2,1)S(1)} %get-tuple-element.33), channel_id=1, source_target_pairs={{8,28},{12,24},{16,4},{20,0},{24,44},{28,40},{32,20},{36,16},{40,6... | collective-permute-start | bytes 798728 | tf_op jit(solution)/shard_map/ppermute | solution.py:466
  24.8 9.7 %collective-permute-start.3 = (bf16[1040,128]{1,0:T(8,128)(2,1)S(1)}, bf16[1040,128]{1,0:T(8,128)(2,1)S(1)}, u32[]{:S(2)}, u32[]{:S(2)}) collective-permute-start(bf16[1040,128]{1,0:T(8,128)(2,1)S(1)} %get-tuple-element.33), channel_id=1, source_target_pairs={{0,4},{4,0},{8,12},{12,8},{16,20},{20,16},{24,28},{28,24},{32,36},... | collective-permute-start | bytes 798728 | tf_op jit(solution)/shard_map/ppermute | solution.py:466
  38.8 7.6 %collective-permute-start.5 = (f32[2,128]{1,0:T(2,128)S(1)}, f32[2,128]{1,0:T(2,128)S(1)}, u32[]{:S(2)}, u32[]{:S(2)}) collective-permute-start(f32[2,128]{1,0:T(2,128)S(1)} %get-tuple-element.47), channel_id=1, source_target_pairs={{0,16},{4,20},{16,32},{20,36},{24,8},{28,12},{32,48},{36,52},{40,2... | collective-permute-start | bytes 3080 | tf_op jit(solution)/shard_map/ppermute | solution.py:466

commit v7 on v6

--- a/solution.py
+++ b/solution.py
@@ -30,7 +30,7 @@
     ((((2, 3), (3, 4)), ((1, 3), (3, 5))), (((2, 3), (1, 2)), ((0, 2), (2, 4)))),
 )
 GROUPS = 5
-FOUND = GROUP * GROUPS
+FOUND = 2 * GROUP * GROUPS
 
 
 def pair_places(side):
@@ -129,7 +129,7 @@
 def stage_kernel(number, consts, blocks, state, scratch):
     right, left, fold, close, spread = consts
     specs, sizes, offs, found = state
-    power, folded = scratch
+    power, folded, new_specs, new_sizes = scratch
     device = lax.axis_index("member")
     row, side = device // 2, lax.rem(device, 2)
     codes = stage_codes(number, side)
@@ -141,26 +141,42 @@
     if number == 0:
         found[...] = jnp.zeros_like(found)
     right_table, left_table = right[...], left[...]
+
+    def take(block, n, specs, sizes, at):
+        patch = block[n * SIDE : (n + 1) * SIDE, :]
+        if block.shape[1] < SIDE:
+            patch = jnp.concatenate([patch, block[(NODES + n) * SIDE : (NODES + n + 1) * SIDE, :]], axis=1)
+        main, end = transform(patch, right_table, left_table)
+        specs[at, :HALF, :], sizes[at, :HALF, :] = main
+        specs[at, HALF:, :], sizes[at, HALF:, :] = end
+
     for block, place in zip(blocks, places):
         offs[place] = block[block.shape[0] - EXTRA :, :128]
-        for n in range(NODES):
-            patch = block[n * SIDE : (n + 1) * SIDE, :]
-            if block.shape[1] < SIDE:
-                patch = jnp.concatenate([patch, block[(NODES + n) * SIDE : (NODES + n + 1) * SIDE, :]], axis=1)
-            main, end = transform(patch, right_table, left_table)
-            specs[place * NODES + n, :HALF, :], sizes[place * NODES + n, :HALF, :] = main
-            specs[place * NODES + n, HALF:, :], sizes[place * NODES + n, HALF:, :] = end
-
-    for k, code in enumerate(codes):
-        held = NODES * len(STAGES[number][0][k])
-        for j in range(held):
+        for n in range(NODES if number < 3 else 0):
+            take(block, n, specs, sizes, place * NODES + n)
+
+    for n in range(NODES):
+        if number == 3:
+            take(blocks[0], n, new_specs, new_sizes, n)
+        for k, j in [(k, j) for k, pairs in enumerate(STAGES[number][0]) for j in range(n, NODES * len(pairs), NODES)]:
+            code = codes[k]
             bits = jnp.right_shift(code, 8 * (j // NODES))
-            a_at = (bits & 7) * NODES + j % NODES
-            b_at = (jnp.right_shift(bits, 3) & 7) * NODES + j % NODES
+            a_place, b_place = bits & 7, jnp.right_shift(bits, 3) & 7
+            if number < 3:
+                a_from, b_from = (specs, sizes, a_place * NODES + j % NODES), (specs, sizes, b_place * NODES + j % NODES)
+            else:
+                taken = a_place == places[0]
+                a_from = (new_specs, new_sizes, j % NODES)
+                b_from = (specs, sizes, jnp.where(taken, b_place, a_place) * NODES + j % NODES)
+                sign = jnp.where(taken, 1.0, -1.0).astype(jnp.float32)
+
+            def size_of(rows, a_from=a_from, b_from=b_from):
+                return a_from[1][a_from[2], rows, :] * b_from[1][b_from[2], rows, :]
+
             total = jnp.zeros((8, SIDE), jnp.float32)
             for start in range(0, ROWS, chunk):
                 rows = slice(start, start + chunk)
-                size = sizes[a_at, rows, :] * sizes[b_at, rows, :]
+                size = size_of(rows)
                 if start == 0:
                     edge = lax.broadcasted_iota(jnp.int32, (chunk, SIDE), 0) == 0
                     size = jnp.where(edge, 0.5 * size, size)
@@ -170,14 +186,17 @@
             floor = jnp.sum(total) * (2.0 / (SIDE * SIDE)) + 1e-6
             for start in range(0, ROWS, chunk):
                 rows = slice(start, start + chunk)
-                scale = pl.reciprocal(sizes[a_at, rows, :] * sizes[b_at, rows, :] + floor, approx=True)
-                a = specs[a_at, rows, :].astype(jnp.float32)
-                b = specs[b_at, rows, :].astype(jnp.float32)
+                scale = pl.reciprocal(size_of(rows) + floor, approx=True)
+                a = a_from[0][a_from[2], rows, :].astype(jnp.float32)
+                b = b_from[0][b_from[2], rows, :].astype(jnp.float32)
                 ar, ai, br, bi = a[:, :SIDE], a[:, SIDE:], b[:, :SIDE], b[:, SIDE:]
-                br, bi = br * scale, bi * scale
+                real = (ar * br + ai * bi) * scale
+                imag = (ai * br - ar * bi) * (scale if number < 3 else scale * sign)
                 to = slice(ROWS * (j // 2) + start, ROWS * (j // 2) + start + chunk)
-                power[k, j % 2, to, :SIDE] = (ar * br + ai * bi).astype(jnp.bfloat16)
-                power[k, j % 2, to, SIDE:] = (ai * br - ar * bi).astype(jnp.bfloat16)
+                power[k, j % 2, to, :SIDE] = real.astype(jnp.bfloat16)
+                power[k, j % 2, to, SIDE:] = imag.astype(jnp.bfloat16)
+    for k, pairs in enumerate(STAGES[number][0]):
+        held = NODES * len(pairs)
         used = ROWS * held // 2
         both = sum(
             jnp.dot(power[k, odd, :used, :], fold[odd], preferred_element_type=jnp.float32) for odd in range(2)
@@ -233,10 +252,9 @@
         ratio_y, ratio_x = total[1:2] / total[0:1], total[2:3] / total[0:1]
         for n in range(NODES):
             at = slice(128 * n, 128 * (n + 1))
-            both = jnp.concatenate(
-                [own[n : n + 1] + ratio_y[:, at], own[NODES + n : NODES + n + 1] + ratio_x[:, at]], axis=0
-            )
-            result = jnp.where(lane[:2] == GROUP * first_group + NODES * pair + n, both, result)
+            column = 2 * (GROUP * first_group + NODES * pair + n)
+            result = jnp.where(lane[:1] == column, own[n : n + 1] + ratio_y[:, at], result)
+            result = jnp.where(lane[:1] == column + 1, own[NODES + n : NODES + n + 1] + ratio_x[:, at], result)
     found[...] = result
 
 
@@ -246,7 +264,7 @@
         ((WINDOW * NODES, ROWS, 2 * SIDE), jnp.bfloat16),
         ((WINDOW * NODES, ROWS, SIDE), jnp.float32),
         ((WINDOW, EXTRA, 128), jnp.bfloat16),
-        ((2, 128), jnp.float32),
+        ((1, 128), jnp.float32),
     )
     first = number == 0
     if first:
@@ -264,18 +282,18 @@
         if first:
             held, sems = outs[4 : 4 + count], scratch[-1]
             sources = [*tables_in, *refs[fixed : len(args)]]
-            targets = [*held, *scratch[2:4]]
+            targets = [*held, *scratch[4:6]]
             copies = [pltpu.make_async_copy(a, b, sems.at[k]) for k, (a, b) in enumerate(zip(sources, targets))]
             for copy in copies:
                 copy.start()
             for copy in copies[:2]:
                 copy.wait()
             tables_in = held
-        stage_kernel(number, tables_in, blocks_in, outs[:4], scratch[:2])
+        stage_kernel(number, tables_in, blocks_in, outs[:4], scratch[:4])
         if first:
             for copy in copies[2:]:
                 copy.wait()
-            mesh_rows(*scratch[2:4], *outs[4 + count :], scratch[4])
+            mesh_rows(*scratch[4:6], *outs[4 + count :], scratch[6])
 
     groups = max(len(STAGES[number][0]), 1)
     out = pl.pallas_call(
@@ -289,6 +307,8 @@
         scratch_shapes=[
             pltpu.VMEM((groups, 2, 2 * ROWS, 2 * SIDE), jnp.bfloat16),
             pltpu.VMEM((ROWS, 256 * groups), jnp.float32),
+            pltpu.VMEM((NODES, ROWS, 2 * SIDE), jnp.bfloat16),
+            pltpu.VMEM((NODES, ROWS, SIDE), jnp.float32),
         ]
         + [pltpu.VMEM(x.shape, x.dtype) for x in mesh_inputs]
         + ([pltpu.VMEM((8, 128), jnp.int32), pltpu.SemaphoreType.DMA((count + 2,))] if first else []),
@@ -368,8 +388,9 @@
 
     def shifts_of(member, step, column):
         if (member, step, column) not in spread:
-            values = every[member * tiles + near_tiles[step]][:, column : column + 1]
-            spread[member, step, column] = jnp.broadcast_to(values, (2, 128))
+            values = every[member * tiles + near_tiles[step]]
+            parts = [jnp.broadcast_to(values[:, column + part : column + part + 1], (1, 128)) for part in range(2)]
+            spread[member, step, column] = jnp.concatenate(parts, axis=0)
         return spread[member, step, column]
 
     def put(held, start, row, section, partner, step, source=0):
@@ -377,7 +398,7 @@
         for side in range(2):
             group, number = places[side][(first, first + partner)]
             for n in range(NODES):
-                value = shifts_of(2 * row + side, step, FOUND * source + GROUP * group + NODES * number + n)
+                value = shifts_of(2 * row + side, step, FOUND * source + 2 * (GROUP * group + NODES * number + n))
                 held = jnp.where(lane == start + 2 * side + n, value, held)
         return held
 
@@ -479,9 +500,9 @@
     found = state[3]
 
     near = send(found, (4, 4, -4, -4))
-    rest = jnp.zeros((2, 128 - 2 * FOUND), jnp.float32)
+    rest = jnp.zeros((1, 128 - 2 * FOUND), jnp.float32)
     found = jnp.concatenate([found[:, :FOUND], near[:, :FOUND], rest], axis=1)
-    every = lax.all_to_all(jnp.broadcast_to(found[None], (4 * tiles, 2, 128)), ("member", "tile"), 0, 0)
+    every = lax.all_to_all(jnp.broadcast_to(found[None], (4 * tiles, 1, 128)), ("member", "tile"), 0, 0)
     near_by = [pltpu.with_memory_space_constraint(x, pltpu.VMEM) for x in (every, counts, own_offsets)]
     return finish(*near_by, 4 * groups)
 

time: 62.8 us -> 62.5 us (level)
  no operation moved by 1% of the time
where the time goes in v7:
time: 62.5 us; the launch traced here: 62.2 us
  starting transfers between devices  27.3 us (44%)
  blocking collectives  14.9 us (24%)
  Pallas kernels  9.92 us (16%)
  waiting for transfers between devices  9.33 us (15%)
  between operations  0.73 us (1%)
    ppermute x6, starting transfers between devices, send(): return lax.ppermute(value, ('group', 'member'), pairs)  27.3 us
    all_to_all x1, blocking collectives, shards(): lax.all_to_all(jnp.broadcast_to(found[None], (4 * tiles, 1, 128)), ('memb...  14.9 us
    ppermute x6, waiting for transfers between devices, send(): return lax.ppermute(value, ('group', 'member'), pairs)  9.33 us
    pallas_call x4, Pallas kernels, run_stage(): pl.pallas_call(kernel, out_shape=tuple((pltpu.VMEM(shape, dtype) for shap...  7.45 us
    pallas_call x1, Pallas kernels, prepare(): pl.pallas_call(prepare_kernel, out_shape=tuple((pltpu.VMEM(shape, jnp.bfl...  1.26 us
  transfers between devices with their start and end apart: 6, of which 3 were waited for; matrix products, arithmetic and copies ran while one was open for 0% of the time, Pallas kernels for 9%

profile of v7, /device:TPU:6, one launch (start us, length us, event | category | flops | bytes accessed | tf_op | source)
XLA Modules:
  0.0 62.2 jit_solution(7900566096724100256)
XLA Ops:
  0.6 1.3 %prepare.1 = (bf16[1040,128]{1,0:T(8,128)(2,1)S(1)}, bf16[1040,128]{1,0:T(8,128)(2,1)S(1)}, bf16[528,256]{1,0:T(8,128)(2,1)S(1)}, bf16[528,256]{1,0:T(8,128)(2,1)S(1)}) custom-call(bf16[4,512,256]{2,1,0:T(8,128)(2,1)} %bitcast.10, s32[2,2,1,8]{3,2,1,0:T(1,128)} %refs_8_.1), custom_call_target="tpu_custom_call" | custom-call | flops 1 | bytes 1 | tf_op jit(solution)/shard_map/prepare/pallas_call | solution.py:365
  1.9 7.7 %collective-permute-start.4 = (bf16[528,256]{1,0:T(8,128)(2,1)S(1)}, bf16[528,256]{1,0:T(8,128)(2,1)S(1)}, u32[]{:S(2)}, u32[]{:S(2)}) collective-permute-start(bf16[528,256]{1,0:T(8,128)(2,1)S(1)} %get-tuple-element.34), channel_id=1, source_target_pairs={{0,8},{4,12},{8,0},{12,4},{16,24},{20,28},{24,16},{28,20},{32,40},... | collective-permute-start | bytes 811016 | tf_op jit(solution)/shard_map/ppermute | solution.py:487
  9.6 1.9 %collective-permute-start.1 = (bf16[528,256]{1,0:T(8,128)(2,1)S(1)}, bf16[528,256]{1,0:T(8,128)(2,1)S(1)}, u32[]{:S(2)}, u32[]{:S(2)}) collective-permute-start(bf16[528,256]{1,0:T(8,128)(2,1)S(1)} %get-tuple-element.32), channel_id=1, source_target_pairs={{0,12},{4,8},{8,4},{12,0},{16,28},{20,24},{24,20},{28,16},{32,44},... | collective-permute-start | bytes 811016 | tf_op jit(solution)/shard_map/ppermute | solution.py:487
  11.6 11.2 %collective-permute-start = (bf16[1040,128]{1,0:T(8,128)(2,1)S(1)}, bf16[1040,128]{1,0:T(8,128)(2,1)S(1)}, u32[]{:S(2)}, u32[]{:S(2)}) collective-permute-start(bf16[1040,128]{1,0:T(8,128)(2,1)S(1)} %get-tuple-element.26.refs_5_), channel_id=1, source_target_pairs={{8,24},{12,28},{16,0},{20,4},{24,40},{28,44},{32,16},{36,20},{40,5... | collective-permute-start | bytes 798728 | tf_op jit(solution)/shard_map/ppermute | solution.py:487
  22.8 2.0 %collective-permute-start.2 = (bf16[1040,128]{1,0:T(8,128)(2,1)S(1)}, bf16[1040,128]{1,0:T(8,128)(2,1)S(1)}, u32[]{:S(2)}, u32[]{:S(2)}) collective-permute-start(bf16[1040,128]{1,0:T(8,128)(2,1)S(1)} %get-tuple-element.33), channel_id=1, source_target_pairs={{8,28},{12,24},{16,4},{20,0},{24,44},{28,40},{32,20},{36,16},{40,6... | collective-permute-start | bytes 798728 | tf_op jit(solution)/shard_map/ppermute | solution.py:487
  24.8 2.5 %collective-permute-start.3 = (bf16[1040,128]{1,0:T(8,128)(2,1)S(1)}, bf16[1040,128]{1,0:T(8,128)(2,1)S(1)}, u32[]{:S(2)}, u32[]{:S(2)}) collective-permute-start(bf16[1040,128]{1,0:T(8,128)(2,1)S(1)} %get-tuple-element.33), channel_id=1, source_target_pairs={{0,4},{4,0},{8,12},{12,8},{16,20},{20,16},{24,28},{28,24},{32,36},... | collective-permute-start | bytes 798728 | tf_op jit(solution)/shard_map/ppermute | solution.py:487
  27.3 2.2 %collective-permute-done.refs_6_ = bf16[1040,128]{1,0:T(8,128)(2,1)S(1)} collective-permute-done((bf16[1040,128]{1,0:T(8,128)(2,1)S(1)}, bf16[1040,128]{1,0:T(8,128)(2,1)S(1)}, u32[]{:S(2)}, u32[]{:S(2)}) %collective-permute-start) | collective-permute-done | bytes 266272 | tf_op jit(solution)/shard_map/ppermute | solution.py:487
  29.5 1.9 %stage0.1 = (bf16[12,144,512]{2,1,0:T(8,128)(2,1)S(1)}, f32[12,144,256]{2,1,0:T(8,128)S(1)}, bf16[6,16,128]{2,1,0:T(8,128)(2,1)S(1)}, f32[1,128]{1,0:T(1,128)S(1...) custom-call(bf16[256,256]{1,0:T(8,128)(2,1)} %constant.12.clone.refs, ...), custom_call_target="tpu_custom_call" | custom-call | flops 1 | bytes 1 | tf_op jit(solution)/shard_map/stage0/pallas_call | solution.py:299
  31.5 0.0 collective-permute-done.4.refs_5_
  31.5 1.5 %stage1.1 = (bf16[12,144,512]{2,1,0:T(8,128)(2,1)S(1)}, f32[12,144,256]{2,1,0:T(8,128)S(1)}, bf16[6,16,128]{2,1,0:T(8,128)(2,1)S(1)}, f32[1,128]{1,0:T(1,128)S(1)}) custom-call(bf16[256,256]{1,0:T(8,128)(2,1)S(1)} %get-tuple-element.27.refs_0_, ...), custom_call_target="tpu_custom_call", output_to_operand_aliasing={{0}: (6, {}), {1}: (7, {}), {2}: (8, {}), {3}: (9, {})} | custom-call | flops 1 | bytes 1 | tf_op jit(solution)/shard_map/stage1/pallas_call | solution.py:299
  33.0 1.5 %collective-permute-done.2.refs_5_ = bf16[1040,128]{1,0:T(8,128)(2,1)S(1)} collective-permute-done((bf16[1040,128]{1,0:T(8,128)(2,1)S(1)}, bf16[1040,128]{1,0:T(8,128)(2,1)S(1)}, u32[]{:S(2)}, u32[]{:S(2)}) %collective-permute-start.2) | collective-permute-done | bytes 266272 | tf_op jit(solution)/shard_map/ppermute | solution.py:487
  34.5 0.0 collective-permute-done.3.refs_6_
  34.5 2.0 %stage2.1 = (bf16[12,144,512]{2,1,0:T(8,128)(2,1)S(1)}, f32[12,144,256]{2,1,0:T(8,128)S(1)}, bf16[6,16,128]{2,1,0:T(8,128)(2,1)S(1)}, f32[1,128]{1,0:T(1,128)S(1)}) custom-call(bf16[256,256]{1,0:T(8,128)(2,1)S(1)} %get-tuple-element.27.refs_0_, ...), custom_call_target="tpu_custom_call", output_to_operand_aliasing={{0}: (7, {}), {1}: (8, {}), {2}: (9, {}), {3}: (10, {})} | custom-call | flops 1 | bytes 1 | tf_op jit(solution)/shard_map/stage2/pallas_call | solution.py:299
  36.5 0.0 collective-permute-done.1.refs_5_
  36.5 1.9 %stage3.1 = (bf16[12,144,512]{2,1,0:T(8,128)(2,1)S(1)}, f32[12,144,256]{2,1,0:T(8,128)S(1)}, bf16[6,16,128]{2,1,0:T(8,128)(2,1)S(1)}, f32[1,128]{1,0:T(1,128)S(1)}) custom-call(bf16[256,256]{1,0:T(8,128)(2,1)S(1)} %get-tuple-element.27.refs_0_, ...), custom_call_target="tpu_custom_call", output_to_operand_aliasing={{0}: (6, {}), {1}: (7, {}), {2}: (8, {}), {3}: (9, {})} | custom-call | flops 1 | bytes 1 | tf_op jit(solution)/shard_map/stage3/pallas_call | solution.py:299
  38.5 1.9 %collective-permute-start.5 = (f32[1,128]{1,0:T(1,128)S(1)}, f32[1,128]{1,0:T(1,128)S(1)}, u32[]{:S(2)}, u32[]{:S(2)}) collective-permute-start(f32[1,128]{1,0:T(1,128)S(1)} %get-tuple-element.47), channel_id=1, source_target_pairs={{0,16},{4,20},{16,32},{20,36},{24,8},{28,12},{32,48},{36,52},{40,2... | collective-permute-start | bytes 1544 | tf_op jit(solution)/shard_map/ppermute | solution.py:487
  40.4 5.6 %collective-permute-done.5 = f32[1,128]{1,0:T(1,128)S(1)} collective-permute-done((f32[1,128]{1,0:T(1,128)S(1)}, f32[1,128]{1,0:T(1,128)S(1)}, u32[]{:S(2)}, u32[]{:S(2)}) %collective-permute-start.5) | collective-permute-done | bytes 544 | tf_op jit(solution)/shard_map/ppermute | solution.py:487
  46.0 0.1 fusion
  46.1 14.9 %all_to_all.5.every = f32[16,1,128]{2,1,0:T(1,128)S(1)} all-to-all(f32[16,1,128]{2,1,0:T(1,128)S(1)} %broadcast_in_dim.13), channel_id=1, replica_groups=mesh['group'=32,'member'=4,'tile'=4] {'member','tile'}, dimensions={0} | all-to-all | bytes 16384 | tf_op jit(solution)/shard_map/all_to_all | solution.py:505
  61.0 1.2 %finish.1 = (f32[2,2,1,8]{3,2,1,0:T(1,128)}, f32[2,1,8]{2,1,0:T(1,128)}) custom-call(f32[16,1,128]{2,1,0:T(1,128)S(1)} %all_to_all.5.every, f32[16,128]{1,0:T(8,128)S(1)} %get-tuple-element.48.counts, f32[8,128]{1,0:T(8,128)S(1)} %get-tuple-element.49.offsets), custom_call_target="tpu_custom_call" | custom-call | flops 1 | bytes 1 | tf_op jit(solution)/shard_map/finish/pallas_call | solution.py:469
  (2 shorter events, 0.0 us)
Async XLA Ops:
  1.9 29.6 %collective-permute-start.4 = (bf16[528,256]{1,0:T(8,128)(2,1)S(1)}, bf16[528,256]{1,0:T(8,128)(2,1)S(1)}, u32[]{:S(2)}, u32[]{:S(2)}) collective-permute-start(bf16[528,256]{1,0:T(8,128)(2,1)S(1)} %get-tuple-element.34), channel_id=1, source_target_pairs={{0,8},{4,12},{8,0},{12,4},{16,24},{20,28},{24,16},{28,20},{32,40},... | collective-permute-start | bytes 811016 | tf_op jit(solution)/shard_map/ppermute | solution.py:487
  9.6 26.9 %collective-permute-start.1 = (bf16[528,256]{1,0:T(8,128)(2,1)S(1)}, bf16[528,256]{1,0:T(8,128)(2,1)S(1)}, u32[]{:S(2)}, u32[]{:S(2)}) collective-permute-start(bf16[528,256]{1,0:T(8,128)(2,1)S(1)} %get-tuple-element.32), channel_id=1, source_target_pairs={{0,12},{4,8},{8,4},{12,0},{16,28},{20,24},{24,20},{28,16},{32,44},... | collective-permute-start | bytes 811016 | tf_op jit(solution)/shard_map/ppermute | solution.py:487
  11.6 17.9 %collective-permute-start = (bf16[1040,128]{1,0:T(8,128)(2,1)S(1)}, bf16[1040,128]{1,0:T(8,128)(2,1)S(1)}, u32[]{:S(2)}, u32[]{:S(2)}) collective-permute-start(bf16[1040,128]{1,0:T(8,128)(2,1)S(1)} %get-tuple-element.26.refs_5_), channel_id=1, source_target_pairs={{8,24},{12,28},{16,0},{20,4},{24,40},{28,44},{32,16},{36,20},{40,5... | collective-permute-start | bytes 798728 | tf_op jit(solution)/shard_map/ppermute | solution.py:487
  22.8 11.7 %collective-permute-start.2 = (bf16[1040,128]{1,0:T(8,128)(2,1)S(1)}, bf16[1040,128]{1,0:T(8,128)(2,1)S(1)}, u32[]{:S(2)}, u32[]{:S(2)}) collective-permute-start(bf16[1040,128]{1,0:T(8,128)(2,1)S(1)} %get-tuple-element.33), channel_id=1, source_target_pairs={{8,28},{12,24},{16,4},{20,0},{24,44},{28,40},{32,20},{36,16},{40,6... | collective-permute-start | bytes 798728 | tf_op jit(solution)/shard_map/ppermute | solution.py:487
  24.8 9.7 %collective-permute-start.3 = (bf16[1040,128]{1,0:T(8,128)(2,1)S(1)}, bf16[1040,128]{1,0:T(8,128)(2,1)S(1)}, u32[]{:S(2)}, u32[]{:S(2)}) collective-permute-start(bf16[1040,128]{1,0:T(8,128)(2,1)S(1)} %get-tuple-element.33), channel_id=1, source_target_pairs={{0,4},{4,0},{8,12},{12,8},{16,20},{20,16},{24,28},{28,24},{32,36},... | collective-permute-start | bytes 798728 | tf_op jit(solution)/shard_map/ppermute | solution.py:487
  38.5 7.5 %collective-permute-start.5 = (f32[1,128]{1,0:T(1,128)S(1)}, f32[1,128]{1,0:T(1,128)S(1)}, u32[]{:S(2)}, u32[]{:S(2)}) collective-permute-start(f32[1,128]{1,0:T(1,128)S(1)} %get-tuple-element.47), channel_id=1, source_target_pairs={{0,16},{4,20},{16,32},{20,36},{24,8},{28,12},{32,48},{36,52},{40,2... | collective-permute-start | bytes 1544 | tf_op jit(solution)/shard_map/ppermute | solution.py:487

commit v8 on v7

--- a/solution.py
+++ b/solution.py
@@ -336,6 +336,8 @@
     device = lax.axis_index("member")
     row, side = device // 2, lax.rem(device, 2)
     numbers = [2 * r + s for r in (row, 1 - row) for s in (side, 1 - side)]
+    offsets_copy = pltpu.make_async_copy(all_offsets, offsets, sems.at[6])
+    offsets_copy.start()
     copies = []
     for k in (2, 3, 0, 1):
         block, width = blocks[k], blocks[k].shape[1]
@@ -344,8 +346,6 @@
             target = block.at[pl.ds(half * NODES * SIDE, NODES * SIDE)]
             copies.append(pltpu.make_async_copy(source, target, sems.at[len(copies)]))
             copies[-1].start()
-    offsets_copy = pltpu.make_async_copy(all_offsets, offsets, sems.at[6])
-    offsets_copy.start()
     offsets_copy.wait()
     line = lax.broadcasted_iota(jnp.int32, (EXTRA, 128), 0)
     for block, number in zip(blocks, numbers):
@@ -380,6 +380,7 @@
     device, tile = lax.axis_index("member"), lax.axis_index("tile")
     position = 4 * lax.axis_index("group") + device
     lane = lax.broadcasted_iota(jnp.int32, (2, 128), 1)
+    part_row = lax.broadcasted_iota(jnp.int32, (2, 128), 0)
     own = slice(NODE_COLS, 3 * NODE_COLS)
     tiles = lax.axis_size("tile")
     places = [pair_places(side) for side in range(2)]
@@ -389,8 +390,8 @@
     def shifts_of(member, step, column):
         if (member, step, column) not in spread:
             values = every[member * tiles + near_tiles[step]]
-            parts = [jnp.broadcast_to(values[:, column + part : column + part + 1], (1, 128)) for part in range(2)]
-            spread[member, step, column] = jnp.concatenate(parts, axis=0)
+            parts = [jnp.broadcast_to(values[:, column + part : column + part + 1], (2, 128)) for part in range(2)]
+            spread[member, step, column] = jnp.where(part_row == 0, *parts)
         return spread[member, step, column]
 
     def put(held, start, row, section, partner, step, source=0):

time: 62.5 us -> 62.5 us (level)
  no operation moved by 1% of the time
where the time goes in v8:
time: 62.5 us; the launch traced here: 62.2 us
  starting transfers between devices  27.3 us (44%)
  blocking collectives  14.9 us (24%)
  Pallas kernels  9.92 us (16%)
  waiting for transfers between devices  9.32 us (15%)
  between operations  0.73 us (1%)
    ppermute x6, starting transfers between devices, send(): return lax.ppermute(value, ('group', 'member'), pairs)  27.3 us
    all_to_all x1, blocking collectives, shards(): lax.all_to_all(jnp.broadcast_to(found[None], (4 * tiles, 1, 128)), ('memb...  14.9 us
    ppermute x6, waiting for transfers between devices, send(): return lax.ppermute(value, ('group', 'member'), pairs)  9.32 us
    pallas_call x4, Pallas kernels, run_stage(): pl.pallas_call(kernel, out_shape=tuple((pltpu.VMEM(shape, dtype) for shap...  7.45 us
    pallas_call x1, Pallas kernels, prepare(): pl.pallas_call(prepare_kernel, out_shape=tuple((pltpu.VMEM(shape, jnp.bfl...  1.26 us
  transfers between devices with their start and end apart: 6, of which 3 were waited for; matrix products, arithmetic and copies ran while one was open for 0% of the time, Pallas kernels for 9%

profile of v8, /device:TPU:6, one launch (start us, length us, event | category | flops | bytes accessed | tf_op | source)
XLA Modules:
  0.0 62.2 jit_solution(8454881152162476784)
XLA Ops:
  0.6 1.3 %prepare.1 = (bf16[1040,128]{1,0:T(8,128)(2,1)S(1)}, bf16[1040,128]{1,0:T(8,128)(2,1)S(1)}, bf16[528,256]{1,0:T(8,128)(2,1)S(1)}, bf16[528,256]{1,0:T(8,128)(2,1)S(1)}) custom-call(bf16[4,512,256]{2,1,0:T(8,128)(2,1)} %bitcast.10, s32[2,2,1,8]{3,2,1,0:T(1,128)} %refs_8_.1), custom_call_target="tpu_custom_call" | custom-call | flops 1 | bytes 1 | tf_op jit(solution)/shard_map/prepare/pallas_call | solution.py:365
  1.9 7.7 %collective-permute-start.4 = (bf16[528,256]{1,0:T(8,128)(2,1)S(1)}, bf16[528,256]{1,0:T(8,128)(2,1)S(1)}, u32[]{:S(2)}, u32[]{:S(2)}) collective-permute-start(bf16[528,256]{1,0:T(8,128)(2,1)S(1)} %get-tuple-element.34), channel_id=1, source_target_pairs={{0,8},{4,12},{8,0},{12,4},{16,24},{20,28},{24,16},{28,20},{32,40},... | collective-permute-start | bytes 811016 | tf_op jit(solution)/shard_map/ppermute | solution.py:488
  9.6 1.9 %collective-permute-start.1 = (bf16[528,256]{1,0:T(8,128)(2,1)S(1)}, bf16[528,256]{1,0:T(8,128)(2,1)S(1)}, u32[]{:S(2)}, u32[]{:S(2)}) collective-permute-start(bf16[528,256]{1,0:T(8,128)(2,1)S(1)} %get-tuple-element.32), channel_id=1, source_target_pairs={{0,12},{4,8},{8,4},{12,0},{16,28},{20,24},{24,20},{28,16},{32,44},... | collective-permute-start | bytes 811016 | tf_op jit(solution)/shard_map/ppermute | solution.py:488
  11.6 11.2 %collective-permute-start = (bf16[1040,128]{1,0:T(8,128)(2,1)S(1)}, bf16[1040,128]{1,0:T(8,128)(2,1)S(1)}, u32[]{:S(2)}, u32[]{:S(2)}) collective-permute-start(bf16[1040,128]{1,0:T(8,128)(2,1)S(1)} %get-tuple-element.26.refs_5_), channel_id=1, source_target_pairs={{8,24},{12,28},{16,0},{20,4},{24,40},{28,44},{32,16},{36,20},{40,5... | collective-permute-start | bytes 798728 | tf_op jit(solution)/shard_map/ppermute | solution.py:488
  22.8 2.0 %collective-permute-start.2 = (bf16[1040,128]{1,0:T(8,128)(2,1)S(1)}, bf16[1040,128]{1,0:T(8,128)(2,1)S(1)}, u32[]{:S(2)}, u32[]{:S(2)}) collective-permute-start(bf16[1040,128]{1,0:T(8,128)(2,1)S(1)} %get-tuple-element.33), channel_id=1, source_target_pairs={{8,28},{12,24},{16,4},{20,0},{24,44},{28,40},{32,20},{36,16},{40,6... | collective-permute-start | bytes 798728 | tf_op jit(solution)/shard_map/ppermute | solution.py:488
  24.8 2.5 %collective-permute-start.3 = (bf16[1040,128]{1,0:T(8,128)(2,1)S(1)}, bf16[1040,128]{1,0:T(8,128)(2,1)S(1)}, u32[]{:S(2)}, u32[]{:S(2)}) collective-permute-start(bf16[1040,128]{1,0:T(8,128)(2,1)S(1)} %get-tuple-element.33), channel_id=1, source_target_pairs={{0,4},{4,0},{8,12},{12,8},{16,20},{20,16},{24,28},{28,24},{32,36},... | collective-permute-start | bytes 798728 | tf_op jit(solution)/shard_map/ppermute | solution.py:488
  27.3 2.2 %collective-permute-done.refs_6_ = bf16[1040,128]{1,0:T(8,128)(2,1)S(1)} collective-permute-done((bf16[1040,128]{1,0:T(8,128)(2,1)S(1)}, bf16[1040,128]{1,0:T(8,128)(2,1)S(1)}, u32[]{:S(2)}, u32[]{:S(2)}) %collective-permute-start) | collective-permute-done | bytes 266272 | tf_op jit(solution)/shard_map/ppermute | solution.py:488
  29.5 1.9 %stage0.1 = (bf16[12,144,512]{2,1,0:T(8,128)(2,1)S(1)}, f32[12,144,256]{2,1,0:T(8,128)S(1)}, bf16[6,16,128]{2,1,0:T(8,128)(2,1)S(1)}, f32[1,128]{1,0:T(1,128)S(1...) custom-call(bf16[256,256]{1,0:T(8,128)(2,1)} %constant.12.clone.refs, ...), custom_call_target="tpu_custom_call" | custom-call | flops 1 | bytes 1 | tf_op jit(solution)/shard_map/stage0/pallas_call | solution.py:299
  31.5 0.0 collective-permute-done.4.refs_5_
  31.5 1.6 %stage1.1 = (bf16[12,144,512]{2,1,0:T(8,128)(2,1)S(1)}, f32[12,144,256]{2,1,0:T(8,128)S(1)}, bf16[6,16,128]{2,1,0:T(8,128)(2,1)S(1)}, f32[1,128]{1,0:T(1,128)S(1)}) custom-call(bf16[256,256]{1,0:T(8,128)(2,1)S(1)} %get-tuple-element.27.refs_0_, ...), custom_call_target="tpu_custom_call", output_to_operand_aliasing={{0}: (6, {}), {1}: (7, {}), {2}: (8, {}), {3}: (9, {})} | custom-call | flops 1 | bytes 1 | tf_op jit(solution)/shard_map/stage1/pallas_call | solution.py:299
  33.0 1.5 %collective-permute-done.2.refs_5_ = bf16[1040,128]{1,0:T(8,128)(2,1)S(1)} collective-permute-done((bf16[1040,128]{1,0:T(8,128)(2,1)S(1)}, bf16[1040,128]{1,0:T(8,128)(2,1)S(1)}, u32[]{:S(2)}, u32[]{:S(2)}) %collective-permute-start.2) | collective-permute-done | bytes 266272 | tf_op jit(solution)/shard_map/ppermute | solution.py:488
  34.5 0.0 collective-permute-done.3.refs_6_
  34.5 2.0 %stage2.1 = (bf16[12,144,512]{2,1,0:T(8,128)(2,1)S(1)}, f32[12,144,256]{2,1,0:T(8,128)S(1)}, bf16[6,16,128]{2,1,0:T(8,128)(2,1)S(1)}, f32[1,128]{1,0:T(1,128)S(1)}) custom-call(bf16[256,256]{1,0:T(8,128)(2,1)S(1)} %get-tuple-element.27.refs_0_, ...), custom_call_target="tpu_custom_call", output_to_operand_aliasing={{0}: (7, {}), {1}: (8, {}), {2}: (9, {}), {3}: (10, {})} | custom-call | flops 1 | bytes 1 | tf_op jit(solution)/shard_map/stage2/pallas_call | solution.py:299
  36.5 0.0 collective-permute-done.1.refs_5_
  36.5 1.9 %stage3.1 = (bf16[12,144,512]{2,1,0:T(8,128)(2,1)S(1)}, f32[12,144,256]{2,1,0:T(8,128)S(1)}, bf16[6,16,128]{2,1,0:T(8,128)(2,1)S(1)}, f32[1,128]{1,0:T(1,128)S(1)}) custom-call(bf16[256,256]{1,0:T(8,128)(2,1)S(1)} %get-tuple-element.27.refs_0_, ...), custom_call_target="tpu_custom_call", output_to_operand_aliasing={{0}: (6, {}), {1}: (7, {}), {2}: (8, {}), {3}: (9, {})} | custom-call | flops 1 | bytes 1 | tf_op jit(solution)/shard_map/stage3/pallas_call | solution.py:299
  38.5 1.9 %collective-permute-start.5 = (f32[1,128]{1,0:T(1,128)S(1)}, f32[1,128]{1,0:T(1,128)S(1)}, u32[]{:S(2)}, u32[]{:S(2)}) collective-permute-start(f32[1,128]{1,0:T(1,128)S(1)} %get-tuple-element.47), channel_id=1, source_target_pairs={{0,16},{4,20},{16,32},{20,36},{24,8},{28,12},{32,48},{36,52},{40,2... | collective-permute-start | bytes 1544 | tf_op jit(solution)/shard_map/ppermute | solution.py:488
  40.4 5.6 %collective-permute-done.5 = f32[1,128]{1,0:T(1,128)S(1)} collective-permute-done((f32[1,128]{1,0:T(1,128)S(1)}, f32[1,128]{1,0:T(1,128)S(1)}, u32[]{:S(2)}, u32[]{:S(2)}) %collective-permute-start.5) | collective-permute-done | bytes 544 | tf_op jit(solution)/shard_map/ppermute | solution.py:488
  46.0 0.1 fusion
  46.1 14.9 %all_to_all.5.every = f32[16,1,128]{2,1,0:T(1,128)S(1)} all-to-all(f32[16,1,128]{2,1,0:T(1,128)S(1)} %broadcast_in_dim.13), channel_id=1, replica_groups=mesh['group'=32,'member'=4,'tile'=4] {'member','tile'}, dimensions={0} | all-to-all | bytes 16384 | tf_op jit(solution)/shard_map/all_to_all | solution.py:506
  61.0 1.2 %finish.1 = (f32[2,2,1,8]{3,2,1,0:T(1,128)}, f32[2,1,8]{2,1,0:T(1,128)}) custom-call(f32[16,1,128]{2,1,0:T(1,128)S(1)} %all_to_all.5.every, f32[16,128]{1,0:T(8,128)S(1)} %get-tuple-element.48.counts, f32[8,128]{1,0:T(8,128)S(1)} %get-tuple-element.49.offsets), custom_call_target="tpu_custom_call" | custom-call | flops 1 | bytes 1 | tf_op jit(solution)/shard_map/finish/pallas_call | solution.py:470
  (2 shorter events, 0.0 us)
Async XLA Ops:
  1.9 29.6 %collective-permute-start.4 = (bf16[528,256]{1,0:T(8,128)(2,1)S(1)}, bf16[528,256]{1,0:T(8,128)(2,1)S(1)}, u32[]{:S(2)}, u32[]{:S(2)}) collective-permute-start(bf16[528,256]{1,0:T(8,128)(2,1)S(1)} %get-tuple-element.34), channel_id=1, source_target_pairs={{0,8},{4,12},{8,0},{12,4},{16,24},{20,28},{24,16},{28,20},{32,40},... | collective-permute-start | bytes 811016 | tf_op jit(solution)/shard_map/ppermute | solution.py:488
  9.6 26.9 %collective-permute-start.1 = (bf16[528,256]{1,0:T(8,128)(2,1)S(1)}, bf16[528,256]{1,0:T(8,128)(2,1)S(1)}, u32[]{:S(2)}, u32[]{:S(2)}) collective-permute-start(bf16[528,256]{1,0:T(8,128)(2,1)S(1)} %get-tuple-element.32), channel_id=1, source_target_pairs={{0,12},{4,8},{8,4},{12,0},{16,28},{20,24},{24,20},{28,16},{32,44},... | collective-permute-start | bytes 811016 | tf_op jit(solution)/shard_map/ppermute | solution.py:488
  11.6 17.9 %collective-permute-start = (bf16[1040,128]{1,0:T(8,128)(2,1)S(1)}, bf16[1040,128]{1,0:T(8,128)(2,1)S(1)}, u32[]{:S(2)}, u32[]{:S(2)}) collective-permute-start(bf16[1040,128]{1,0:T(8,128)(2,1)S(1)} %get-tuple-element.26.refs_5_), channel_id=1, source_target_pairs={{8,24},{12,28},{16,0},{20,4},{24,40},{28,44},{32,16},{36,20},{40,5... | collective-permute-start | bytes 798728 | tf_op jit(solution)/shard_map/ppermute | solution.py:488
  22.8 11.7 %collective-permute-start.2 = (bf16[1040,128]{1,0:T(8,128)(2,1)S(1)}, bf16[1040,128]{1,0:T(8,128)(2,1)S(1)}, u32[]{:S(2)}, u32[]{:S(2)}) collective-permute-start(bf16[1040,128]{1,0:T(8,128)(2,1)S(1)} %get-tuple-element.33), channel_id=1, source_target_pairs={{8,28},{12,24},{16,4},{20,0},{24,44},{28,40},{32,20},{36,16},{40,6... | collective-permute-start | bytes 798728 | tf_op jit(solution)/shard_map/ppermute | solution.py:488
  24.8 9.7 %collective-permute-start.3 = (bf16[1040,128]{1,0:T(8,128)(2,1)S(1)}, bf16[1040,128]{1,0:T(8,128)(2,1)S(1)}, u32[]{:S(2)}, u32[]{:S(2)}) collective-permute-start(bf16[1040,128]{1,0:T(8,128)(2,1)S(1)} %get-tuple-element.33), channel_id=1, source_target_pairs={{0,4},{4,0},{8,12},{12,8},{16,20},{20,16},{24,28},{28,24},{32,36},... | collective-permute-start | bytes 798728 | tf_op jit(solution)/shard_map/ppermute | solution.py:488
  38.5 7.5 %collective-permute-start.5 = (f32[1,128]{1,0:T(1,128)S(1)}, f32[1,128]{1,0:T(1,128)S(1)}, u32[]{:S(2)}, u32[]{:S(2)}) collective-permute-start(f32[1,128]{1,0:T(1,128)S(1)} %get-tuple-element.47), channel_id=1, source_target_pairs={{0,16},{4,20},{16,32},{20,36},{24,8},{28,12},{32,48},{36,52},{40,2... | collective-permute-start | bytes 1544 | tf_op jit(solution)/shard_map/ppermute | solution.py:488

commit v9 on v8

--- a/solution.py
+++ b/solution.py
@@ -86,7 +86,7 @@
     low = (close - high.astype(np.float32)).astype(ml_dtypes.bfloat16)
     lane, wide = np.arange(128)[:, None], np.arange(256)[None, :]
     spread = ((lane // 64 == wide // 128) & (lane % 64 < SPAN)).astype(ml_dtypes.bfloat16)
-    return right, left, fold, np.concatenate([high, low], axis=0), spread
+    return right, left, fold, np.concatenate([high, high, low], axis=1), spread
 
 
 def transform(patch, right, left):
@@ -209,9 +209,8 @@
     sums = folded[...]
     high = sums.astype(jnp.bfloat16)
     low = (sums - high.astype(jnp.float32)).astype(jnp.bfloat16)
-    closed = jnp.dot(close[...], high, preferred_element_type=jnp.float32)
-    rest = jnp.dot(close[: 2 * SPAN], low, preferred_element_type=jnp.float32)
-    closed = closed[: 2 * SPAN] + closed[2 * SPAN :] + rest
+    parts = jnp.concatenate([high, low, high], axis=0)
+    closed = jnp.dot(close[...], parts, preferred_element_type=jnp.float32)
     lane = lax.broadcasted_iota(jnp.int32, (SPAN, 128), 1)
     step_u = ((lane & (SPAN - 1)) - REACH).astype(jnp.float32)
     step_v = (lax.broadcasted_iota(jnp.int32, (SPAN, 128), 0) - REACH).astype(jnp.float32)

time: 62.5 us -> 62.6 us (level)
  no operation moved by 1% of the time
where the time goes in v9:
time: 62.6 us; the launch traced here: 62.2 us
  starting transfers between devices  27.3 us (44%)
  blocking collectives  14.8 us (24%)
  Pallas kernels  9.98 us (16%)
  waiting for transfers between devices  9.31 us (15%)
  between operations  0.73 us (1%)
    ppermute x6, starting transfers between devices, send(): return lax.ppermute(value, ('group', 'member'), pairs)  27.3 us
    all_to_all x1, blocking collectives, shards(): lax.all_to_all(jnp.broadcast_to(found[None], (4 * tiles, 1, 128)), ('memb...  14.8 us
    ppermute x6, waiting for transfers between devices, send(): return lax.ppermute(value, ('group', 'member'), pairs)  9.31 us
    pallas_call x4, Pallas kernels, run_stage(): pl.pallas_call(kernel, out_shape=tuple((pltpu.VMEM(shape, dtype) for shap...  7.51 us
    pallas_call x1, Pallas kernels, prepare(): pl.pallas_call(prepare_kernel, out_shape=tuple((pltpu.VMEM(shape, jnp.bfl...  1.26 us
  transfers between devices with their start and end apart: 6, of which 3 were waited for; matrix products, arithmetic and copies ran while one was open for 0% of the time, Pallas kernels for 9%

profile of v9, /device:TPU:6, one launch (start us, length us, event | category | flops | bytes accessed | tf_op | source)
XLA Modules:
  0.0 62.2 jit_solution(18264375477820340958)
XLA Ops:
  0.6 1.3 %prepare.1 = (bf16[1040,128]{1,0:T(8,128)(2,1)S(1)}, bf16[1040,128]{1,0:T(8,128)(2,1)S(1)}, bf16[528,256]{1,0:T(8,128)(2,1)S(1)}, bf16[528,256]{1,0:T(8,128)(2,1)S(1)}) custom-call(bf16[4,512,256]{2,1,0:T(8,128)(2,1)} %bitcast.10, s32[2,2,1,8]{3,2,1,0:T(1,128)} %refs_8_.1), custom_call_target="tpu_custom_call" | custom-call | flops 1 | bytes 1 | tf_op jit(solution)/shard_map/prepare/pallas_call | solution.py:364
  1.9 7.7 %collective-permute-start.4 = (bf16[528,256]{1,0:T(8,128)(2,1)S(1)}, bf16[528,256]{1,0:T(8,128)(2,1)S(1)}, u32[]{:S(2)}, u32[]{:S(2)}) collective-permute-start(bf16[528,256]{1,0:T(8,128)(2,1)S(1)} %get-tuple-element.34), channel_id=1, source_target_pairs={{0,8},{4,12},{8,0},{12,4},{16,24},{20,28},{24,16},{28,20},{32,40},... | collective-permute-start | bytes 811016 | tf_op jit(solution)/shard_map/ppermute | solution.py:487
  9.6 1.9 %collective-permute-start.1 = (bf16[528,256]{1,0:T(8,128)(2,1)S(1)}, bf16[528,256]{1,0:T(8,128)(2,1)S(1)}, u32[]{:S(2)}, u32[]{:S(2)}) collective-permute-start(bf16[528,256]{1,0:T(8,128)(2,1)S(1)} %get-tuple-element.32), channel_id=1, source_target_pairs={{0,12},{4,8},{8,4},{12,0},{16,28},{20,24},{24,20},{28,16},{32,44},... | collective-permute-start | bytes 811016 | tf_op jit(solution)/shard_map/ppermute | solution.py:487
  11.6 11.2 %collective-permute-start = (bf16[1040,128]{1,0:T(8,128)(2,1)S(1)}, bf16[1040,128]{1,0:T(8,128)(2,1)S(1)}, u32[]{:S(2)}, u32[]{:S(2)}) collective-permute-start(bf16[1040,128]{1,0:T(8,128)(2,1)S(1)} %get-tuple-element.26.refs_5_), channel_id=1, source_target_pairs={{8,24},{12,28},{16,0},{20,4},{24,40},{28,44},{32,16},{36,20},{40,5... | collective-permute-start | bytes 798728 | tf_op jit(solution)/shard_map/ppermute | solution.py:487
  22.8 2.0 %collective-permute-start.2 = (bf16[1040,128]{1,0:T(8,128)(2,1)S(1)}, bf16[1040,128]{1,0:T(8,128)(2,1)S(1)}, u32[]{:S(2)}, u32[]{:S(2)}) collective-permute-start(bf16[1040,128]{1,0:T(8,128)(2,1)S(1)} %get-tuple-element.33), channel_id=1, source_target_pairs={{8,28},{12,24},{16,4},{20,0},{24,44},{28,40},{32,20},{36,16},{40,6... | collective-permute-start | bytes 798728 | tf_op jit(solution)/shard_map/ppermute | solution.py:487
  24.8 2.5 %collective-permute-start.3 = (bf16[1040,128]{1,0:T(8,128)(2,1)S(1)}, bf16[1040,128]{1,0:T(8,128)(2,1)S(1)}, u32[]{:S(2)}, u32[]{:S(2)}) collective-permute-start(bf16[1040,128]{1,0:T(8,128)(2,1)S(1)} %get-tuple-element.33), channel_id=1, source_target_pairs={{0,4},{4,0},{8,12},{12,8},{16,20},{20,16},{24,28},{28,24},{32,36},... | collective-permute-start | bytes 798728 | tf_op jit(solution)/shard_map/ppermute | solution.py:487
  27.3 2.2 %collective-permute-done.refs_6_ = bf16[1040,128]{1,0:T(8,128)(2,1)S(1)} collective-permute-done((bf16[1040,128]{1,0:T(8,128)(2,1)S(1)}, bf16[1040,128]{1,0:T(8,128)(2,1)S(1)}, u32[]{:S(2)}, u32[]{:S(2)}) %collective-permute-start) | collective-permute-done | bytes 266272 | tf_op jit(solution)/shard_map/ppermute | solution.py:487
  29.5 1.9 %stage0.1 = (bf16[12,144,512]{2,1,0:T(8,128)(2,1)S(1)}, f32[12,144,256]{2,1,0:T(8,128)S(1)}, bf16[6,16,128]{2,1,0:T(8,128)(2,1)S(1)}, f32[1,128]{1,0:T(1,128)S(1...) custom-call(bf16[256,256]{1,0:T(8,128)(2,1)} %constant.12.clone.refs, ...), custom_call_target="tpu_custom_call" | custom-call | flops 1 | bytes 1 | tf_op jit(solution)/shard_map/stage0/pallas_call | solution.py:298
  31.5 0.0 collective-permute-done.4.refs_5_
  31.5 1.6 %stage1.1 = (bf16[12,144,512]{2,1,0:T(8,128)(2,1)S(1)}, f32[12,144,256]{2,1,0:T(8,128)S(1)}, bf16[6,16,128]{2,1,0:T(8,128)(2,1)S(1)}, f32[1,128]{1,0:T(1,128)S(1)}) custom-call(bf16[256,256]{1,0:T(8,128)(2,1)S(1)} %get-tuple-element.27.refs_0_, ...), custom_call_target="tpu_custom_call", output_to_operand_aliasing={{0}: (6, {}), {1}: (7, {}), {2}: (8, {}), {3}: (9, {})} | custom-call | flops 1 | bytes 1 | tf_op jit(solution)/shard_map/stage1/pallas_call | solution.py:298
  33.0 1.5 %collective-permute-done.2.refs_5_ = bf16[1040,128]{1,0:T(8,128)(2,1)S(1)} collective-permute-done((bf16[1040,128]{1,0:T(8,128)(2,1)S(1)}, bf16[1040,128]{1,0:T(8,128)(2,1)S(1)}, u32[]{:S(2)}, u32[]{:S(2)}) %collective-permute-start.2) | collective-permute-done | bytes 266272 | tf_op jit(solution)/shard_map/ppermute | solution.py:487
  34.5 0.0 collective-permute-done.3.refs_6_
  34.5 2.1 %stage2.1 = (bf16[12,144,512]{2,1,0:T(8,128)(2,1)S(1)}, f32[12,144,256]{2,1,0:T(8,128)S(1)}, bf16[6,16,128]{2,1,0:T(8,128)(2,1)S(1)}, f32[1,128]{1,0:T(1,128)S(1)}) custom-call(bf16[256,256]{1,0:T(8,128)(2,1)S(1)} %get-tuple-element.27.refs_0_, ...), custom_call_target="tpu_custom_call", output_to_operand_aliasing={{0}: (7, {}), {1}: (8, {}), {2}: (9, {}), {3}: (10, {})} | custom-call | flops 1 | bytes 1 | tf_op jit(solution)/shard_map/stage2/pallas_call | solution.py:298
  36.6 0.0 collective-permute-done.1.refs_5_
  36.6 1.9 %stage3.1 = (bf16[12,144,512]{2,1,0:T(8,128)(2,1)S(1)}, f32[12,144,256]{2,1,0:T(8,128)S(1)}, bf16[6,16,128]{2,1,0:T(8,128)(2,1)S(1)}, f32[1,128]{1,0:T(1,128)S(1)}) custom-call(bf16[256,256]{1,0:T(8,128)(2,1)S(1)} %get-tuple-element.27.refs_0_, ...), custom_call_target="tpu_custom_call", output_to_operand_aliasing={{0}: (6, {}), {1}: (7, {}), {2}: (8, {}), {3}: (9, {})} | custom-call | flops 1 | bytes 1 | tf_op jit(solution)/shard_map/stage3/pallas_call | solution.py:298
  38.5 1.9 %collective-permute-start.5 = (f32[1,128]{1,0:T(1,128)S(1)}, f32[1,128]{1,0:T(1,128)S(1)}, u32[]{:S(2)}, u32[]{:S(2)}) collective-permute-start(f32[1,128]{1,0:T(1,128)S(1)} %get-tuple-element.47), channel_id=1, source_target_pairs={{0,16},{4,20},{16,32},{20,36},{24,8},{28,12},{32,48},{36,52},{40,2... | collective-permute-start | bytes 1544 | tf_op jit(solution)/shard_map/ppermute | solution.py:487
  40.5 5.6 %collective-permute-done.5 = f32[1,128]{1,0:T(1,128)S(1)} collective-permute-done((f32[1,128]{1,0:T(1,128)S(1)}, f32[1,128]{1,0:T(1,128)S(1)}, u32[]{:S(2)}, u32[]{:S(2)}) %collective-permute-start.5) | collective-permute-done | bytes 544 | tf_op jit(solution)/shard_map/ppermute | solution.py:487
  46.1 0.1 fusion
  46.2 14.8 %all_to_all.5.every = f32[16,1,128]{2,1,0:T(1,128)S(1)} all-to-all(f32[16,1,128]{2,1,0:T(1,128)S(1)} %broadcast_in_dim.13), channel_id=1, replica_groups=mesh['group'=32,'member'=4,'tile'=4] {'member','tile'}, dimensions={0} | all-to-all | bytes 16384 | tf_op jit(solution)/shard_map/all_to_all | solution.py:505
  61.0 1.2 %finish.1 = (f32[2,2,1,8]{3,2,1,0:T(1,128)}, f32[2,1,8]{2,1,0:T(1,128)}) custom-call(f32[16,1,128]{2,1,0:T(1,128)S(1)} %all_to_all.5.every, f32[16,128]{1,0:T(8,128)S(1)} %get-tuple-element.48.counts, f32[8,128]{1,0:T(8,128)S(1)} %get-tuple-element.49.offsets), custom_call_target="tpu_custom_call" | custom-call | flops 1 | bytes 1 | tf_op jit(solution)/shard_map/finish/pallas_call | solution.py:469
  (2 shorter events, 0.0 us)
Async XLA Ops:
  1.9 29.6 %collective-permute-start.4 = (bf16[528,256]{1,0:T(8,128)(2,1)S(1)}, bf16[528,256]{1,0:T(8,128)(2,1)S(1)}, u32[]{:S(2)}, u32[]{:S(2)}) collective-permute-start(bf16[528,256]{1,0:T(8,128)(2,1)S(1)} %get-tuple-element.34), channel_id=1, source_target_pairs={{0,8},{4,12},{8,0},{12,4},{16,24},{20,28},{24,16},{28,20},{32,40},... | collective-permute-start | bytes 811016 | tf_op jit(solution)/shard_map/ppermute | solution.py:487
  9.6 26.9 %collective-permute-start.1 = (bf16[528,256]{1,0:T(8,128)(2,1)S(1)}, bf16[528,256]{1,0:T(8,128)(2,1)S(1)}, u32[]{:S(2)}, u32[]{:S(2)}) collective-permute-start(bf16[528,256]{1,0:T(8,128)(2,1)S(1)} %get-tuple-element.32), channel_id=1, source_target_pairs={{0,12},{4,8},{8,4},{12,0},{16,28},{20,24},{24,20},{28,16},{32,44},... | collective-permute-start | bytes 811016 | tf_op jit(solution)/shard_map/ppermute | solution.py:487
  11.6 17.9 %collective-permute-start = (bf16[1040,128]{1,0:T(8,128)(2,1)S(1)}, bf16[1040,128]{1,0:T(8,128)(2,1)S(1)}, u32[]{:S(2)}, u32[]{:S(2)}) collective-permute-start(bf16[1040,128]{1,0:T(8,128)(2,1)S(1)} %get-tuple-element.26.refs_5_), channel_id=1, source_target_pairs={{8,24},{12,28},{16,0},{20,4},{24,40},{28,44},{32,16},{36,20},{40,5... | collective-permute-start | bytes 798728 | tf_op jit(solution)/shard_map/ppermute | solution.py:487
  22.8 11.7 %collective-permute-start.2 = (bf16[1040,128]{1,0:T(8,128)(2,1)S(1)}, bf16[1040,128]{1,0:T(8,128)(2,1)S(1)}, u32[]{:S(2)}, u32[]{:S(2)}) collective-permute-start(bf16[1040,128]{1,0:T(8,128)(2,1)S(1)} %get-tuple-element.33), channel_id=1, source_target_pairs={{8,28},{12,24},{16,4},{20,0},{24,44},{28,40},{32,20},{36,16},{40,6... | collective-permute-start | bytes 798728 | tf_op jit(solution)/shard_map/ppermute | solution.py:487
  24.8 9.7 %collective-permute-start.3 = (bf16[1040,128]{1,0:T(8,128)(2,1)S(1)}, bf16[1040,128]{1,0:T(8,128)(2,1)S(1)}, u32[]{:S(2)}, u32[]{:S(2)}) collective-permute-start(bf16[1040,128]{1,0:T(8,128)(2,1)S(1)} %get-tuple-element.33), channel_id=1, source_target_pairs={{0,4},{4,0},{8,12},{12,8},{16,20},{20,16},{24,28},{28,24},{32,36},... | collective-permute-start | bytes 798728 | tf_op jit(solution)/shard_map/ppermute | solution.py:487
  38.5 7.5 %collective-permute-start.5 = (f32[1,128]{1,0:T(1,128)S(1)}, f32[1,128]{1,0:T(1,128)S(1)}, u32[]{:S(2)}, u32[]{:S(2)}) collective-permute-start(f32[1,128]{1,0:T(1,128)S(1)} %get-tuple-element.47), channel_id=1, source_target_pairs={{0,16},{4,20},{16,32},{20,36},{24,8},{28,12},{32,48},{36,52},{40,2... | collective-permute-start | bytes 1544 | tf_op jit(solution)/shard_map/ppermute | solution.py:487
